TPU v7x, 128 devices: a whole 4x4x4 slice. The times are simulated.
128 devices in a mesh: row: 4 (over x), col: 2 (over z_hi), ga: 16 (over z_lo, y, core).
Axes of the slice: x: 4, y: 4, z: 4 (z_hi: 2, z_lo: 2; z = z_hi * 2 + z_lo), core: 2. Of those that a mesh axis runs over, the one named last changes fastest.
Arguments:
- matrix_elements: bfloat16 [2, 2, 2048, 2048], P(None, None, 'ga', ('row', 'col')), may hold values from -6 to 6
- screening: bfloat16 [2, 2, 2048, 2048], P(None, None, 'ga'), may hold values from -0.09375 to 0.09375
- pair_list: int32 [3, 2], replicated, may hold values from 0 to 1, as said below
- pair_q: int32 [3], replicated, may hold values from 0 to 1, as said below
Outputs:
- direct_kernel: bfloat16 [3, 2048, 2, 2048], P(None, 'ga', None, ('row', 'col'))
Inputs may be any that keep to these rules, and one draw needn't show every extreme that they name: `pair_list`: each row is a pair (k, k') with k <= k'; no pair appears twice; every difference k' - k from 0 to 1 occurs. `pair_q`: rows with equal k' - k have equal entries and rows with different k' - k different ones.
All inputs are finite; a program needn't handle non-finite values.
Results may differ from a plain program's by a relative error of at most 0.022.
Values may be sent and summed in bfloat16 or wider, within the bound.
No kernel may reach another device: no remote copies, remote signals or barrier semaphores. Data moves between devices by JAX's collectives and lax.ppermute only.
A program may use at most 64 MiB of HBM per device.

v0:
```python
import math

import jax
import jax.numpy as jnp
from jax import lax
from jax.sharding import PartitionSpec as P


def apply_screening(weights, columns):
    real_part = jnp.dot(weights[0], columns[0], preferred_element_type=jnp.float32) - jnp.dot(
        weights[1], columns[1], preferred_element_type=jnp.float32
    )
    imag_part = jnp.dot(weights[0], columns[1], preferred_element_type=jnp.float32) + jnp.dot(
        weights[1], columns[0], preferred_element_type=jnp.float32
    )
    return (real_part, imag_part)


def contract_rows(left_part, right_part):
    return lax.dot_general(
        left_part, right_part, (((0,), (0,)), ((), ())), preferred_element_type=jnp.float32
    )


def per_device(matrix_elements, screening, pair_list, pair_q):
    factor = 1.0 / math.sqrt(2.0 * screening.shape[3])
    kernels = []
    for position in range(pair_list.shape[0]):
        k_row = pair_list[position, 0]
        k_column = pair_list[position, 1]
        weights = lax.dynamic_index_in_dim(screening, pair_q[position], 0, keepdims=False)
        own_columns = lax.dynamic_index_in_dim(matrix_elements, k_column, 0, keepdims=False)
        part_re, part_im = apply_screening(
            weights, lax.all_gather(own_columns, "ga", axis=1, tiled=True)
        )
        own_rows = lax.dynamic_index_in_dim(matrix_elements, k_row, 0, keepdims=False)
        row_block = lax.all_gather(own_rows, ("row", "col"), axis=2, tiled=True)
        screened_re = part_re.astype(jnp.bfloat16)
        screened_im = part_im.astype(jnp.bfloat16)
        kernel_part_re = contract_rows(row_block[0], screened_re) + contract_rows(
            row_block[1], screened_im
        )
        kernel_part_im = contract_rows(row_block[0], screened_im) - contract_rows(
            row_block[1], screened_re
        )
        summed = lax.psum_scatter(
            (jnp.stack((kernel_part_re, kernel_part_im), 1) * factor).astype(jnp.bfloat16),
            "ga",
            scatter_dimension=0,
            tiled=True,
        )
        kernels.append(summed)
    return jnp.stack(kernels, 0)


def solution(mesh):
    return jax.shard_map(
        per_device,
        mesh=mesh,
        in_specs=(P(None, None, "ga", ("row", "col")), P(None, None, "ga", None), P(), P()),
        out_specs=P(None, "ga", None, ("row", "col")),
        check_vma=False,
    )
```

profile of v0, /device:TPU:6, one launch (start us, length us, event | category | flops | bytes accessed | tf_op | source)
XLA Modules:
  0.0 479.9 jit_solution(5831782716447552253)
XLA Ops:
  6.5 1.6 fusion.39
  19.5 2.1 constant_dynamic-slice_fusion.5
  27.5 30.5 %all-gather.15.cloned.1.call-done = bf16[1,2,2048,256]{3,2,1,0:T(8,128)(2,1)} async-done(((bf16[1,2,128,256]{3,2,1,0:T(8,128)(2,1)}), bf16[1,2,2048,256]{3,2,1,0:T(8,128)(2,1)}) %all-gather.15.cloned.1.call-update) | async-done | bytes 2097168 | tf_op jit(solution)/shard_map/all_gather | solution.py:34
  58.0 1.7 fusion.16
  59.7 1.5 fusion.15
  61.9 46.4 %all-gather.13.cloned.1.call-done = bf16[1,2,128,2048]{3,2,1,0:T(8,128)(2,1)} async-done(((bf16[1,2,128,256]{3,2,1,0:T(8,128)(2,1)}), bf16[1,2,128,2048]{3,2,1,0:T(8,128)(2,1)}) %all-gather.13.cloned.1.call-update) | async-done | bytes 1048592 | tf_op jit(solution)/shard_map/all_gather | solution.py:37
  108.4 1.6 fusion.21
  111.4 1.8 fusion
  114.9 28.0 %all-gather.19.cloned.1.call-done = bf16[1,2,2048,256]{3,2,1,0:T(8,128)(2,1)} async-done(((bf16[1,2,128,256]{3,2,1,0:T(8,128)(2,1)}), bf16[1,2,2048,256]{3,2,1,0:T(8,128)(2,1)}) %all-gather.19.cloned.1.call-update) | async-done | bytes 2097168 | tf_op jit(solution)/shard_map/all_gather | solution.py:34
  142.9 1.7 fusion.18
  144.6 1.5 fusion.17
  146.8 46.2 %all-gather.17.cloned.1.call-done = bf16[1,2,128,2048]{3,2,1,0:T(8,128)(2,1)} async-done(((bf16[1,2,128,256]{3,2,1,0:T(8,128)(2,1)}), bf16[1,2,128,2048]{3,2,1,0:T(8,128)(2,1)}) %all-gather.17.cloned.1.call-update) | async-done | bytes 1048592 | tf_op jit(solution)/shard_map/all_gather | solution.py:37
  193.1 1.6 fusion.23
  196.1 1.8 fusion.1
  199.8 27.6 %all-gather.23.cloned.1.call-done = bf16[1,2,2048,256]{3,2,1,0:T(8,128)(2,1)} async-done(((bf16[1,2,128,256]{3,2,1,0:T(8,128)(2,1)}), bf16[1,2,2048,256]{3,2,1,0:T(8,128)(2,1)}) %all-gather.23.cloned.1.call-update) | async-done | bytes 2097168 | tf_op jit(solution)/shard_map/all_gather | solution.py:34
  227.5 1.7 fusion.19
  229.2 1.5 fusion.20
  231.4 46.2 %all-gather.21.cloned.1.call-done = bf16[1,2,128,2048]{3,2,1,0:T(8,128)(2,1)} async-done(((bf16[1,2,128,256]{3,2,1,0:T(8,128)(2,1)}), bf16[1,2,128,2048]{3,2,1,0:T(8,128)(2,1)}) %all-gather.21.cloned.1.call-update) | async-done | bytes 1048592 | tf_op jit(solution)/shard_map/all_gather | solution.py:37
  277.6 1.6 fusion.26
  280.7 1.8 fusion.2
  282.5 59.9 %reduce-scatter.4.cloned.1.call-done = bf16[128,2,256]{2,0,1:T(8,128)(2,1)} async-done(((bf16[2048,2,256]{2,0,1:T(8,128)(2,1)}), bf16[128,2,256]{2,0,1:T(8,128)(2,1)}) %reduce-scatter.4.cloned.1.call-update) | async-done | bytes 131088 | tf_op jit(solution)/shard_map/reduce_scatter | solution.py:46
  342.4 64.4 %reduce-scatter.6.cloned.1.call-done = bf16[128,2,256]{2,0,1:T(8,128)(2,1)} async-done(((bf16[2048,2,256]{2,0,1:T(8,128)(2,1)}), bf16[128,2,256]{2,0,1:T(8,128)(2,1)}) %reduce-scatter.6.cloned.1.call-update) | async-done | bytes 131088 | tf_op jit(solution)/shard_map/reduce_scatter | solution.py:46
  406.8 64.4 %reduce-scatter.8.cloned.1.call-done = bf16[128,2,256]{2,0,1:T(8,128)(2,1)} async-done(((bf16[2048,2,256]{2,0,1:T(8,128)(2,1)}), bf16[128,2,256]{2,0,1:T(8,128)(2,1)}) %reduce-scatter.8.cloned.1.call-update) | async-done | bytes 131088 | tf_op jit(solution)/shard_map/reduce_scatter | solution.py:46
  472.2 1.2 copy.5
  (51 shorter events, 11.2 us)
Async XLA Ops:
  6.5 51.5 %copy-start = (bf16[2,2,128,2048]{3,2,1,0:T(8,128)(2,1)S(1)}, bf16[2,2,128,2048]{3,2,1,0:T(8,128)(2,1)}, u32[]{:S(2)}) copy-start(bf16[2,2,128,2048]{3,2,1,0:T(8,128)(2,1)} %param.5) | copy-start | bytes 6291460
  6.5 18.3 %copy-start.4 = (s32[3]{0:T(128)S(1)}, s32[3]{0:T(128)}, u32[]{:S(2)}) copy-start(s32[3]{0:T(128)} %param.7) | copy-start | bytes 40
  6.5 51.5 %all-gather.15.cloned.1.call-start = ((), (), s32[]{:S(2)}) async-start(), calls=%async_computation.7 | async-start | bytes 2228224 | tf_op jit(solution)/shard_map/all_gather | solution.py:34
  21.6 86.8 %all-gather.13.cloned.1.call-start = ((), (), s32[]{:S(2)}) async-start(), calls=%async_computation.6 | async-start | bytes 1179648 | tf_op jit(solution)/shard_map/all_gather | solution.py:37
  22.3 120.6 %all-gather.19.cloned.1.call-start = ((), (), s32[]{:S(2)}) async-start(), calls=%async_computation.9 | async-start | bytes 2228224 | tf_op jit(solution)/shard_map/all_gather | solution.py:34
  23.1 170.0 %all-gather.17.cloned.1.call-start = ((), (), s32[]{:S(2)}) async-start(), calls=%async_computation.8 | async-start | bytes 1179648 | tf_op jit(solution)/shard_map/all_gather | solution.py:37
  23.6 203.8 %all-gather.23.cloned.1.call-start = ((), (), s32[]{:S(2)}) async-start(), calls=%async_computation.11 | async-start | bytes 2228224 | tf_op jit(solution)/shard_map/all_gather | solution.py:34
  24.2 253.4 %all-gather.21.cloned.1.call-start = ((), (), s32[]{:S(2)}) async-start(), calls=%async_computation.10 | async-start | bytes 1179648 | tf_op jit(solution)/shard_map/all_gather | solution.py:37
  24.8 317.6 %reduce-scatter.4.cloned.1.call-start = ((), (), s32[]{:S(2)}) async-start(), calls=%async_computation.3 | async-start | bytes 2228224 | tf_op jit(solution)/shard_map/reduce_scatter | solution.py:46
  58.0 3.2 copy-start.7
  108.3 1.6 copy-start.3
  113.2 293.6 %reduce-scatter.6.cloned.1.call-start = ((), (), s32[]{:S(2)}) async-start(), calls=%async_computation.4 | async-start | bytes 2228224 | tf_op jit(solution)/shard_map/reduce_scatter | solution.py:46
  142.9 3.2 copy-start.6
  193.1 1.6 copy-start.2
  198.0 273.2 %reduce-scatter.8.cloned.1.call-start = ((), (), s32[]{:S(2)}) async-start(), calls=%async_computation.5 | async-start | bytes 2228224 | tf_op jit(solution)/shard_map/reduce_scatter | solution.py:46
  227.5 3.2 copy-start.5
  277.6 1.6 copy-start.1
Sparse Core Ops, SparseCore 0:
  21.7 36.2 all-gather.14
  60.2 48.0 all-gather.12
  110.0 32.8 all-gather.18
  145.0 48.0 all-gather.16
  194.6 32.8 all-gather.22
  229.5 48.0 all-gather.20
  280.0 62.3 reduce-scatter.3
  344.8 61.9 reduce-scatter.5
  409.2 61.9 reduce-scatter.7
where the time goes:
time: 481 us; the launch traced here: 480 us
  waiting for transfers between devices  417 us (87%)
  between operations  30.4 us (6%)
  matrix products  20.6 us (4%)
  other arithmetic  6.43 us (1%)
  local copies, waits for them, and re-layouts  5.44 us (1%)
    reduce_scatter x3, waiting for transfers between devices, per_device(): lax.psum_scatter((jnp.stack((kernel_part_re, kernel_part_im), 1) * factor...  189 us
    all_gather x3, waiting for transfers between devices, per_device(): row_block = lax.all_gather(own_rows, ('row', 'col'), axis=2, tiled=True)  139 us
    all_gather x3, waiting for transfers between devices, per_device(): lax.all_gather(own_columns, 'ga', axis=1, tiled=True)  86.2 us
  transfers between devices with their start and end apart: 9, of which 9 were waited for; matrix products, arithmetic and copies ran while one was open for 6% of the time, Pallas kernels for 0%

commit v1 on v0

v1 whole, which is shorter than its diff:
```python
import functools
import math

import jax
import jax.numpy as jnp
from jax import lax
from jax.experimental import pallas as pl
from jax.experimental.pallas import tpu as pltpu
from jax.sharding import Mesh, PartitionSpec as P

BF = jnp.bfloat16
F32 = jnp.float32
VMEM = pl.BlockSpec(memory_space=pltpu.VMEM)
SMEM = pl.BlockSpec(memory_space=pltpu.SMEM)
LIMIT = 24 * 1024 * 1024
PAIRS = ((0, 0), (0, 1), (1, 1))


def call(body, outs, *args, scratch=(), smem=0):
    return pl.pallas_call(
        body,
        out_shape=[jax.ShapeDtypeStruct(s, BF) for s in outs],
        in_specs=[SMEM] * smem + [VMEM] * (len(args) - smem),
        out_specs=[VMEM] * len(outs),
        scratch_shapes=list(scratch),
        compiler_params=pltpu.CompilerParams(vmem_limit_bytes=LIMIT),
    )(*args)


def shift(x, axis, size, step):
    return lax.ppermute(x, axis, [(i, (i + step) % size) for i in range(size)])


def transpose_halves(m_ref, mine_ref, other_ref):
    c = lax.axis_index("c")
    for k in range(2):
        for part in range(2):
            lanes = slice(part * 128, (part + 1) * 128)
            mine_ref[k, :, lanes] = m_ref[k, part, :, pl.ds(pl.multiple_of(c * 128, 128), 128)].T
            other_ref[k, :, lanes] = m_ref[k, part, :, pl.ds(pl.multiple_of((1 - c) * 128, 128), 128)].T


def join_halves(mine_ref, got_ref, out_ref):
    out_ref[:, :, :256] = mine_ref[...]
    out_ref[:, :, 256:] = got_ref[...]


def weight_rows(list_ref, q_ref, own_ref, mate_ref, out_ref):
    zl, y, c = lax.axis_index("zl"), lax.axis_index("y"), lax.axis_index("c")
    for slot, (k, kp) in enumerate(((0, 0), (0, 1))):
        q = q_ref[0]
        for r in range(1, 3):
            hit = (list_ref[r, 0] == k) & (list_ref[r, 1] == kp)
            q = jnp.where(hit, q_ref[r], q)
        for b in range(2):
            for s in range(4):
                block = (zl ^ b) * 4 + lax.rem(y + s, 4)
                lanes = pl.ds(pl.multiple_of(block * 256 + c * 128, 128), 128)
                col = (b * 4 + s) * 256
                for o, ref in enumerate((own_ref, mate_ref)):
                    re, im = ref[q, 0, :, lanes], ref[q, 1, :, lanes]
                    row = o * 256
                    out_ref[slot, row : row + 128, col : col + 128] = re
                    out_ref[slot, row : row + 128, col + 128 : col + 256] = -im
                    out_ref[slot, row + 128 : row + 256, col : col + 128] = im
                    out_ref[slot, row + 128 : row + 256, col + 128 : col + 256] = re


def screen(w_ref, *refs):
    shards, out_ref, acc = refs[:8], refs[8], refs[9]
    for i, ref in enumerate(shards):
        cols = slice(i * 256, (i + 1) * 256)
        for p, (k, kp) in enumerate(PAIRS):
            term = jnp.dot(
                w_ref[kp - k, :, cols], ref[kp].reshape(256, 256), preferred_element_type=F32
            )
            if i == 0:
                acc[p] = term
            else:
                acc[p] += term
    out_ref[...] = acc[...].reshape(3, 2, 2, 128, 256).astype(BF)


def sort_rows(*refs):
    shards, out_ref = refs[:8], refs[8]
    x, zh, zl, y = (lax.axis_index(a) for a in ("x", "zh", "zl", "y"))
    for dz in range(2):
        for dx in range(4):
            j = lax.rem(x + dx, 4) * 2 + (zh ^ dz)
            b, s = (j // 4) ^ zl, lax.rem((j % 4) - y + 4, 4)
            out_ref[:, b * 4 + s] = shards[dz * 4 + dx][...]


def contract(factor, mine_ref, got_ref, rows_ref, ak_ref, as_ref, bk_ref, b1_ref, b2_ref, b3_ref):
    for p, (k, kp) in enumerate(PAIRS):
        blocks = []
        for o in range(2):
            re = (mine_ref[p, o, 0].astype(F32) + got_ref[p, 1 - o, 0].astype(F32)).astype(BF)
            im = (mine_ref[p, o, 1].astype(F32) + got_ref[p, 1 - o, 1].astype(F32)).astype(BF)
            blocks += [jnp.concatenate((re, im), 1), jnp.concatenate((im, -re), 1)]
        rhs = jnp.concatenate(blocks, 0)
        for b in range(2):
            for s in range(4):
                part = jnp.dot(rows_ref[k, b * 4 + s], rhs, preferred_element_type=F32)
                part = (part * factor).astype(BF)
                a_part = part if p == 0 else part[:, :256] if p == 2 else None
                b_part = part if p == 1 else part[:, 256:] if p == 2 else None
                if a_part is not None:
                    lanes = slice(0, 512) if p == 0 else slice(512, 768)
                    (ak_ref, as_ref)[b][s, :, lanes] = a_part
                if b_part is not None:
                    lanes = slice(0, 512) if p == 1 else slice(512, 768)
                    (bk_ref, b1_ref, b2_ref, b3_ref)[s][b, :, lanes] = b_part


def add_a(keep_ref, got_ref, *outs):
    for s, ref in enumerate(outs):
        ref[...] = (keep_ref[s].astype(F32) + got_ref[s].astype(F32)).astype(BF)


def add_b(keep_ref, g1_ref, g2_ref, g3_ref, out_ref, send_ref):
    total = [keep_ref[b].astype(F32) + g1_ref[b].astype(F32) + (g2_ref[b].astype(F32) + g3_ref[b].astype(F32)) for b in range(2)]
    out_ref[...] = total[0].astype(BF)
    send_ref[...] = total[1].astype(BF)


def finish(list_ref, a0_ref, a1_ref, a2_ref, a3_ref, b0_ref, b1_ref, out_ref):
    a = a0_ref[...].astype(F32) + a1_ref[...].astype(F32) + (a2_ref[...].astype(F32) + a3_ref[...].astype(F32))
    b = b0_ref[...].astype(F32) + b1_ref[...].astype(F32)
    sums = (a[:, :512], b[:, :512], jnp.concatenate((a[:, 512:], b[:, 512:]), 1))
    for (k, kp), value in zip(PAIRS, sums):
        place = 0
        for r in range(1, 3):
            place = jnp.where((list_ref[r, 0] == k) & (list_ref[r, 1] == kp), r, place)
        out_ref[place] = value.astype(BF)


def gather(x, swap_axis, ring_axis):
    mate = shift(x, swap_axis, 2, 1)
    own = [x, shift(x, ring_axis, 4, -1), shift(x, ring_axis, 4, 2), shift(x, ring_axis, 4, 1)]
    far = [mate, shift(mate, ring_axis, 4, -1), shift(own[2], swap_axis, 2, 1), shift(mate, ring_axis, 4, 1)]
    return own + far


def per_device(matrix_elements, screening, pair_list, pair_q):
    factor = 1.0 / math.sqrt(2.0 * screening.shape[3])
    columns = gather(matrix_elements, "zl", "y")
    mate_weights = shift(screening, "c", 2, 1)
    mine, other = call(transpose_halves, [(2, 128, 256)] * 2, matrix_elements)
    (rows,) = call(join_halves, [(2, 128, 512)], mine, shift(other, "c", 2, 1))
    row_shards = gather(rows, "zh", "x")
    (weights,) = call(weight_rows, [(2, 512, 2048)], pair_list, pair_q, screening, mate_weights, smem=2)
    (part,) = call(screen, [(3, 2, 2, 128, 256)], weights, *columns, scratch=[pltpu.VMEM((3, 512, 256), F32)])
    (sorted_rows,) = call(sort_rows, [(2, 8, 128, 512)], *row_shards)
    got = shift(part, "c", 2, 1)
    ak, asend, bk, b1, b2, b3 = call(
        functools.partial(contract, factor), [(4, 128, 768)] * 2 + [(2, 128, 768)] * 4, part, got, sorted_rows
    )
    a_got = shift(asend, "zl", 2, 1)
    b_got = [shift(b1, "y", 4, 1), shift(b2, "y", 4, 2), shift(b3, "y", 4, -1)]
    q = call(add_a, [(128, 768)] * 4, ak, a_got)
    b_keep, b_send = call(add_b, [(128, 768)] * 2, bk, *b_got)
    a_last = [shift(q[1], "y", 4, 1), shift(q[2], "y", 4, 2), shift(q[3], "y", 4, -1)]
    b_last = shift(b_send, "zl", 2, 1)
    (out,) = call(finish, [(3, 128, 512)], pair_list, q[0], *a_last, b_keep, b_last, smem=1)
    return out.reshape(3, 128, 2, 256)


def solution(mesh):
    split = Mesh(mesh.devices.reshape(4, 2, 2, 4, 2), ("x", "zh", "zl", "y", "c"))
    ga = ("zl", "y", "c")
    return jax.shard_map(
        per_device,
        mesh=split,
        in_specs=(P(None, None, ga, ("x", "zh")), P(None, None, ga, None), P(), P()),
        out_specs=P(None, ga, None, ("x", "zh")),
        check_vma=False,
    )
```

time: 481 us -> 95.5 us (0.20)
  waiting for transfers between devices: 417 us -> 47.9 us
  starting transfers between devices: 0.32 us -> 36.1 us
  between operations: 30.4 us -> 0.11 us
  matrix products: 20.6 us -> 0 us
  Pallas kernels: 0 us -> 7.27 us
  other arithmetic: 6.43 us -> 0 us
    all_gather x6 -> x0, waiting for transfers between devices: 225 us -> none  [the longest x3 139 us: per_device(): row_block = lax.all_gather(own_rows, ('row', 'col'), axis=2, tiled=True)]
    reduce_scatter x3 -> x0, waiting for transfers between devices: 189 us -> none  [per_device(): lax.psum_scatter((jnp.stack((kernel_part_re, kernel_part_im), 1) * factor...]
    ppermute x0 -> x25, waiting for transfers between devices: none -> 47.9 us  [shift(): return lax.ppermute(x, axis, [(i, (i + step) % size) for i in range(size)])]
    ppermute x0 -> x25, starting transfers between devices: none -> 36.1 us  [shift(): return lax.ppermute(x, axis, [(i, (i + step) % size) for i in range(size)])]
    dot_general x24 -> x0, matrix products: 20.6 us -> none  [the longest x12 8.99 us: contract_rows(): lax.dot_general(left_part, right_part, (((0,), (0,)), ((), ())), preferre...]
    pallas_call x0 -> x9, Pallas kernels: none -> 7.27 us  [call(): pl.pallas_call(body, out_shape=[jax.ShapeDtypeStruct(s, BF) for s in outs...]
    convert_element_type x3 -> x0, other arithmetic: 5.36 us -> none  [per_device(): (jnp.stack((kernel_part_re, kernel_part_im), 1) * factor).astype(jnp.bflo...]
  transfers between devices with their start and end apart: 9 -> 25, of which waited for: 9 -> 13; matrix products, arithmetic and copies ran while one was open for 6% -> 1% of each run, Pallas kernels for 0% -> 2%
where the time goes in v1:
time: 95.5 us; the launch traced here: 95.3 us
  waiting for transfers between devices  47.9 us (50%)
  starting transfers between devices  36.1 us (38%)
  Pallas kernels  7.27 us (8%)
  local copies, waits for them, and re-layouts  3.85 us (4%)
    ppermute x25, waiting for transfers between devices, shift(): return lax.ppermute(x, axis, [(i, (i + step) % size) for i in range(size)])  47.9 us
    ppermute x25, starting transfers between devices, shift(): return lax.ppermute(x, axis, [(i, (i + step) % size) for i in range(size)])  36.1 us
    pallas_call x9, Pallas kernels, call(): pl.pallas_call(body, out_shape=[jax.ShapeDtypeStruct(s, BF) for s in outs...  7.27 us
    unnamed x7, local copies, waits for them, and re-layouts  3.01 us
  transfers between devices with their start and end apart: 25, of which 13 were waited for; matrix products, arithmetic and copies ran while one was open for 1% of the time, Pallas kernels for 2%

profile of v1, /device:TPU:6, one launch (start us, length us, event | category | flops | bytes accessed | tf_op | source)
XLA Modules:
  0.0 95.3 jit_solution(7345809307884699849)
XLA Ops:
  0.0 1.9 %collective-permute-start.4 = (bf16[2,2,128,256]{3,2,1,0:T(8,128)(2,1)}, bf16[2,2,128,256]{3,2,1,0:T(8,128)(2,1)S(1)}, u32[]{:S(2)}, u32[]{:S(2)}) collective-permute-start(bf16[2,2,128,256]{3,2,1,0:T(8,128)(2,1)} %m_ref.1), channel_id=1, source_target_pairs={{0,8},{8,0},{1,9},{9,1},{2,10},{10,2},{3,11},{11,3},{4,12},{12,4},... | collective-permute-start | bytes 786440 | tf_op jit(solution)/shard_map/ppermute | solution.py:31
  1.9 3.2 %collective-permute-start.2 = (bf16[2,2,128,256]{3,2,1,0:T(8,128)(2,1)}, bf16[2,2,128,256]{3,2,1,0:T(8,128)(2,1)S(1)}, u32[]{:S(2)}, u32[]{:S(2)}) collective-permute-start(bf16[2,2,128,256]{3,2,1,0:T(8,128)(2,1)} %m_ref.1), channel_id=1, source_target_pairs={{0,4},{2,6},{4,0},{6,2},{1,5},{3,7},{5,1},{7,3},{8,12},{10,14},{12... | collective-permute-start | bytes 786440 | tf_op jit(solution)/shard_map/ppermute | solution.py:31
  7.1 2.0 %collective-permute-done.4.refs_4_ = bf16[2,2,128,256]{3,2,1,0:T(8,128)(2,1)S(1)} collective-permute-done((bf16[2,2,128,256]{3,2,1,0:T(8,128)(2,1)}, bf16[2,2,128,256]{3,2,1,0:T(8,128)(2,1)S(1)}, u32[]{:S(2)}, u32[]{:S(2)}) %collective-permute-start.4) | collective-permute-done | bytes 262176 | tf_op jit(solution)/shard_map/ppermute | solution.py:31
  9.1 3.0 %collective-permute-start.5 = (bf16[2,2,128,256]{3,2,1,0:T(8,128)(2,1)S(1)}, bf16[2,2,128,256]{3,2,1,0:T(8,128)(2,1)S(1)}, u32[]{:S(2)}, u32[]{:S(2)}) collective-permute-start(bf16[2,2,128,256]{3,2,1,0:T(8,128)(2,1)S(1)} %collective-permute-done.4.refs_4_), channel_id=1, source_target_pairs={{0,6},{2,0},{4,2},{6,4},{1,7},{3,1},{5,3},{7,5},{8,14},{10,8},{12,... | collective-permute-start | bytes 786440 | tf_op jit(solution)/shard_map/ppermute | solution.py:31
  15.2 1.6 %copy-done = bf16[2,2,128,2048]{3,2,1,0:T(8,128)(2,1)S(1)} copy-done((bf16[2,2,128,2048]{3,2,1,0:T(8,128)(2,1)S(1)}, bf16[2,2,128,2048]{3,2,1,0:T(8,128)(2,1)}, u32[]{:S(2)}) %copy-start) | copy-done | bytes 2097176
  18.8 4.9 %collective-permute-done.5.refs_5_ = bf16[2,2,128,256]{3,2,1,0:T(8,128)(2,1)S(1)} collective-permute-done((bf16[2,2,128,256]{3,2,1,0:T(8,128)(2,1)S(1)}, bf16[2,2,128,256]{3,2,1,0:T(8,128)(2,1)S(1)}, u32[]{:S(2)}, u32[]{:S(2)}) %collective-permute-start.5) | collective-permute-done | bytes 262176 | tf_op jit(solution)/shard_map/ppermute | solution.py:31
  23.7 2.8 %shard_map.47.mine_ref = bf16[3,2,2,128,256]{4,3,2,1,0:T(8,128)(2,1)S(1)} custom-call(bf16[2,512,2048]{2,1,0:T(8,128)(2,1)S(1)} %shard_map.46.w_ref, bf16[2,2,128,256]{3,2,1,0:T(8,128)(2,1)S(1)} %copy-done.1, bf16[2,2,128,256]{3,2,1,0:T(8,128)(2,1)S(1)} %collective-permute-done.1.refs_1_, bf16[2,2,128,256]{3,2,1,0:T(8,128)(2,1)S(1)} %collective-permute-done.2.refs_2_, ...), custom_call_target="tpu_custom_call" | custom-call | tf_op jit(solution)/shard_map/pallas_call | solution.py:20
  27.3 1.8 %collective-permute-done.9.got_ref = bf16[2,128,256]{2,1,0:T(8,128)(2,1)S(1)} collective-permute-done((bf16[2,128,256]{2,1,0:T(8,128)(2,1)S(1)}, bf16[2,128,256]{2,1,0:T(8,128)(2,1)S(1)}, u32[]{:S(2)}, u32[]{:S(2)}) %collective-permute-start.9) | collective-permute-done | bytes 131104 | tf_op jit(solution)/shard_map/ppermute | solution.py:31
  29.1 3.7 %collective-permute-start.13 = (bf16[2,128,512]{2,1,0:T(8,128)(2,1)S(1)}, bf16[2,128,512]{2,1,0:T(8,128)(2,1)S(1)}, u32[]{:S(2)}, u32[]{:S(2)}) collective-permute-start(bf16[2,128,512]{2,1,0:T(8,128)(2,1)S(1)} %shard_map.49.refs_0_), channel_id=1, source_target_pairs={{0,16},{16,0},{1,17},{17,1},{2,18},{18,2},{3,19},{19,3},{4,20},{20... | collective-permute-start | bytes 786440 | tf_op jit(solution)/shard_map/ppermute | solution.py:31
  34.2 3.2 %collective-permute-start.12 = (bf16[2,128,512]{2,1,0:T(8,128)(2,1)S(1)}, bf16[2,128,512]{2,1,0:T(8,128)(2,1)S(1)}, u32[]{:S(2)}, u32[]{:S(2)}) collective-permute-start(bf16[2,128,512]{2,1,0:T(8,128)(2,1)S(1)} %shard_map.49.refs_0_), channel_id=1, source_target_pairs={{0,32},{32,64},{64,96},{96,0},{1,33},{33,65},{65,97},{97,1},{2,34}... | collective-permute-start | bytes 786440 | tf_op jit(solution)/shard_map/ppermute | solution.py:31
  37.4 2.0 %collective-permute-done.13.refs_4_ = bf16[2,128,512]{2,1,0:T(8,128)(2,1)S(1)} collective-permute-done((bf16[2,128,512]{2,1,0:T(8,128)(2,1)S(1)}, bf16[2,128,512]{2,1,0:T(8,128)(2,1)S(1)}, u32[]{:S(2)}, u32[]{:S(2)}) %collective-permute-start.13) | collective-permute-done | bytes 262176 | tf_op jit(solution)/shard_map/ppermute | solution.py:31
  40.2 3.3 %collective-permute-done.11.refs_2_ = bf16[2,128,512]{2,1,0:T(8,128)(2,1)S(1)} collective-permute-done((bf16[2,128,512]{2,1,0:T(8,128)(2,1)S(1)}, bf16[2,128,512]{2,1,0:T(8,128)(2,1)S(1)}, u32[]{:S(2)}, u32[]{:S(2)}) %collective-permute-start.11) | collective-permute-done | bytes 262176 | tf_op jit(solution)/shard_map/ppermute | solution.py:31
  43.6 4.5 %collective-permute-done.10.refs_1_ = bf16[2,128,512]{2,1,0:T(8,128)(2,1)S(1)} collective-permute-done((bf16[2,128,512]{2,1,0:T(8,128)(2,1)S(1)}, bf16[2,128,512]{2,1,0:T(8,128)(2,1)S(1)}, u32[]{:S(2)}, u32[]{:S(2)}) %collective-permute-start.10) | collective-permute-done | bytes 262176 | tf_op jit(solution)/shard_map/ppermute | solution.py:31
  48.1 1.6 %collective-permute-start.16 = (bf16[2,128,512]{2,1,0:T(8,128)(2,1)S(1)}, bf16[2,128,512]{2,1,0:T(8,128)(2,1)S(1)}, u32[]{:S(2)}, u32[]{:S(2)}) collective-permute-start(bf16[2,128,512]{2,1,0:T(8,128)(2,1)S(1)} %collective-permute-done.13.refs_4_), channel_id=1, source_target_pairs={{0,32},{32,64},{64,96},{96,0},{1,33},{33,65},{65,97},{97,1},{2,34}... | collective-permute-start | bytes 786440 | tf_op jit(solution)/shard_map/ppermute | solution.py:31
  49.7 3.9 %collective-permute-done.14.refs_5_ = bf16[2,128,512]{2,1,0:T(8,128)(2,1)S(1)} collective-permute-done((bf16[2,128,512]{2,1,0:T(8,128)(2,1)S(1)}, bf16[2,128,512]{2,1,0:T(8,128)(2,1)S(1)}, u32[]{:S(2)}, u32[]{:S(2)}) %collective-permute-start.14) | collective-permute-done | bytes 262176 | tf_op jit(solution)/shard_map/ppermute | solution.py:31
  53.6 2.6 %collective-permute-done.16.refs_7_ = bf16[2,128,512]{2,1,0:T(8,128)(2,1)S(1)} collective-permute-done((bf16[2,128,512]{2,1,0:T(8,128)(2,1)S(1)}, bf16[2,128,512]{2,1,0:T(8,128)(2,1)S(1)}, u32[]{:S(2)}, u32[]{:S(2)}) %collective-permute-start.16) | collective-permute-done | bytes 262176 | tf_op jit(solution)/shard_map/ppermute | solution.py:31
  56.4 1.8 %shard_map.51 = (bf16[4,128,768]{2,1,0:T(8,128)(2,1)S(1)}, bf16[4,128,768]{2,1,0:T(8,128)(2,1)S(1)}, bf16[2,128,768]{2,1,0:T(8,128)(2,1)S(1)}, bf16[2,128,768]{2...) custom-call(bf16[3,2,2,128,256]{4,3,2,1,0:T(8,128)(2,1)S(1)} %shard_map.47.mine_ref, ...), custom_call_target="tpu_custom_call" | custom-call | tf_op jit(solution)/shard_map/pallas_call | solution.py:20
  59.8 2.6 %collective-permute-start.22 = (bf16[2,128,768]{2,1,0:T(8,128)(2,1)S(1)}, bf16[2,128,768]{2,1,0:T(8,128)(2,1)S(1)}, u32[]{:S(2)}, u32[]{:S(2)}) collective-permute-start(bf16[2,128,768]{2,1,0:T(8,128)(2,1)S(1)} %get-tuple-element.29), channel_id=1, source_target_pairs={{0,4},{2,6},{4,0},{6,2},{1,5},{3,7},{5,1},{7,3},{8,12},{10,14},{12... | collective-permute-start | bytes 1179656 | tf_op jit(solution)/shard_map/ppermute | solution.py:31
  63.9 6.9 %collective-permute-done.21.g1_ref = bf16[2,128,768]{2,1,0:T(8,128)(2,1)S(1)} collective-permute-done((bf16[2,128,768]{2,1,0:T(8,128)(2,1)S(1)}, bf16[2,128,768]{2,1,0:T(8,128)(2,1)S(1)}, u32[]{:S(2)}, u32[]{:S(2)}) %collective-permute-start.21) | collective-permute-done | bytes 393248 | tf_op jit(solution)/shard_map/ppermute | solution.py:31
  70.8 8.2 %collective-permute-done.22.g2_ref = bf16[2,128,768]{2,1,0:T(8,128)(2,1)S(1)} collective-permute-done((bf16[2,128,768]{2,1,0:T(8,128)(2,1)S(1)}, bf16[2,128,768]{2,1,0:T(8,128)(2,1)S(1)}, u32[]{:S(2)}, u32[]{:S(2)}) %collective-permute-start.22) | collective-permute-done | bytes 393248 | tf_op jit(solution)/shard_map/ppermute | solution.py:31
  79.1 1.7 %collective-permute-start.24 = (bf16[128,768]{1,0:T(8,128)(2,1)S(1)}, bf16[128,768]{1,0:T(8,128)(2,1)S(1)}, u32[]{:S(2)}, u32[]{:S(2)}) collective-permute-start(bf16[128,768]{1,0:T(8,128)(2,1)S(1)} %get-tuple-element.32), channel_id=1, source_target_pairs={{0,8},{8,0},{1,9},{9,1},{2,10},{10,2},{3,11},{11,3},{4,12},{12,4},... | collective-permute-start | bytes 589832 | tf_op jit(solution)/shard_map/ppermute | solution.py:31
  82.6 2.4 %collective-permute-start.19 = (bf16[128,768]{1,0:T(8,128)(2,1)S(1)}, bf16[128,768]{1,0:T(8,128)(2,1)S(1)}, u32[]{:S(2)}, u32[]{:S(2)}) collective-permute-start(bf16[128,768]{1,0:T(8,128)(2,1)S(1)} %get-tuple-element.25), channel_id=1, source_target_pairs={{0,4},{2,6},{4,0},{6,2},{1,5},{3,7},{5,1},{7,3},{8,12},{10,14},{12... | collective-permute-start | bytes 589832 | tf_op jit(solution)/shard_map/ppermute | solution.py:31
  86.4 2.0 %collective-permute-done.18.a1_ref = bf16[128,768]{1,0:T(8,128)(2,1)S(1)} collective-permute-done((bf16[128,768]{1,0:T(8,128)(2,1)S(1)}, bf16[128,768]{1,0:T(8,128)(2,1)S(1)}, u32[]{:S(2)}, u32[]{:S(2)}) %collective-permute-start.18) | collective-permute-done | bytes 196640 | tf_op jit(solution)/shard_map/ppermute | solution.py:31
  88.4 5.3 %collective-permute-done.19.a2_ref = bf16[128,768]{1,0:T(8,128)(2,1)S(1)} collective-permute-done((bf16[128,768]{1,0:T(8,128)(2,1)S(1)}, bf16[128,768]{1,0:T(8,128)(2,1)S(1)}, u32[]{:S(2)}, u32[]{:S(2)}) %collective-permute-start.19) | collective-permute-done | bytes 196640 | tf_op jit(solution)/shard_map/ppermute | solution.py:31
  (43 shorter events, 18.3 us)
Async XLA Ops:
  0.0 13.9 %collective-permute-start = (bf16[2,2,128,2048]{3,2,1,0:T(8,128)(2,1)}, bf16[2,2,128,2048]{3,2,1,0:T(8,128)(2,1)S(1)}, u32[]{:S(2)}, u32[]{:S(2)}) collective-permute-start(bf16[2,2,128,2048]{3,2,1,0:T(8,128)(2,1)} %own_ref.1), channel_id=1, source_target_pairs={{0,1},{1,0},{2,3},{3,2},{4,5},{5,4},{6,7},{7,6},{8,9},{9,8},{10,11... | collective-permute-start | bytes 6291464 | tf_op jit(solution)/shard_map/ppermute | solution.py:31
  0.0 9.1 %collective-permute-start.4 = (bf16[2,2,128,256]{3,2,1,0:T(8,128)(2,1)}, bf16[2,2,128,256]{3,2,1,0:T(8,128)(2,1)S(1)}, u32[]{:S(2)}, u32[]{:S(2)}) collective-permute-start(bf16[2,2,128,256]{3,2,1,0:T(8,128)(2,1)} %m_ref.1), channel_id=1, source_target_pairs={{0,8},{8,0},{1,9},{9,1},{2,10},{10,2},{3,11},{11,3},{4,12},{12,4},... | collective-permute-start | bytes 786440 | tf_op jit(solution)/shard_map/ppermute | solution.py:31
  1.9 10.9 %collective-permute-start.2 = (bf16[2,2,128,256]{3,2,1,0:T(8,128)(2,1)}, bf16[2,2,128,256]{3,2,1,0:T(8,128)(2,1)S(1)}, u32[]{:S(2)}, u32[]{:S(2)}) collective-permute-start(bf16[2,2,128,256]{3,2,1,0:T(8,128)(2,1)} %m_ref.1), channel_id=1, source_target_pairs={{0,4},{2,6},{4,0},{6,2},{1,5},{3,7},{5,1},{7,3},{8,12},{10,14},{12... | collective-permute-start | bytes 786440 | tf_op jit(solution)/shard_map/ppermute | solution.py:31
  5.1 13.7 %collective-permute-start.1 = (bf16[2,2,128,256]{3,2,1,0:T(8,128)(2,1)}, bf16[2,2,128,256]{3,2,1,0:T(8,128)(2,1)S(1)}, u32[]{:S(2)}, u32[]{:S(2)}) collective-permute-start(bf16[2,2,128,256]{3,2,1,0:T(8,128)(2,1)} %m_ref.1), channel_id=1, source_target_pairs={{0,6},{2,0},{4,2},{6,4},{1,7},{3,1},{5,3},{7,5},{8,14},{10,8},{12,... | collective-permute-start | bytes 786440 | tf_op jit(solution)/shard_map/ppermute | solution.py:31
  6.2 12.6 %collective-permute-start.3 = (bf16[2,2,128,256]{3,2,1,0:T(8,128)(2,1)}, bf16[2,2,128,256]{3,2,1,0:T(8,128)(2,1)S(1)}, u32[]{:S(2)}, u32[]{:S(2)}) collective-permute-start(bf16[2,2,128,256]{3,2,1,0:T(8,128)(2,1)} %m_ref.1), channel_id=1, source_target_pairs={{0,2},{2,4},{4,6},{6,0},{1,3},{3,5},{5,7},{7,1},{8,10},{10,12},{12... | collective-permute-start | bytes 786440 | tf_op jit(solution)/shard_map/ppermute | solution.py:31
  9.1 14.6 %collective-permute-start.5 = (bf16[2,2,128,256]{3,2,1,0:T(8,128)(2,1)S(1)}, bf16[2,2,128,256]{3,2,1,0:T(8,128)(2,1)S(1)}, u32[]{:S(2)}, u32[]{:S(2)}) collective-permute-start(bf16[2,2,128,256]{3,2,1,0:T(8,128)(2,1)S(1)} %collective-permute-done.4.refs_4_), channel_id=1, source_target_pairs={{0,6},{2,0},{4,2},{6,4},{1,7},{3,1},{5,3},{7,5},{8,14},{10,8},{12,... | collective-permute-start | bytes 786440 | tf_op jit(solution)/shard_map/ppermute | solution.py:31
  12.8 10.9 %collective-permute-start.6 = (bf16[2,2,128,256]{3,2,1,0:T(8,128)(2,1)S(1)}, bf16[2,2,128,256]{3,2,1,0:T(8,128)(2,1)}, u32[]{:S(2)}, u32[]{:S(2)}) collective-permute-start(bf16[2,2,128,256]{3,2,1,0:T(8,128)(2,1)S(1)} %collective-permute-done.2.refs_2_), channel_id=1, source_target_pairs={{0,8},{8,0},{1,9},{9,1},{2,10},{10,2},{3,11},{11,3},{4,12},{12,4},... | collective-permute-start | bytes 786440 | tf_op jit(solution)/shard_map/ppermute | solution.py:31
  13.9 9.8 %collective-permute-start.7 = (bf16[2,2,128,256]{3,2,1,0:T(8,128)(2,1)S(1)}, bf16[2,2,128,256]{3,2,1,0:T(8,128)(2,1)}, u32[]{:S(2)}, u32[]{:S(2)}) collective-permute-start(bf16[2,2,128,256]{3,2,1,0:T(8,128)(2,1)S(1)} %collective-permute-done.4.refs_4_), channel_id=1, source_target_pairs={{0,2},{2,4},{4,6},{6,0},{1,3},{3,5},{5,7},{7,1},{8,10},{10,12},{12... | collective-permute-start | bytes 786440 | tf_op jit(solution)/shard_map/ppermute | solution.py:31
  26.5 29.8 %collective-permute-start.8 = (bf16[3,2,2,128,256]{4,3,2,1,0:T(8,128)(2,1)S(1)}, bf16[3,2,2,128,256]{4,3,2,1,0:T(8,128)(2,1)S(1)}, u32[]{:S(2)}, u32[]{:S(2)}) collective-permute-start(bf16[3,2,2,128,256]{4,3,2,1,0:T(8,128)(2,1)S(1)} %shard_map.47.mine_ref), channel_id=1, source_target_pairs={{0,1},{1,0},{2,3},{3,2},{4,5},{5,4},{6,7},{7,6},{8,9},{9,8},{10,11... | collective-permute-start | bytes 2359304 | tf_op jit(solution)/shard_map/ppermute | solution.py:31
  29.1 10.3 %collective-permute-start.13 = (bf16[2,128,512]{2,1,0:T(8,128)(2,1)S(1)}, bf16[2,128,512]{2,1,0:T(8,128)(2,1)S(1)}, u32[]{:S(2)}, u32[]{:S(2)}) collective-permute-start(bf16[2,128,512]{2,1,0:T(8,128)(2,1)S(1)} %shard_map.49.refs_0_), channel_id=1, source_target_pairs={{0,16},{16,0},{1,17},{17,1},{2,18},{18,2},{3,19},{19,3},{4,20},{20... | collective-permute-start | bytes 786440 | tf_op jit(solution)/shard_map/ppermute | solution.py:31
  32.8 10.7 %collective-permute-start.11 = (bf16[2,128,512]{2,1,0:T(8,128)(2,1)S(1)}, bf16[2,128,512]{2,1,0:T(8,128)(2,1)S(1)}, u32[]{:S(2)}, u32[]{:S(2)}) collective-permute-start(bf16[2,128,512]{2,1,0:T(8,128)(2,1)S(1)} %shard_map.49.refs_0_), channel_id=1, source_target_pairs={{0,64},{32,96},{64,0},{96,32},{1,65},{33,97},{65,1},{97,33},{2,66}... | collective-permute-start | bytes 786440 | tf_op jit(solution)/shard_map/ppermute | solution.py:31
  34.2 13.9 %collective-permute-start.10 = (bf16[2,128,512]{2,1,0:T(8,128)(2,1)S(1)}, bf16[2,128,512]{2,1,0:T(8,128)(2,1)S(1)}, u32[]{:S(2)}, u32[]{:S(2)}) collective-permute-start(bf16[2,128,512]{2,1,0:T(8,128)(2,1)S(1)} %shard_map.49.refs_0_), channel_id=1, source_target_pairs={{0,96},{32,0},{64,32},{96,64},{1,97},{33,1},{65,33},{97,65},{2,98}... | collective-permute-start | bytes 786440 | tf_op jit(solution)/shard_map/ppermute | solution.py:31
  34.2 15.5 %collective-permute-start.12 = (bf16[2,128,512]{2,1,0:T(8,128)(2,1)S(1)}, bf16[2,128,512]{2,1,0:T(8,128)(2,1)S(1)}, u32[]{:S(2)}, u32[]{:S(2)}) collective-permute-start(bf16[2,128,512]{2,1,0:T(8,128)(2,1)S(1)} %shard_map.49.refs_0_), channel_id=1, source_target_pairs={{0,32},{32,64},{64,96},{96,0},{1,33},{33,65},{65,97},{97,1},{2,34}... | collective-permute-start | bytes 786440 | tf_op jit(solution)/shard_map/ppermute | solution.py:31
  39.4 14.2 %collective-permute-start.14 = (bf16[2,128,512]{2,1,0:T(8,128)(2,1)S(1)}, bf16[2,128,512]{2,1,0:T(8,128)(2,1)S(1)}, u32[]{:S(2)}, u32[]{:S(2)}) collective-permute-start(bf16[2,128,512]{2,1,0:T(8,128)(2,1)S(1)} %collective-permute-done.13.refs_4_), channel_id=1, source_target_pairs={{0,96},{32,0},{64,32},{96,64},{1,97},{33,1},{65,33},{97,65},{2,98}... | collective-permute-start | bytes 786440 | tf_op jit(solution)/shard_map/ppermute | solution.py:31
  43.5 10.1 %collective-permute-start.15 = (bf16[2,128,512]{2,1,0:T(8,128)(2,1)S(1)}, bf16[2,128,512]{2,1,0:T(8,128)(2,1)S(1)}, u32[]{:S(2)}, u32[]{:S(2)}) collective-permute-start(bf16[2,128,512]{2,1,0:T(8,128)(2,1)S(1)} %collective-permute-done.11.refs_2_), channel_id=1, source_target_pairs={{0,16},{16,0},{1,17},{17,1},{2,18},{18,2},{3,19},{19,3},{4,20},{20... | collective-permute-start | bytes 786440 | tf_op jit(solution)/shard_map/ppermute | solution.py:31
  48.1 8.1 %collective-permute-start.16 = (bf16[2,128,512]{2,1,0:T(8,128)(2,1)S(1)}, bf16[2,128,512]{2,1,0:T(8,128)(2,1)S(1)}, u32[]{:S(2)}, u32[]{:S(2)}) collective-permute-start(bf16[2,128,512]{2,1,0:T(8,128)(2,1)S(1)} %collective-permute-done.13.refs_4_), channel_id=1, source_target_pairs={{0,32},{32,64},{64,96},{96,0},{1,33},{33,65},{65,97},{97,1},{2,34}... | collective-permute-start | bytes 786440 | tf_op jit(solution)/shard_map/ppermute | solution.py:31
  58.2 22.7 %collective-permute-start.17 = (bf16[4,128,768]{2,1,0:T(8,128)(2,1)S(1)}, bf16[4,128,768]{2,1,0:T(8,128)(2,1)S(1)}, u32[]{:S(2)}, u32[]{:S(2)}) collective-permute-start(bf16[4,128,768]{2,1,0:T(8,128)(2,1)S(1)} %get-tuple-element.22), channel_id=1, source_target_pairs={{0,8},{8,0},{1,9},{9,1},{2,10},{10,2},{3,11},{11,3},{4,12},{12,4},... | collective-permute-start | bytes 2359304 | tf_op jit(solution)/shard_map/ppermute | solution.py:31
  58.3 12.5 %collective-permute-start.21 = (bf16[2,128,768]{2,1,0:T(8,128)(2,1)S(1)}, bf16[2,128,768]{2,1,0:T(8,128)(2,1)S(1)}, u32[]{:S(2)}, u32[]{:S(2)}) collective-permute-start(bf16[2,128,768]{2,1,0:T(8,128)(2,1)S(1)} %get-tuple-element.28), channel_id=1, source_target_pairs={{0,2},{2,4},{4,6},{6,0},{1,3},{3,5},{5,7},{7,1},{8,10},{10,12},{12... | collective-permute-start | bytes 1179656 | tf_op jit(solution)/shard_map/ppermute | solution.py:31
  59.8 19.1 %collective-permute-start.22 = (bf16[2,128,768]{2,1,0:T(8,128)(2,1)S(1)}, bf16[2,128,768]{2,1,0:T(8,128)(2,1)S(1)}, u32[]{:S(2)}, u32[]{:S(2)}) collective-permute-start(bf16[2,128,768]{2,1,0:T(8,128)(2,1)S(1)} %get-tuple-element.29), channel_id=1, source_target_pairs={{0,4},{2,6},{4,0},{6,2},{1,5},{3,7},{5,1},{7,3},{8,12},{10,14},{12... | collective-permute-start | bytes 1179656 | tf_op jit(solution)/shard_map/ppermute | solution.py:31
  62.5 16.5 %collective-permute-start.23 = (bf16[2,128,768]{2,1,0:T(8,128)(2,1)S(1)}, bf16[2,128,768]{2,1,0:T(8,128)(2,1)S(1)}, u32[]{:S(2)}, u32[]{:S(2)}) collective-permute-start(bf16[2,128,768]{2,1,0:T(8,128)(2,1)S(1)} %get-tuple-element.30), channel_id=1, source_target_pairs={{0,6},{2,0},{4,2},{6,4},{1,7},{3,1},{5,3},{7,5},{8,14},{10,8},{12,... | collective-permute-start | bytes 1179656 | tf_op jit(solution)/shard_map/ppermute | solution.py:31
  79.1 7.3 %collective-permute-start.24 = (bf16[128,768]{1,0:T(8,128)(2,1)S(1)}, bf16[128,768]{1,0:T(8,128)(2,1)S(1)}, u32[]{:S(2)}, u32[]{:S(2)}) collective-permute-start(bf16[128,768]{1,0:T(8,128)(2,1)S(1)} %get-tuple-element.32), channel_id=1, source_target_pairs={{0,8},{8,0},{1,9},{9,1},{2,10},{10,2},{3,11},{11,3},{4,12},{12,4},... | collective-permute-start | bytes 589832 | tf_op jit(solution)/shard_map/ppermute | solution.py:31
  81.1 7.3 %collective-permute-start.18 = (bf16[128,768]{1,0:T(8,128)(2,1)S(1)}, bf16[128,768]{1,0:T(8,128)(2,1)S(1)}, u32[]{:S(2)}, u32[]{:S(2)}) collective-permute-start(bf16[128,768]{1,0:T(8,128)(2,1)S(1)} %get-tuple-element.24), channel_id=1, source_target_pairs={{0,2},{2,4},{4,6},{6,0},{1,3},{3,5},{5,7},{7,1},{8,10},{10,12},{12... | collective-permute-start | bytes 589832 | tf_op jit(solution)/shard_map/ppermute | solution.py:31
  82.6 11.1 %collective-permute-start.19 = (bf16[128,768]{1,0:T(8,128)(2,1)S(1)}, bf16[128,768]{1,0:T(8,128)(2,1)S(1)}, u32[]{:S(2)}, u32[]{:S(2)}) collective-permute-start(bf16[128,768]{1,0:T(8,128)(2,1)S(1)} %get-tuple-element.25), channel_id=1, source_target_pairs={{0,4},{2,6},{4,0},{6,2},{1,5},{3,7},{5,1},{7,3},{8,12},{10,14},{12... | collective-permute-start | bytes 589832 | tf_op jit(solution)/shard_map/ppermute | solution.py:31
  85.0 8.7 %collective-permute-start.20 = (bf16[128,768]{1,0:T(8,128)(2,1)S(1)}, bf16[128,768]{1,0:T(8,128)(2,1)S(1)}, u32[]{:S(2)}, u32[]{:S(2)}) collective-permute-start(bf16[128,768]{1,0:T(8,128)(2,1)S(1)} %get-tuple-element.26), channel_id=1, source_target_pairs={{0,6},{2,0},{4,2},{6,4},{1,7},{3,1},{5,3},{7,5},{8,14},{10,8},{12,... | collective-permute-start | bytes 589832 | tf_op jit(solution)/shard_map/ppermute | solution.py:31
  (4 other events, 10.8 us)

commit v2 on v1

v2 whole, which is shorter than its diff:
```python
import functools
import math

import jax
import jax.numpy as jnp
from jax import lax
from jax.experimental import pallas as pl
from jax.experimental.pallas import tpu as pltpu
from jax.sharding import Mesh, PartitionSpec as P

BF = jnp.bfloat16
F32 = jnp.float32
MIB = 1024 * 1024
VMEM = pl.BlockSpec(memory_space=pltpu.VMEM)
SMEM = pl.BlockSpec(memory_space=pltpu.SMEM)
ANY = pl.BlockSpec(memory_space=pl.ANY)
PAIRS = ((0, 0), (0, 1), (1, 1))
CUT = 256
WIDE_Y = 512 + CUT
WIDE_Z = 1024 - CUT


def call(body, outs, specs, *args, scratch=(), limit=2):
    return pl.pallas_call(
        body,
        out_shape=[jax.ShapeDtypeStruct(s, BF) for s in outs],
        in_specs=specs,
        out_specs=[VMEM] * len(outs),
        scratch_shapes=list(scratch),
        compiler_params=pltpu.CompilerParams(vmem_limit_bytes=limit * MIB),
    )(*args)


def copy_all(moves, sems):
    copies = [pltpu.make_async_copy(src, dst, sems.at[i]) for i, (src, dst) in enumerate(moves)]
    for copy in copies:
        copy.start()
    return copies


def transpose_halves(m_ref, mine_ref, other_ref):
    c = lax.axis_index("c")
    for k in range(2):
        for part in range(2):
            lanes = slice(part * 128, (part + 1) * 128)
            mine_ref[k, :, lanes] = m_ref[k, part, :, pl.ds(pl.multiple_of(c * 128, 128), 128)].T
            other_ref[k, :, lanes] = m_ref[k, part, :, pl.ds(pl.multiple_of((1 - c) * 128, 128), 128)].T


def join_halves(mine_ref, got_ref, out_ref):
    out_ref[:, :, :256] = mine_ref[...]
    out_ref[:, :, 256:] = got_ref[...]


def join(a_ref, b_ref, out_ref, sems):
    for copy in copy_all([(a_ref, out_ref.at[0]), (b_ref, out_ref.at[1])], sems):
        copy.wait()


def ring_masks():
    c = lax.axis_index("c")
    return (0, 1 + 2 * c, 3 - 2 * c, 2)


def pair_row(list_ref, pair):
    row = 0
    for r in range(1, 3):
        row = jnp.where((list_ref[0, r] == pair[0]) & (list_ref[1, r] == pair[1]), r, row)
    return row


def weight_rows(list_ref, q_ref, own_ref, mate_ref, out_ref, held, sems):
    zl, y, c = lax.axis_index("zl"), lax.axis_index("y"), lax.axis_index("c")
    moves = []
    for slot in range(2):
        q = q_ref[pair_row(list_ref, PAIRS[slot])]
        for o, ref in enumerate((own_ref, mate_ref)):
            moves.append((ref.at[q], held.at[slot, o]))
    copies = copy_all(moves, sems)
    for slot in range(2):
        for o in range(2):
            copies[slot * 2 + o].wait()
            for b in range(2):
                for s, mask in enumerate(ring_masks()):
                    block = (zl ^ b) * 4 + (y ^ mask)
                    lanes = pl.ds(pl.multiple_of(block * 256 + c * 128, 128), 128)
                    re, im = held[slot, o, 0, :, lanes], held[slot, o, 1, :, lanes]
                    row, col = o * 256, (b * 4 + s) * 256
                    out_ref[slot, row : row + 128, col : col + 128] = re
                    out_ref[slot, row : row + 128, col + 128 : col + 256] = -im
                    out_ref[slot, row + 128 : row + 256, col : col + 128] = im
                    out_ref[slot, row + 128 : row + 256, col + 128 : col + 256] = re


def screen(w_ref, *refs):
    pieces, (out_ref, acc, held, sems) = refs[:4], refs[4:]
    copies = copy_all([(ref, held.at[i]) for i, ref in enumerate(pieces)], sems)
    for i in range(8):
        if i % 2 == 0:
            copies[i // 2].wait()
        cols = slice(i * 256, (i + 1) * 256)
        for p, (k, kp) in enumerate(PAIRS):
            rhs = held[i // 2, i % 2, kp].reshape(256, 256)
            term = jnp.dot(w_ref[kp - k, :, cols], rhs, preferred_element_type=F32)
            if i == 0:
                acc[p] = term
            else:
                acc[p] += term
    out_ref[...] = acc[...].reshape(3, 2, 2, 128, 256).astype(BF)


def right_side(p, mine_ref, got_ref):
    blocks = []
    for o in range(2):
        re = (mine_ref[p, o, 0].astype(F32) + got_ref[p, 1 - o, 0].astype(F32)).astype(BF)
        im = (mine_ref[p, o, 1].astype(F32) + got_ref[p, 1 - o, 1].astype(F32)).astype(BF)
        blocks += [jnp.concatenate((re, im), 1), jnp.concatenate((im, -re), 1)]
    return jnp.concatenate(blocks, 0)


def rows_for(b, s, k, pieces):
    x, zh, zl, y, c = (lax.axis_index(a) for a in ("x", "zh", "zl", "y", "c"))
    j = (zl ^ b) * 4 + lax.rem(y + s, 4)
    mask = (j // 2) ^ x
    near = (mask == 0) | (mask == 1 + 2 * c)
    unit = jnp.where((mask == 0) | (mask == 3 - 2 * c), 0, 1)
    same = lax.rem(j, 2) == zh
    values = [ref[unit, k] for ref in pieces]
    own = jnp.where(near, values[0], values[1])
    far = jnp.where(near, values[2], values[3])
    return jnp.where(same, own, far)


def contract_y(factor, mine_ref, got_ref, r0, r1, r2, r3, k_ref, s1_ref, s2_ref, s3_ref, rest_ref):
    rhs = [right_side(p, mine_ref, got_ref) for p in range(2)]
    for b in range(2):
        for s, ref in enumerate((k_ref, s1_ref, s2_ref, s3_ref)):
            rows = rows_for(b, s, 0, (r0, r1, r2, r3))
            for p in range(2):
                part = jnp.dot(rows, rhs[p], preferred_element_type=F32)
                part = (part * factor).astype(BF)
                if p == 0:
                    ref[b, :, :512] = part
                else:
                    ref[b, :, 512:] = part[:, :CUT]
                    rest_ref[b, s] = part[:, CUT:]


def contract_z(factor, mine_ref, got_ref, r0, r1, r2, r3, rest_ref, k_ref, s_ref):
    rhs = right_side(2, mine_ref, got_ref)
    for b, ref in enumerate((k_ref, s_ref)):
        for s in range(4):
            part = jnp.dot(rows_for(b, s, 1, (r0, r1, r2, r3)), rhs, preferred_element_type=F32)
            ref[s, :, :512] = (part * factor).astype(BF)
            ref[s, :, 512:] = rest_ref[b, s]


def add_z(keep_ref, got_ref, *outs):
    for s, ref in enumerate(outs):
        ref[...] = (keep_ref[s].astype(F32) + got_ref[s].astype(F32)).astype(BF)


def add_y(keep_ref, g1_ref, g2_ref, g3_ref, out_ref, send_ref):
    for b, ref in enumerate((out_ref, send_ref)):
        near = keep_ref[b].astype(F32) + g1_ref[b].astype(F32)
        ref[...] = (near + (g2_ref[b].astype(F32) + g3_ref[b].astype(F32))).astype(BF)


def finish(list_ref, z0_ref, z1_ref, z2_ref, z3_ref, y0_ref, y1_ref, out_ref):
    z = z0_ref[...].astype(F32) + z1_ref[...].astype(F32) + (z2_ref[...].astype(F32) + z3_ref[...].astype(F32))
    y = y0_ref[...].astype(F32) + y1_ref[...].astype(F32)
    sums = (y[:, :512], jnp.concatenate((y[:, 512:], z[:, 512:]), 1), z[:, :512])
    for pair, value in zip(PAIRS, sums):
        out_ref[pair_row(list_ref, pair)] = value.astype(BF)


def shift(x, axis, size, step):
    return lax.ppermute(x, axis, [(i, (i + step) % size) for i in range(size)])


def ring_swap(x, axis, second):
    pairs = [(i * 2 + c, (i ^ (3 if c ^ second else 1)) * 2 + c) for i in range(4) for c in range(2)]
    return lax.ppermute(x, (axis, "c"), pairs)


def double(x, got):
    return call(join, [(2,) + x.shape], [ANY] * 2, x, got, scratch=[pltpu.SemaphoreType.DMA((2,))])[0]


def tie(*xs):
    return lax.optimization_barrier(xs)


def per_device(matrix_elements, screening, pair_list, pair_q):
    factor = 1.0 / math.sqrt(2.0 * screening.shape[3])
    m, pairs = matrix_elements, pair_list.T
    mine, other = call(transpose_halves, [(2, 128, 256)] * 2, [VMEM], m)
    (rows,) = call(join_halves, [(2, 128, 512)], [VMEM] * 2, mine, shift(other, "c", 2, 1))
    mate_weights = shift(screening, "c", 2, 1)
    m_far = shift(m, "zl", 2, 1)
    m_got = ring_swap(m, "y", 0)
    rows_far = shift(rows, "zh", 2, 1)
    rows_got = ring_swap(rows, "x", 0)
    m_near = double(m, m_got)
    m_next = ring_swap(m_near, "y", 1)
    rows_near = double(rows, rows_got)
    rows_next = ring_swap(rows_near, "x", 1)
    m_far_got = ring_swap(m_far, "y", 0)
    m_far_got, rows_far = tie(m_far_got, rows_far)
    rows_far_got = ring_swap(rows_far, "x", 0)
    m_far_near = double(m_far, m_far_got)
    m_far_next = ring_swap(m_far_near, "y", 1)
    rows_far_near = double(rows_far, rows_far_got)
    rows_far_next = ring_swap(rows_far_near, "x", 1)
    (weights,) = call(
        weight_rows,
        [(2, 512, 2048)],
        [SMEM] * 2 + [ANY] * 2,
        pairs,
        pair_q,
        screening,
        mate_weights,
        limit=8,
        scratch=[pltpu.VMEM((2, 2, 2, 128, 2048), BF), pltpu.SemaphoreType.DMA((4,))],
    )
    weights, rows_next = tie(weights, rows_next)
    (part,) = call(
        screen,
        [(3, 2, 2, 128, 256)],
        [VMEM] + [ANY] * 4,
        weights,
        m_near,
        m_next,
        m_far_near,
        m_far_next,
        limit=8,
        scratch=[pltpu.VMEM((3, 512, 256), F32), pltpu.VMEM((4, 2, 2, 2, 128, 256), BF), pltpu.SemaphoreType.DMA((4,))],
    )
    left = [part, shift(part, "c", 2, 1), rows_near, rows_next, rows_far_near, rows_far_next]
    y_keep, y1, y2, y3, rest = call(
        functools.partial(contract_y, factor),
        [(2, 128, WIDE_Y)] * 4 + [(2, 4, 128, 512 - CUT)],
        [VMEM] * 6,
        *left,
        limit=8,
    )
    z_keep, z_send = call(
        functools.partial(contract_z, factor), [(4, 128, WIDE_Z)] * 2, [VMEM] * 7, *left, rest, limit=8
    )
    z_got = shift(z_send, "zl", 2, 1)
    y_got = [shift(y1, "y", 4, 1), shift(y2, "y", 4, 2), shift(y3, "y", 4, -1)]
    z_sums = call(add_z, [(128, WIDE_Z)] * 4, [VMEM] * 2, z_keep, z_got)
    y_keep, y_send = call(add_y, [(128, WIDE_Y)] * 2, [VMEM] * 4, y_keep, *y_got)
    z_last = [shift(z_sums[1], "y", 4, 1), shift(z_sums[2], "y", 4, 2), shift(z_sums[3], "y", 4, -1)]
    y_last = shift(y_send, "zl", 2, 1)
    (out,) = call(finish, [(3, 128, 512)], [SMEM] + [VMEM] * 6, pairs, z_sums[0], *z_last, y_keep, y_last)
    return out.reshape(3, 128, 2, 256)


def solution(mesh):
    split = Mesh(mesh.devices.reshape(4, 2, 2, 4, 2), ("x", "zh", "zl", "y", "c"))
    ga = ("zl", "y", "c")
    return jax.shard_map(
        per_device,
        mesh=split,
        in_specs=(P(None, None, ga, ("x", "zh")), P(None, None, ga, None), P(), P()),
        out_specs=P(None, ga, None, ("x", "zh")),
        check_vma=False,
    )
```

time: 95.5 us -> 82 us (0.86)
  waiting for transfers between devices: 47.9 us -> 39.7 us
  starting transfers between devices: 36.1 us -> 30.5 us
  local copies, waits for them, and re-layouts: 3.85 us -> 0.85 us
  Pallas kernels: 7.27 us -> 10 us
    ppermute x25 -> x13, waiting for transfers between devices: 47.9 us -> 26.6 us  [shift(): return lax.ppermute(x, axis, [(i, (i + step) % size) for i in range(size)])]
    ppermute x25 -> x13, starting transfers between devices: 36.1 us -> 17.2 us  [shift(): return lax.ppermute(x, axis, [(i, (i + step) % size) for i in range(size)])]
    ppermute x0 -> x8, starting transfers between devices: none -> 13.3 us  [ring_swap(): return lax.ppermute(x, (axis, 'c'), pairs)]
    ppermute x0 -> x8, waiting for transfers between devices: none -> 13.2 us  [ring_swap(): return lax.ppermute(x, (axis, 'c'), pairs)]
    unnamed x7 -> x6, local copies, waits for them, and re-layouts: 3.01 us -> 0.01 us
    pallas_call x9 -> x13, Pallas kernels: 7.27 us -> 10 us  [call(): pl.pallas_call(body, out_shape=[jax.ShapeDtypeStruct(s, BF) for s in outs...]
  transfers between devices with their start and end apart: 25 -> 21, of which waited for: 13 -> 9; matrix products, arithmetic and copies ran while one was open for 1% -> 0% of each run, Pallas kernels for 2% -> 9%
where the time goes in v2:
time: 82 us; the launch traced here: 81.3 us
  waiting for transfers between devices  39.7 us (48%)
  starting transfers between devices  30.5 us (37%)
  Pallas kernels  10 us (12%)
  local copies, waits for them, and re-layouts  0.85 us (1%)
    ppermute x13, waiting for transfers between devices, shift(): return lax.ppermute(x, axis, [(i, (i + step) % size) for i in range(size)])  26.6 us
    ppermute x13, starting transfers between devices, shift(): return lax.ppermute(x, axis, [(i, (i + step) % size) for i in range(size)])  17.2 us
    ppermute x8, starting transfers between devices, ring_swap(): return lax.ppermute(x, (axis, 'c'), pairs)  13.3 us
    ppermute x8, waiting for transfers between devices, ring_swap(): return lax.ppermute(x, (axis, 'c'), pairs)  13.2 us
    pallas_call x13, Pallas kernels, call(): pl.pallas_call(body, out_shape=[jax.ShapeDtypeStruct(s, BF) for s in outs...  10 us
  transfers between devices with their start and end apart: 21, of which 9 were waited for; matrix products, arithmetic and copies ran while one was open for 0% of the time, Pallas kernels for 9%

profile of v2, /device:TPU:6, one launch (start us, length us, event | category | flops | bytes accessed | tf_op | source)
XLA Modules:
  0.0 81.3 jit_solution(12673520069093996074)
XLA Ops:
  0.1 2.0 %collective-permute-start.6 = (bf16[2,2,128,256]{3,2,1,0:T(8,128)(2,1)}, bf16[2,2,128,256]{3,2,1,0:T(8,128)(2,1)S(1)}, u32[]{:S(2)}, u32[]{:S(2)}) collective-permute-start(bf16[2,2,128,256]{3,2,1,0:T(8,128)(2,1)} %a_ref.1), channel_id=1, source_target_pairs={{0,8},{8,0},{1,9},{9,1},{2,10},{10,2},{3,11},{11,3},{4,12},{12,4},... | collective-permute-start | bytes 786440 | tf_op jit(solution)/shard_map/ppermute | solution.py:178
  2.1 1.1 %shard_map.47 = (bf16[2,128,256]{2,1,0:T(8,128)(2,1)S(1)}, bf16[2,128,256]{2,1,0:T(8,128)(2,1)S(1)}) custom-call(bf16[2,2,128,256]{3,2,1,0:T(8,128)(2,1)} %a_ref.1), custom_call_target="tpu_custom_call" | custom-call | tf_op jit(solution)/shard_map/pallas_call | solution.py:24
  3.4 1.6 %collective-permute-start.4 = (bf16[2,2,128,256]{3,2,1,0:T(8,128)(2,1)}, bf16[2,2,128,256]{3,2,1,0:T(8,128)(2,1)S(1)}, u32[]{:S(2)}, u32[]{:S(2)}) collective-permute-start(bf16[2,2,128,256]{3,2,1,0:T(8,128)(2,1)} %a_ref.1), channel_id=1, source_target_pairs={{0,2},{1,7},{2,0},{3,5},{4,6},{5,3},{6,4},{7,1},{8,10},{9,15},{10,... | collective-permute-start | bytes 786440 | tf_op jit(solution)/shard_map/ppermute | solution.py:183
  6.0 3.6 %collective-permute-start.8 = (bf16[2,128,512]{2,1,0:T(8,128)(2,1)S(1)}, bf16[2,128,512]{2,1,0:T(8,128)(2,1)S(1)}, u32[]{:S(2)}, u32[]{:S(2)}) collective-permute-start(bf16[2,128,512]{2,1,0:T(8,128)(2,1)S(1)} %shard_map.48.a_ref), channel_id=1, source_target_pairs={{0,16},{16,0},{1,17},{17,1},{2,18},{18,2},{3,19},{19,3},{4,20},{20... | collective-permute-start | bytes 786440 | tf_op jit(solution)/shard_map/ppermute | solution.py:178
  9.5 1.3 %collective-permute-start.7 = (bf16[2,2,128,256]{3,2,1,0:T(8,128)(2,1)S(1)}, bf16[2,2,128,256]{3,2,1,0:T(8,128)(2,1)S(1)}, u32[]{:S(2)}, u32[]{:S(2)}) collective-permute-start(bf16[2,2,128,256]{3,2,1,0:T(8,128)(2,1)S(1)} %collective-permute-done.6.a_ref), channel_id=1, source_target_pairs={{0,2},{1,7},{2,0},{3,5},{4,6},{5,3},{6,4},{7,1},{8,10},{9,15},{10,... | collective-permute-start | bytes 786440 | tf_op jit(solution)/shard_map/ppermute | solution.py:183
  11.8 2.3 %collective-permute-start.5 = (bf16[2,2,2,128,256]{4,3,2,1,0:T(8,128)(2,1)S(1)}, bf16[2,2,2,128,256]{4,3,2,1,0:T(8,128)(2,1)S(1)}, u32[]{:S(2)}, u32[]{:S(2)}) collective-permute-start(bf16[2,2,2,128,256]{4,3,2,1,0:T(8,128)(2,1)S(1)} %shard_map.50.refs_0_), channel_id=1, source_target_pairs={{0,6},{1,3},{2,4},{3,1},{4,2},{5,7},{6,0},{7,5},{8,14},{9,11},{10,... | collective-permute-start | bytes 1572872 | tf_op jit(solution)/shard_map/ppermute | solution.py:183
  14.2 1.2 %collective-permute-start.3 = (bf16[2,2,128,512]{3,2,1,0:T(8,128)(2,1)S(1)}, bf16[2,2,128,512]{3,2,1,0:T(8,128)(2,1)S(1)}, u32[]{:S(2)}, u32[]{:S(2)}) collective-permute-start(bf16[2,2,128,512]{3,2,1,0:T(8,128)(2,1)S(1)} %shard_map.49.r0), channel_id=1, source_target_pairs={{0,96},{1,33},{32,64},{33,1},{64,32},{65,97},{96,0},{97,65},{2,98}... | collective-permute-start | bytes 1572872 | tf_op jit(solution)/shard_map/ppermute | solution.py:183
  15.4 2.8 %collective-permute-done.8.a_ref = bf16[2,128,512]{2,1,0:T(8,128)(2,1)S(1)} collective-permute-done((bf16[2,128,512]{2,1,0:T(8,128)(2,1)S(1)}, bf16[2,128,512]{2,1,0:T(8,128)(2,1)S(1)}, u32[]{:S(2)}, u32[]{:S(2)}) %collective-permute-start.8) | collective-permute-done | bytes 262176 | tf_op jit(solution)/shard_map/ppermute | solution.py:178
  18.2 3.1 %collective-permute-start.9 = (bf16[2,2,2,128,256]{4,3,2,1,0:T(8,128)(2,1)S(1)}, bf16[2,2,2,128,256]{4,3,2,1,0:T(8,128)(2,1)S(1)}, u32[]{:S(2)}, u32[]{:S(2)}) collective-permute-start(bf16[2,2,2,128,256]{4,3,2,1,0:T(8,128)(2,1)S(1)} %shard_map.51.refs_2_), channel_id=1, source_target_pairs={{0,6},{1,3},{2,4},{3,1},{4,2},{5,7},{6,0},{7,5},{8,14},{9,11},{10,... | collective-permute-start | bytes 1572872 | tf_op jit(solution)/shard_map/ppermute | solution.py:183
  22.1 1.7 %shard_map.46.w_ref = bf16[2,512,2048]{2,1,0:T(8,128)(2,1)S(1)} custom-call(s32[2,3]{1,0:T(2,128)S(1)} %bitcast.1, s32[3]{0:T(128)S(1)} %copy-done.2, bf16[2,2,128,2048]{3,2,1,0:T(8,128)(2,1)S(1)} %copy-done, bf16[2,2,128,2048]{3,2,1,0:T(8,128)(2,1)S(1)} %collective-permute-done.mate_ref), custom_call_target="tpu_custom_call" | custom-call | tf_op jit(solution)/shard_map/pallas_call | solution.py:24
  23.8 2.4 %collective-permute-done.3.r1 = bf16[2,2,128,512]{3,2,1,0:T(8,128)(2,1)S(1)} collective-permute-done((bf16[2,2,128,512]{3,2,1,0:T(8,128)(2,1)S(1)}, bf16[2,2,128,512]{3,2,1,0:T(8,128)(2,1)S(1)}, u32[]{:S(2)}, u32[]{:S(2)}) %collective-permute-start.3) | collective-permute-done | bytes 524320 | tf_op jit(solution)/shard_map/ppermute | solution.py:183
  26.2 2.5 %collective-permute-done.9.refs_3_ = bf16[2,2,2,128,256]{4,3,2,1,0:T(8,128)(2,1)S(1)} collective-permute-done((bf16[2,2,2,128,256]{4,3,2,1,0:T(8,128)(2,1)S(1)}, bf16[2,2,2,128,256]{4,3,2,1,0:T(8,128)(2,1)S(1)}, u32[]{:S(2)}, u32[]{:S(2)}) %collective-permute-start.9) | collective-permute-done | bytes 524320 | tf_op jit(solution)/shard_map/ppermute | solution.py:183
  28.7 3.0 %shard_map.52.mine_ref = bf16[3,2,2,128,256]{4,3,2,1,0:T(8,128)(2,1)S(1)} custom-call(bf16[2,512,2048]{2,1,0:T(8,128)(2,1)S(1)} %shard_map.46.w_ref, bf16[2,2,2,128,256]{4,3,2,1,0:T(8,128)(2,1)S(1)} %shard_map.50.refs_0_, bf16[2,2,2,128,256]{4,3,2,1,0:T(8,128)(2,1)S(1)} %collective-permute-done.5.refs_1_, ...), custom_call_target="tpu_custom_call" | custom-call | tf_op jit(solution)/shard_map/pallas_call | solution.py:24
  31.8 2.2 %collective-permute-start.12 = (bf16[2,2,128,512]{3,2,1,0:T(8,128)(2,1)S(1)}, bf16[2,2,128,512]{3,2,1,0:T(8,128)(2,1)S(1)}, u32[]{:S(2)}, u32[]{:S(2)}) collective-permute-start(bf16[2,2,128,512]{3,2,1,0:T(8,128)(2,1)S(1)} %shard_map.53.r2), channel_id=1, source_target_pairs={{0,96},{1,33},{32,64},{33,1},{64,32},{65,97},{96,0},{97,65},{2,98}... | collective-permute-start | bytes 1572872 | tf_op jit(solution)/shard_map/ppermute | solution.py:183
  34.0 8.3 %collective-permute-done.12.r3 = bf16[2,2,128,512]{3,2,1,0:T(8,128)(2,1)S(1)} collective-permute-done((bf16[2,2,128,512]{3,2,1,0:T(8,128)(2,1)S(1)}, bf16[2,2,128,512]{3,2,1,0:T(8,128)(2,1)S(1)}, u32[]{:S(2)}, u32[]{:S(2)}) %collective-permute-start.12) | collective-permute-done | bytes 524320 | tf_op jit(solution)/shard_map/ppermute | solution.py:183
  42.3 1.3 %shard_map.54 = (bf16[2,128,768]{2,1,0:T(8,128)(2,1)S(1)}, bf16[2,128,768]{2,1,0:T(8,128)(2,1)S(1)}, bf16[2,128,768]{2,1,0:T(8,128)(2,1)S(1)}, bf16[2,128,768]{2...) custom-call(bf16[3,2,2,128,256]{4,3,2,1,0:T(8,128)(2,1)S(1)} %shard_map.52.mine_ref, ...), custom_call_target="tpu_custom_call" | custom-call | tf_op jit(solution)/shard_map/pallas_call | solution.py:24
  44.4 1.9 %collective-permute-start.13 = (bf16[4,128,768]{2,1,0:T(8,128)(2,1)S(1)}, bf16[4,128,768]{2,1,0:T(8,128)(2,1)S(1)}, u32[]{:S(2)}, u32[]{:S(2)}) collective-permute-start(bf16[4,128,768]{2,1,0:T(8,128)(2,1)S(1)} %get-tuple-element.32), channel_id=1, source_target_pairs={{0,8},{8,0},{1,9},{9,1},{2,10},{10,2},{3,11},{11,3},{4,12},{12,4},... | collective-permute-start | bytes 2359304 | tf_op jit(solution)/shard_map/ppermute | solution.py:178
  46.4 4.6 %collective-permute-start.18 = (bf16[2,128,768]{2,1,0:T(8,128)(2,1)S(1)}, bf16[2,128,768]{2,1,0:T(8,128)(2,1)S(1)}, u32[]{:S(2)}, u32[]{:S(2)}) collective-permute-start(bf16[2,128,768]{2,1,0:T(8,128)(2,1)S(1)} %get-tuple-element.39), channel_id=1, source_target_pairs={{0,4},{2,6},{4,0},{6,2},{1,5},{3,7},{5,1},{7,3},{8,12},{10,14},{12... | collective-permute-start | bytes 1179656 | tf_op jit(solution)/shard_map/ppermute | solution.py:178
  51.1 7.5 %collective-permute-done.17.g1_ref = bf16[2,128,768]{2,1,0:T(8,128)(2,1)S(1)} collective-permute-done((bf16[2,128,768]{2,1,0:T(8,128)(2,1)S(1)}, bf16[2,128,768]{2,1,0:T(8,128)(2,1)S(1)}, u32[]{:S(2)}, u32[]{:S(2)}) %collective-permute-start.17) | collective-permute-done | bytes 393248 | tf_op jit(solution)/shard_map/ppermute | solution.py:178
  58.6 7.9 %collective-permute-done.18.g2_ref = bf16[2,128,768]{2,1,0:T(8,128)(2,1)S(1)} collective-permute-done((bf16[2,128,768]{2,1,0:T(8,128)(2,1)S(1)}, bf16[2,128,768]{2,1,0:T(8,128)(2,1)S(1)}, u32[]{:S(2)}, u32[]{:S(2)}) %collective-permute-start.18) | collective-permute-done | bytes 393248 | tf_op jit(solution)/shard_map/ppermute | solution.py:178
  68.1 2.9 %collective-permute-start.15 = (bf16[128,768]{1,0:T(8,128)(2,1)S(1)}, bf16[128,768]{1,0:T(8,128)(2,1)S(1)}, u32[]{:S(2)}, u32[]{:S(2)}) collective-permute-start(bf16[128,768]{1,0:T(8,128)(2,1)S(1)} %get-tuple-element.35), channel_id=1, source_target_pairs={{0,4},{2,6},{4,0},{6,2},{1,5},{3,7},{5,1},{7,3},{8,12},{10,14},{12... | collective-permute-start | bytes 589832 | tf_op jit(solution)/shard_map/ppermute | solution.py:178
  71.4 1.1 %collective-permute-done.20.y1_ref = bf16[128,768]{1,0:T(8,128)(2,1)S(1)} collective-permute-done((bf16[128,768]{1,0:T(8,128)(2,1)S(1)}, bf16[128,768]{1,0:T(8,128)(2,1)S(1)}, u32[]{:S(2)}, u32[]{:S(2)}) %collective-permute-start.20) | collective-permute-done | bytes 196640 | tf_op jit(solution)/shard_map/ppermute | solution.py:178
  72.4 2.0 %collective-permute-done.14.z1_ref = bf16[128,768]{1,0:T(8,128)(2,1)S(1)} collective-permute-done((bf16[128,768]{1,0:T(8,128)(2,1)S(1)}, bf16[128,768]{1,0:T(8,128)(2,1)S(1)}, u32[]{:S(2)}, u32[]{:S(2)}) %collective-permute-start.14) | collective-permute-done | bytes 196640 | tf_op jit(solution)/shard_map/ppermute | solution.py:178
  74.4 5.3 %collective-permute-done.15.z2_ref = bf16[128,768]{1,0:T(8,128)(2,1)S(1)} collective-permute-done((bf16[128,768]{1,0:T(8,128)(2,1)S(1)}, bf16[128,768]{1,0:T(8,128)(2,1)S(1)}, u32[]{:S(2)}, u32[]{:S(2)}) %collective-permute-start.15) | collective-permute-done | bytes 196640 | tf_op jit(solution)/shard_map/ppermute | solution.py:178
  (38 shorter events, 7.9 us)
Async XLA Ops:
  0.0 22.1 %copy-start = (bf16[2,2,128,2048]{3,2,1,0:T(8,128)(2,1)S(1)}, bf16[2,2,128,2048]{3,2,1,0:T(8,128)(2,1)}, u32[]{:S(2)}) copy-start(bf16[2,2,128,2048]{3,2,1,0:T(8,128)(2,1)} %own_ref.1) | copy-start | bytes 6291460
  0.0 22.1 %copy-start.1 = (s32[3,2]{0,1:T(2,128)S(1)}, s32[3,2]{0,1:T(2,128)}, u32[]{:S(2)}) copy-start(s32[3,2]{0,1:T(2,128)} %param.6) | copy-start | bytes 76
  0.0 22.1 %copy-start.2 = (s32[3]{0:T(128)S(1)}, s32[3]{0:T(128)}, u32[]{:S(2)}) copy-start(s32[3]{0:T(128)} %q_ref.1) | copy-start | bytes 40
  0.0 22.1 %collective-permute-start = (bf16[2,2,128,2048]{3,2,1,0:T(8,128)(2,1)}, bf16[2,2,128,2048]{3,2,1,0:T(8,128)(2,1)S(1)}, u32[]{:S(2)}, u32[]{:S(2)}) collective-permute-start(bf16[2,2,128,2048]{3,2,1,0:T(8,128)(2,1)} %own_ref.1), channel_id=1, source_target_pairs={{0,1},{1,0},{2,3},{3,2},{4,5},{5,4},{6,7},{7,6},{8,9},{9,8},{10,11... | collective-permute-start | bytes 6291464 | tf_op jit(solution)/shard_map/ppermute | solution.py:178
  0.1 9.4 %collective-permute-start.6 = (bf16[2,2,128,256]{3,2,1,0:T(8,128)(2,1)}, bf16[2,2,128,256]{3,2,1,0:T(8,128)(2,1)S(1)}, u32[]{:S(2)}, u32[]{:S(2)}) collective-permute-start(bf16[2,2,128,256]{3,2,1,0:T(8,128)(2,1)} %a_ref.1), channel_id=1, source_target_pairs={{0,8},{8,0},{1,9},{9,1},{2,10},{10,2},{3,11},{11,3},{4,12},{12,4},... | collective-permute-start | bytes 786440 | tf_op jit(solution)/shard_map/ppermute | solution.py:178
  3.2 1.8 %collective-permute-start.1 = (bf16[2,128,256]{2,1,0:T(8,128)(2,1)S(1)}, bf16[2,128,256]{2,1,0:T(8,128)(2,1)S(1)}, u32[]{:S(2)}, u32[]{:S(2)}) collective-permute-start(bf16[2,128,256]{2,1,0:T(8,128)(2,1)S(1)} %get-tuple-element.25), channel_id=1, source_target_pairs={{0,1},{1,0},{2,3},{3,2},{4,5},{5,4},{6,7},{7,6},{8,9},{9,8},{10,11... | collective-permute-start | bytes 393224 | tf_op jit(solution)/shard_map/ppermute | solution.py:178
  3.4 7.4 %collective-permute-start.4 = (bf16[2,2,128,256]{3,2,1,0:T(8,128)(2,1)}, bf16[2,2,128,256]{3,2,1,0:T(8,128)(2,1)S(1)}, u32[]{:S(2)}, u32[]{:S(2)}) collective-permute-start(bf16[2,2,128,256]{3,2,1,0:T(8,128)(2,1)} %a_ref.1), channel_id=1, source_target_pairs={{0,2},{1,7},{2,0},{3,5},{4,6},{5,3},{6,4},{7,1},{8,10},{9,15},{10,... | collective-permute-start | bytes 786440 | tf_op jit(solution)/shard_map/ppermute | solution.py:183
  5.0 9.1 %collective-permute-start.2 = (bf16[2,128,512]{2,1,0:T(8,128)(2,1)S(1)}, bf16[2,128,512]{2,1,0:T(8,128)(2,1)S(1)}, u32[]{:S(2)}, u32[]{:S(2)}) collective-permute-start(bf16[2,128,512]{2,1,0:T(8,128)(2,1)S(1)} %shard_map.48.a_ref), channel_id=1, source_target_pairs={{0,32},{1,97},{32,0},{33,65},{64,96},{65,33},{96,64},{97,1},{2,34}... | collective-permute-start | bytes 786440 | tf_op jit(solution)/shard_map/ppermute | solution.py:183
  6.0 12.2 %collective-permute-start.8 = (bf16[2,128,512]{2,1,0:T(8,128)(2,1)S(1)}, bf16[2,128,512]{2,1,0:T(8,128)(2,1)S(1)}, u32[]{:S(2)}, u32[]{:S(2)}) collective-permute-start(bf16[2,128,512]{2,1,0:T(8,128)(2,1)S(1)} %shard_map.48.a_ref), channel_id=1, source_target_pairs={{0,16},{16,0},{1,17},{17,1},{2,18},{18,2},{3,19},{19,3},{4,20},{20... | collective-permute-start | bytes 786440 | tf_op jit(solution)/shard_map/ppermute | solution.py:178
  9.5 8.6 %collective-permute-start.7 = (bf16[2,2,128,256]{3,2,1,0:T(8,128)(2,1)S(1)}, bf16[2,2,128,256]{3,2,1,0:T(8,128)(2,1)S(1)}, u32[]{:S(2)}, u32[]{:S(2)}) collective-permute-start(bf16[2,2,128,256]{3,2,1,0:T(8,128)(2,1)S(1)} %collective-permute-done.6.a_ref), channel_id=1, source_target_pairs={{0,2},{1,7},{2,0},{3,5},{4,6},{5,3},{6,4},{7,1},{8,10},{9,15},{10,... | collective-permute-start | bytes 786440 | tf_op jit(solution)/shard_map/ppermute | solution.py:183
  11.8 14.4 %collective-permute-start.5 = (bf16[2,2,2,128,256]{4,3,2,1,0:T(8,128)(2,1)S(1)}, bf16[2,2,2,128,256]{4,3,2,1,0:T(8,128)(2,1)S(1)}, u32[]{:S(2)}, u32[]{:S(2)}) collective-permute-start(bf16[2,2,2,128,256]{4,3,2,1,0:T(8,128)(2,1)S(1)} %shard_map.50.refs_0_), channel_id=1, source_target_pairs={{0,6},{1,3},{2,4},{3,1},{4,2},{5,7},{6,0},{7,5},{8,14},{9,11},{10,... | collective-permute-start | bytes 1572872 | tf_op jit(solution)/shard_map/ppermute | solution.py:183
  14.2 12.0 %collective-permute-start.3 = (bf16[2,2,128,512]{3,2,1,0:T(8,128)(2,1)S(1)}, bf16[2,2,128,512]{3,2,1,0:T(8,128)(2,1)S(1)}, u32[]{:S(2)}, u32[]{:S(2)}) collective-permute-start(bf16[2,2,128,512]{3,2,1,0:T(8,128)(2,1)S(1)} %shard_map.49.r0), channel_id=1, source_target_pairs={{0,96},{1,33},{32,64},{33,1},{64,32},{65,97},{96,0},{97,65},{2,98}... | collective-permute-start | bytes 1572872 | tf_op jit(solution)/shard_map/ppermute | solution.py:183
  18.2 10.5 %collective-permute-start.9 = (bf16[2,2,2,128,256]{4,3,2,1,0:T(8,128)(2,1)S(1)}, bf16[2,2,2,128,256]{4,3,2,1,0:T(8,128)(2,1)S(1)}, u32[]{:S(2)}, u32[]{:S(2)}) collective-permute-start(bf16[2,2,2,128,256]{4,3,2,1,0:T(8,128)(2,1)S(1)} %shard_map.51.refs_2_), channel_id=1, source_target_pairs={{0,6},{1,3},{2,4},{3,1},{4,2},{5,7},{6,0},{7,5},{8,14},{9,11},{10,... | collective-permute-start | bytes 1572872 | tf_op jit(solution)/shard_map/ppermute | solution.py:183
  21.3 10.5 %collective-permute-start.11 = (bf16[2,128,512]{2,1,0:T(8,128)(2,1)S(1)}, bf16[2,128,512]{2,1,0:T(8,128)(2,1)S(1)}, u32[]{:S(2)}, u32[]{:S(2)}) collective-permute-start(bf16[2,128,512]{2,1,0:T(8,128)(2,1)S(1)} %collective-permute-done.8.a_ref), channel_id=1, source_target_pairs={{0,32},{1,97},{32,0},{33,65},{64,96},{65,33},{96,64},{97,1},{2,34}... | collective-permute-start | bytes 786440 | tf_op jit(solution)/shard_map/ppermute | solution.py:183
  31.7 10.6 %collective-permute-start.10 = (bf16[3,2,2,128,256]{4,3,2,1,0:T(8,128)(2,1)S(1)}, bf16[3,2,2,128,256]{4,3,2,1,0:T(8,128)(2,1)S(1)}, u32[]{:S(2)}, u32[]{:S(2)}) collective-permute-start(bf16[3,2,2,128,256]{4,3,2,1,0:T(8,128)(2,1)S(1)} %shard_map.52.mine_ref), channel_id=1, source_target_pairs={{0,1},{1,0},{2,3},{3,2},{4,5},{5,4},{6,7},{7,6},{8,9},{9,8},{10,11... | collective-permute-start | bytes 2359304 | tf_op jit(solution)/shard_map/ppermute | solution.py:178
  31.8 10.5 %collective-permute-start.12 = (bf16[2,2,128,512]{3,2,1,0:T(8,128)(2,1)S(1)}, bf16[2,2,128,512]{3,2,1,0:T(8,128)(2,1)S(1)}, u32[]{:S(2)}, u32[]{:S(2)}) collective-permute-start(bf16[2,2,128,512]{3,2,1,0:T(8,128)(2,1)S(1)} %shard_map.53.r2), channel_id=1, source_target_pairs={{0,96},{1,33},{32,64},{33,1},{64,32},{65,97},{96,0},{97,65},{2,98}... | collective-permute-start | bytes 1572872 | tf_op jit(solution)/shard_map/ppermute | solution.py:183
  44.4 22.8 %collective-permute-start.13 = (bf16[4,128,768]{2,1,0:T(8,128)(2,1)S(1)}, bf16[4,128,768]{2,1,0:T(8,128)(2,1)S(1)}, u32[]{:S(2)}, u32[]{:S(2)}) collective-permute-start(bf16[4,128,768]{2,1,0:T(8,128)(2,1)S(1)} %get-tuple-element.32), channel_id=1, source_target_pairs={{0,8},{8,0},{1,9},{9,1},{2,10},{10,2},{3,11},{11,3},{4,12},{12,4},... | collective-permute-start | bytes 2359304 | tf_op jit(solution)/shard_map/ppermute | solution.py:178
  46.2 12.4 %collective-permute-start.17 = (bf16[2,128,768]{2,1,0:T(8,128)(2,1)S(1)}, bf16[2,128,768]{2,1,0:T(8,128)(2,1)S(1)}, u32[]{:S(2)}, u32[]{:S(2)}) collective-permute-start(bf16[2,128,768]{2,1,0:T(8,128)(2,1)S(1)} %get-tuple-element.38), channel_id=1, source_target_pairs={{0,2},{2,4},{4,6},{6,0},{1,3},{3,5},{5,7},{7,1},{8,10},{10,12},{12... | collective-permute-start | bytes 1179656 | tf_op jit(solution)/shard_map/ppermute | solution.py:178
  46.4 20.1 %collective-permute-start.18 = (bf16[2,128,768]{2,1,0:T(8,128)(2,1)S(1)}, bf16[2,128,768]{2,1,0:T(8,128)(2,1)S(1)}, u32[]{:S(2)}, u32[]{:S(2)}) collective-permute-start(bf16[2,128,768]{2,1,0:T(8,128)(2,1)S(1)} %get-tuple-element.39), channel_id=1, source_target_pairs={{0,4},{2,6},{4,0},{6,2},{1,5},{3,7},{5,1},{7,3},{8,12},{10,14},{12... | collective-permute-start | bytes 1179656 | tf_op jit(solution)/shard_map/ppermute | solution.py:178
  50.9 15.6 %collective-permute-start.19 = (bf16[2,128,768]{2,1,0:T(8,128)(2,1)S(1)}, bf16[2,128,768]{2,1,0:T(8,128)(2,1)S(1)}, u32[]{:S(2)}, u32[]{:S(2)}) collective-permute-start(bf16[2,128,768]{2,1,0:T(8,128)(2,1)S(1)} %get-tuple-element.40), channel_id=1, source_target_pairs={{0,6},{2,0},{4,2},{6,4},{1,7},{3,1},{5,3},{7,5},{8,14},{10,8},{12,... | collective-permute-start | bytes 1179656 | tf_op jit(solution)/shard_map/ppermute | solution.py:178
  66.7 5.8 %collective-permute-start.20 = (bf16[128,768]{1,0:T(8,128)(2,1)S(1)}, bf16[128,768]{1,0:T(8,128)(2,1)S(1)}, u32[]{:S(2)}, u32[]{:S(2)}) collective-permute-start(bf16[128,768]{1,0:T(8,128)(2,1)S(1)} %get-tuple-element.42), channel_id=1, source_target_pairs={{0,8},{8,0},{1,9},{9,1},{2,10},{10,2},{3,11},{11,3},{4,12},{12,4},... | collective-permute-start | bytes 589832 | tf_op jit(solution)/shard_map/ppermute | solution.py:178
  67.3 7.1 %collective-permute-start.14 = (bf16[128,768]{1,0:T(8,128)(2,1)S(1)}, bf16[128,768]{1,0:T(8,128)(2,1)S(1)}, u32[]{:S(2)}, u32[]{:S(2)}) collective-permute-start(bf16[128,768]{1,0:T(8,128)(2,1)S(1)} %get-tuple-element.34), channel_id=1, source_target_pairs={{0,2},{2,4},{4,6},{6,0},{1,3},{3,5},{5,7},{7,1},{8,10},{10,12},{12... | collective-permute-start | bytes 589832 | tf_op jit(solution)/shard_map/ppermute | solution.py:178
  68.1 11.6 %collective-permute-start.15 = (bf16[128,768]{1,0:T(8,128)(2,1)S(1)}, bf16[128,768]{1,0:T(8,128)(2,1)S(1)}, u32[]{:S(2)}, u32[]{:S(2)}) collective-permute-start(bf16[128,768]{1,0:T(8,128)(2,1)S(1)} %get-tuple-element.35), channel_id=1, source_target_pairs={{0,4},{2,6},{4,0},{6,2},{1,5},{3,7},{5,1},{7,3},{8,12},{10,14},{12... | collective-permute-start | bytes 589832 | tf_op jit(solution)/shard_map/ppermute | solution.py:178
  71.0 8.7 %collective-permute-start.16 = (bf16[128,768]{1,0:T(8,128)(2,1)S(1)}, bf16[128,768]{1,0:T(8,128)(2,1)S(1)}, u32[]{:S(2)}, u32[]{:S(2)}) collective-permute-start(bf16[128,768]{1,0:T(8,128)(2,1)S(1)} %get-tuple-element.36), channel_id=1, source_target_pairs={{0,6},{2,0},{4,2},{6,4},{1,7},{3,1},{5,3},{7,5},{8,14},{10,8},{12,... | collective-permute-start | bytes 589832 | tf_op jit(solution)/shard_map/ppermute | solution.py:178

commit v3 on v2

--- a/solution.py
+++ b/solution.py
@@ -57,8 +57,9 @@
         copy.wait()
 
 
-def ring_masks():
+def ring_masks(flip=0):
     c = lax.axis_index("c")
+    c = 1 - c if flip else c
     return (0, 1 + 2 * c, 3 - 2 * c, 2)
 
 
@@ -81,7 +82,7 @@
         for o in range(2):
             copies[slot * 2 + o].wait()
             for b in range(2):
-                for s, mask in enumerate(ring_masks()):
+                for s, mask in enumerate(ring_masks(b)):
                     block = (zl ^ b) * 4 + (y ^ mask)
                     lanes = pl.ds(pl.multiple_of(block * 256 + c * 128, 128), 128)
                     re, im = held[slot, o, 0, :, lanes], held[slot, o, 1, :, lanes]
@@ -93,7 +94,7 @@
 
 
 def screen(w_ref, *refs):
-    pieces, (out_ref, acc, held, sems) = refs[:4], refs[4:]
+    pieces, outs, (acc, held, sems) = refs[:4], refs[4:7], refs[7:]
     copies = copy_all([(ref, held.at[i]) for i, ref in enumerate(pieces)], sems)
     for i in range(8):
         if i % 2 == 0:
@@ -106,14 +107,15 @@
                 acc[p] = term
             else:
                 acc[p] += term
-    out_ref[...] = acc[...].reshape(3, 2, 2, 128, 256).astype(BF)
-
-
-def right_side(p, mine_ref, got_ref):
+    for p, ref in enumerate(outs):
+        ref[...] = acc[p].reshape(2, 2, 128, 256).astype(BF)
+
+
+def right_side(mine_ref, got_ref):
     blocks = []
     for o in range(2):
-        re = (mine_ref[p, o, 0].astype(F32) + got_ref[p, 1 - o, 0].astype(F32)).astype(BF)
-        im = (mine_ref[p, o, 1].astype(F32) + got_ref[p, 1 - o, 1].astype(F32)).astype(BF)
+        re = (mine_ref[o, 0].astype(F32) + got_ref[1 - o, 0].astype(F32)).astype(BF)
+        im = (mine_ref[o, 1].astype(F32) + got_ref[1 - o, 1].astype(F32)).astype(BF)
         blocks += [jnp.concatenate((re, im), 1), jnp.concatenate((im, -re), 1)]
     return jnp.concatenate(blocks, 0)
 
@@ -131,8 +133,8 @@
     return jnp.where(same, own, far)
 
 
-def contract_y(factor, mine_ref, got_ref, r0, r1, r2, r3, k_ref, s1_ref, s2_ref, s3_ref, rest_ref):
-    rhs = [right_side(p, mine_ref, got_ref) for p in range(2)]
+def contract_y(factor, m0_ref, g0_ref, m1_ref, g1_ref, r0, r1, r2, r3, k_ref, s1_ref, s2_ref, s3_ref, rest_ref):
+    rhs = [right_side(m0_ref, g0_ref), right_side(m1_ref, g1_ref)]
     for b in range(2):
         for s, ref in enumerate((k_ref, s1_ref, s2_ref, s3_ref)):
             rows = rows_for(b, s, 0, (r0, r1, r2, r3))
@@ -147,7 +149,7 @@
 
 
 def contract_z(factor, mine_ref, got_ref, r0, r1, r2, r3, rest_ref, k_ref, s_ref):
-    rhs = right_side(2, mine_ref, got_ref)
+    rhs = right_side(mine_ref, got_ref)
     for b, ref in enumerate((k_ref, s_ref)):
         for s in range(4):
             part = jnp.dot(rows_for(b, s, 1, (r0, r1, r2, r3)), rhs, preferred_element_type=F32)
@@ -205,11 +207,11 @@
     m_next = ring_swap(m_near, "y", 1)
     rows_near = double(rows, rows_got)
     rows_next = ring_swap(rows_near, "x", 1)
-    m_far_got = ring_swap(m_far, "y", 0)
+    m_far_got = ring_swap(m_far, "y", 1)
     m_far_got, rows_far = tie(m_far_got, rows_far)
     rows_far_got = ring_swap(rows_far, "x", 0)
     m_far_near = double(m_far, m_far_got)
-    m_far_next = ring_swap(m_far_near, "y", 1)
+    m_far_next = ring_swap(m_far_near, "y", 0)
     rows_far_near = double(rows_far, rows_far_got)
     rows_far_next = ring_swap(rows_far_near, "x", 1)
     (weights,) = call(
@@ -224,9 +226,9 @@
         scratch=[pltpu.VMEM((2, 2, 2, 128, 2048), BF), pltpu.SemaphoreType.DMA((4,))],
     )
     weights, rows_next = tie(weights, rows_next)
-    (part,) = call(
+    parts = call(
         screen,
-        [(3, 2, 2, 128, 256)],
+        [(2, 2, 128, 256)] * 3,
         [VMEM] + [ANY] * 4,
         weights,
         m_near,
@@ -236,22 +238,25 @@
         limit=8,
         scratch=[pltpu.VMEM((3, 512, 256), F32), pltpu.VMEM((4, 2, 2, 2, 128, 256), BF), pltpu.SemaphoreType.DMA((4,))],
     )
-    left = [part, shift(part, "c", 2, 1), rows_near, rows_next, rows_far_near, rows_far_next]
+    sides = [(part, shift(part, "c", 2, 1)) for part in parts]
+    left = [rows_near, rows_next, rows_far_near, rows_far_next]
     y_keep, y1, y2, y3, rest = call(
         functools.partial(contract_y, factor),
         [(2, 128, WIDE_Y)] * 4 + [(2, 4, 128, 512 - CUT)],
-        [VMEM] * 6,
+        [VMEM] * 8,
+        *sides[0],
+        *sides[1],
         *left,
         limit=8,
     )
     z_keep, z_send = call(
-        functools.partial(contract_z, factor), [(4, 128, WIDE_Z)] * 2, [VMEM] * 7, *left, rest, limit=8
+        functools.partial(contract_z, factor), [(4, 128, WIDE_Z)] * 2, [VMEM] * 7, *sides[2], *left, rest, limit=8
     )
     z_got = shift(z_send, "zl", 2, 1)
-    y_got = [shift(y1, "y", 4, 1), shift(y2, "y", 4, 2), shift(y3, "y", 4, -1)]
+    y_got = [shift(y1, "y", 4, 1), shift(y3, "y", 4, -1), shift(y2, "y", 4, 2)]
     z_sums = call(add_z, [(128, WIDE_Z)] * 4, [VMEM] * 2, z_keep, z_got)
     y_keep, y_send = call(add_y, [(128, WIDE_Y)] * 2, [VMEM] * 4, y_keep, *y_got)
-    z_last = [shift(z_sums[1], "y", 4, 1), shift(z_sums[2], "y", 4, 2), shift(z_sums[3], "y", 4, -1)]
+    z_last = [shift(z_sums[1], "y", 4, 1), shift(z_sums[3], "y", 4, -1), shift(z_sums[2], "y", 4, 2)]
     y_last = shift(y_send, "zl", 2, 1)
     (out,) = call(finish, [(3, 128, 512)], [SMEM] + [VMEM] * 6, pairs, z_sums[0], *z_last, y_keep, y_last)
     return out.reshape(3, 128, 2, 256)

time: 82 us -> 75.2 us (0.917)
  waiting for transfers between devices: 39.7 us -> 35.1 us
  starting transfers between devices: 30.5 us -> 27.8 us
    ppermute x8, waiting for transfers between devices: 13.2 us -> 9.53 us  [ring_swap(): return lax.ppermute(x, (axis, 'c'), pairs)]
    ppermute x8, starting transfers between devices: 13.3 us -> 10.1 us  [ring_swap(): return lax.ppermute(x, (axis, 'c'), pairs)]
    ppermute x13 -> x15, waiting for transfers between devices: 26.6 us -> 25.6 us  [shift(): return lax.ppermute(x, axis, [(i, (i + step) % size) for i in range(size)])]
    ppermute x13 -> x15, starting transfers between devices: 17.2 us -> 17.7 us  [shift(): return lax.ppermute(x, axis, [(i, (i + step) % size) for i in range(size)])]
  transfers between devices with their start and end apart: 21 -> 23, of which waited for: 9 -> 10; matrix products, arithmetic and copies ran while one was open for 0% -> 0% of each run, Pallas kernels for 9% -> 12%
where the time goes in v3:
time: 75.2 us; the launch traced here: 73.9 us
  waiting for transfers between devices  35.1 us (47%)
  starting transfers between devices  27.8 us (37%)
  Pallas kernels  10 us (13%)
  local copies, waits for them, and re-layouts  0.86 us (1%)
    ppermute x15, waiting for transfers between devices, shift(): return lax.ppermute(x, axis, [(i, (i + step) % size) for i in range(size)])  25.6 us
    ppermute x15, starting transfers between devices, shift(): return lax.ppermute(x, axis, [(i, (i + step) % size) for i in range(size)])  17.7 us
    ppermute x8, starting transfers between devices, ring_swap(): return lax.ppermute(x, (axis, 'c'), pairs)  10.1 us
    pallas_call x13, Pallas kernels, call(): pl.pallas_call(body, out_shape=[jax.ShapeDtypeStruct(s, BF) for s in outs...  10 us
    ppermute x8, waiting for transfers between devices, ring_swap(): return lax.ppermute(x, (axis, 'c'), pairs)  9.53 us
  transfers between devices with their start and end apart: 23, of which 10 were waited for; matrix products, arithmetic and copies ran while one was open for 0% of the time, Pallas kernels for 12%

profile of v3, /device:TPU:6, one launch (start us, length us, event | category | flops | bytes accessed | tf_op | source)
XLA Modules:
  0.0 73.9 jit_solution(4588247026424986086)
XLA Ops:
  0.0 1.9 %collective-permute-start.6 = (bf16[2,2,128,256]{3,2,1,0:T(8,128)(2,1)}, bf16[2,2,128,256]{3,2,1,0:T(8,128)(2,1)S(1)}, u32[]{:S(2)}, u32[]{:S(2)}) collective-permute-start(bf16[2,2,128,256]{3,2,1,0:T(8,128)(2,1)} %a_ref.1), channel_id=1, source_target_pairs={{0,8},{8,0},{1,9},{9,1},{2,10},{10,2},{3,11},{11,3},{4,12},{12,4},... | collective-permute-start | bytes 786440 | tf_op jit(solution)/shard_map/ppermute | solution.py:180
  1.9 1.1 %shard_map.47 = (bf16[2,128,256]{2,1,0:T(8,128)(2,1)S(1)}, bf16[2,128,256]{2,1,0:T(8,128)(2,1)S(1)}) custom-call(bf16[2,2,128,256]{3,2,1,0:T(8,128)(2,1)} %a_ref.1), custom_call_target="tpu_custom_call" | custom-call | tf_op jit(solution)/shard_map/pallas_call | solution.py:24
  3.3 1.6 %collective-permute-start.4 = (bf16[2,2,128,256]{3,2,1,0:T(8,128)(2,1)}, bf16[2,2,128,256]{3,2,1,0:T(8,128)(2,1)S(1)}, u32[]{:S(2)}, u32[]{:S(2)}) collective-permute-start(bf16[2,2,128,256]{3,2,1,0:T(8,128)(2,1)} %a_ref.1), channel_id=1, source_target_pairs={{0,2},{1,7},{2,0},{3,5},{4,6},{5,3},{6,4},{7,1},{8,10},{9,15},{10,... | collective-permute-start | bytes 786440 | tf_op jit(solution)/shard_map/ppermute | solution.py:185
  5.9 3.6 %collective-permute-start.8 = (bf16[2,128,512]{2,1,0:T(8,128)(2,1)S(1)}, bf16[2,128,512]{2,1,0:T(8,128)(2,1)S(1)}, u32[]{:S(2)}, u32[]{:S(2)}) collective-permute-start(bf16[2,128,512]{2,1,0:T(8,128)(2,1)S(1)} %shard_map.48.a_ref), channel_id=1, source_target_pairs={{0,16},{16,0},{1,17},{17,1},{2,18},{18,2},{3,19},{19,3},{4,20},{20... | collective-permute-start | bytes 786440 | tf_op jit(solution)/shard_map/ppermute | solution.py:180
  9.5 2.7 %collective-permute-start.7 = (bf16[2,2,128,256]{3,2,1,0:T(8,128)(2,1)S(1)}, bf16[2,2,128,256]{3,2,1,0:T(8,128)(2,1)S(1)}, u32[]{:S(2)}, u32[]{:S(2)}) collective-permute-start(bf16[2,2,128,256]{3,2,1,0:T(8,128)(2,1)S(1)} %collective-permute-done.6.a_ref), channel_id=1, source_target_pairs={{0,6},{1,3},{2,4},{3,1},{4,2},{5,7},{6,0},{7,5},{8,14},{9,11},{10,... | collective-permute-start | bytes 786440 | tf_op jit(solution)/shard_map/ppermute | solution.py:185
  12.2 1.0 %shard_map.50.refs_0_ = bf16[2,2,2,128,256]{4,3,2,1,0:T(8,128)(2,1)S(1)} custom-call(bf16[2,2,128,256]{3,2,1,0:T(8,128)(2,1)} %a_ref.1, bf16[2,2,128,256]{3,2,1,0:T(8,128)(2,1)S(1)} %collective-permute-done.4.b_ref), custom_call_target="tpu_custom_call" | custom-call | tf_op jit(solution)/shard_map/pallas_call | solution.py:24
  14.1 1.0 %collective-permute-start.3 = (bf16[2,2,128,512]{3,2,1,0:T(8,128)(2,1)S(1)}, bf16[2,2,128,512]{3,2,1,0:T(8,128)(2,1)S(1)}, u32[]{:S(2)}, u32[]{:S(2)}) collective-permute-start(bf16[2,2,128,512]{3,2,1,0:T(8,128)(2,1)S(1)} %shard_map.49.r0), channel_id=1, source_target_pairs={{0,96},{1,33},{32,64},{33,1},{64,32},{65,97},{96,0},{97,65},{2,98}... | collective-permute-start | bytes 1572872 | tf_op jit(solution)/shard_map/ppermute | solution.py:185
  15.1 3.0 %collective-permute-done.8.a_ref = bf16[2,128,512]{2,1,0:T(8,128)(2,1)S(1)} collective-permute-done((bf16[2,128,512]{2,1,0:T(8,128)(2,1)S(1)}, bf16[2,128,512]{2,1,0:T(8,128)(2,1)S(1)}, u32[]{:S(2)}, u32[]{:S(2)}) %collective-permute-start.8) | collective-permute-done | bytes 262176 | tf_op jit(solution)/shard_map/ppermute | solution.py:180
  18.1 1.7 %collective-permute-start.9 = (bf16[2,2,2,128,256]{4,3,2,1,0:T(8,128)(2,1)S(1)}, bf16[2,2,2,128,256]{4,3,2,1,0:T(8,128)(2,1)S(1)}, u32[]{:S(2)}, u32[]{:S(2)}) collective-permute-start(bf16[2,2,2,128,256]{4,3,2,1,0:T(8,128)(2,1)S(1)} %shard_map.51.refs_2_), channel_id=1, source_target_pairs={{0,2},{1,7},{2,0},{3,5},{4,6},{5,3},{6,4},{7,1},{8,10},{9,15},{10,... | collective-permute-start | bytes 1572872 | tf_op jit(solution)/shard_map/ppermute | solution.py:185
  20.6 5.5 %collective-permute-done.11.b_ref = bf16[2,128,512]{2,1,0:T(8,128)(2,1)S(1)} collective-permute-done((bf16[2,128,512]{2,1,0:T(8,128)(2,1)S(1)}, bf16[2,128,512]{2,1,0:T(8,128)(2,1)S(1)}, u32[]{:S(2)}, u32[]{:S(2)}) %collective-permute-start.11) | collective-permute-done | bytes 262176 | tf_op jit(solution)/shard_map/ppermute | solution.py:185
  26.8 1.6 %shard_map.46.w_ref = bf16[2,512,2048]{2,1,0:T(8,128)(2,1)S(1)} custom-call(s32[2,3]{1,0:T(2,128)S(1)} %bitcast.1, s32[3]{0:T(128)S(1)} %copy-done.2, bf16[2,2,128,2048]{3,2,1,0:T(8,128)(2,1)S(1)} %copy-done, bf16[2,2,128,2048]{3,2,1,0:T(8,128)(2,1)S(1)} %collective-permute-done.mate_ref), custom_call_target="tpu_custom_call" | custom-call | tf_op jit(solution)/shard_map/pallas_call | solution.py:24
  28.4 3.0 %shard_map.52 = (bf16[2,2,128,256]{3,2,1,0:T(8,128)(2,1)S(1)}, bf16[2,2,128,256]{3,2,1,0:T(8,128)(2,1)S(1)}, bf16[2,2,128,256]{3,2,1,0:T(8,128)(2,1)S(1)}) custom-call(bf16[2,512,2048]{2,1,0:T(8,128)(2,1)S(1)} %shard_map.46.w_ref, bf16[2,2,2,128,256]{4,3,2,1,0:T(8,128)(2,1)S(1)} %shard_map.50.refs_0_, ...), custom_call_target="tpu_custom_call" | custom-call | tf_op jit(solution)/shard_map/pallas_call | solution.py:24
  32.7 4.0 %collective-permute-done.12.r3 = bf16[2,2,128,512]{3,2,1,0:T(8,128)(2,1)S(1)} collective-permute-done((bf16[2,2,128,512]{3,2,1,0:T(8,128)(2,1)S(1)}, bf16[2,2,128,512]{3,2,1,0:T(8,128)(2,1)S(1)}, u32[]{:S(2)}, u32[]{:S(2)}) %collective-permute-start.12) | collective-permute-done | bytes 524320 | tf_op jit(solution)/shard_map/ppermute | solution.py:185
  36.7 1.3 %shard_map.54 = (bf16[2,128,768]{2,1,0:T(8,128)(2,1)S(1)}, bf16[2,128,768]{2,1,0:T(8,128)(2,1)S(1)}, bf16[2,128,768]{2,1,0:T(8,128)(2,1)S(1)}, bf16[2,128,768]{2...) custom-call(bf16[2,2,128,256]{3,2,1,0:T(8,128)(2,1)S(1)} %get-tuple-element.34.m0_ref, ...), custom_call_target="tpu_custom_call" | custom-call | tf_op jit(solution)/shard_map/pallas_call | solution.py:24
  39.7 2.5 %collective-permute-start.20 = (bf16[2,128,768]{2,1,0:T(8,128)(2,1)S(1)}, bf16[2,128,768]{2,1,0:T(8,128)(2,1)S(1)}, u32[]{:S(2)}, u32[]{:S(2)}) collective-permute-start(bf16[2,128,768]{2,1,0:T(8,128)(2,1)S(1)} %get-tuple-element.45), channel_id=1, source_target_pairs={{0,6},{2,0},{4,2},{6,4},{1,7},{3,1},{5,3},{7,5},{8,14},{10,8},{12,... | collective-permute-start | bytes 1179656 | tf_op jit(solution)/shard_map/ppermute | solution.py:180
  42.1 2.0 %collective-permute-start.21 = (bf16[2,128,768]{2,1,0:T(8,128)(2,1)S(1)}, bf16[2,128,768]{2,1,0:T(8,128)(2,1)S(1)}, u32[]{:S(2)}, u32[]{:S(2)}) collective-permute-start(bf16[2,128,768]{2,1,0:T(8,128)(2,1)S(1)} %get-tuple-element.46), channel_id=1, source_target_pairs={{0,4},{2,6},{4,0},{6,2},{1,5},{3,7},{5,1},{7,3},{8,12},{10,14},{12... | collective-permute-start | bytes 1179656 | tf_op jit(solution)/shard_map/ppermute | solution.py:180
  44.2 8.0 %collective-permute-done.19.g1_ref = bf16[2,128,768]{2,1,0:T(8,128)(2,1)S(1)} collective-permute-done((bf16[2,128,768]{2,1,0:T(8,128)(2,1)S(1)}, bf16[2,128,768]{2,1,0:T(8,128)(2,1)S(1)}, u32[]{:S(2)}, u32[]{:S(2)}) %collective-permute-start.19) | collective-permute-done | bytes 393248 | tf_op jit(solution)/shard_map/ppermute | solution.py:180
  52.2 6.4 %collective-permute-done.20.g2_ref = bf16[2,128,768]{2,1,0:T(8,128)(2,1)S(1)} collective-permute-done((bf16[2,128,768]{2,1,0:T(8,128)(2,1)S(1)}, bf16[2,128,768]{2,1,0:T(8,128)(2,1)S(1)}, u32[]{:S(2)}, u32[]{:S(2)}) %collective-permute-start.20) | collective-permute-done | bytes 393248 | tf_op jit(solution)/shard_map/ppermute | solution.py:180
  58.6 0.9 %collective-permute-done.21.g3_ref = bf16[2,128,768]{2,1,0:T(8,128)(2,1)S(1)} collective-permute-done((bf16[2,128,768]{2,1,0:T(8,128)(2,1)S(1)}, bf16[2,128,768]{2,1,0:T(8,128)(2,1)S(1)}, u32[]{:S(2)}, u32[]{:S(2)}) %collective-permute-start.21) | collective-permute-done | bytes 393248 | tf_op jit(solution)/shard_map/ppermute | solution.py:180
  59.7 1.5 %collective-permute-start.22 = (bf16[128,768]{1,0:T(8,128)(2,1)S(1)}, bf16[128,768]{1,0:T(8,128)(2,1)S(1)}, u32[]{:S(2)}, u32[]{:S(2)}) collective-permute-start(bf16[128,768]{1,0:T(8,128)(2,1)S(1)} %get-tuple-element.48), channel_id=1, source_target_pairs={{0,8},{8,0},{1,9},{9,1},{2,10},{10,2},{3,11},{11,3},{4,12},{12,4},... | collective-permute-start | bytes 589832 | tf_op jit(solution)/shard_map/ppermute | solution.py:180
  61.4 1.2 %collective-permute-start.16 = (bf16[128,768]{1,0:T(8,128)(2,1)S(1)}, bf16[128,768]{1,0:T(8,128)(2,1)S(1)}, u32[]{:S(2)}, u32[]{:S(2)}) collective-permute-start(bf16[128,768]{1,0:T(8,128)(2,1)S(1)} %get-tuple-element.40), channel_id=1, source_target_pairs={{0,2},{2,4},{4,6},{6,0},{1,3},{3,5},{5,7},{7,1},{8,10},{10,12},{12... | collective-permute-start | bytes 589832 | tf_op jit(solution)/shard_map/ppermute | solution.py:180
  62.6 2.1 %collective-permute-start.17 = (bf16[128,768]{1,0:T(8,128)(2,1)S(1)}, bf16[128,768]{1,0:T(8,128)(2,1)S(1)}, u32[]{:S(2)}, u32[]{:S(2)}) collective-permute-start(bf16[128,768]{1,0:T(8,128)(2,1)S(1)} %get-tuple-element.41), channel_id=1, source_target_pairs={{0,6},{2,0},{4,2},{6,4},{1,7},{3,1},{5,3},{7,5},{8,14},{10,8},{12,... | collective-permute-start | bytes 589832 | tf_op jit(solution)/shard_map/ppermute | solution.py:180
  65.5 4.8 %collective-permute-done.16.z1_ref = bf16[128,768]{1,0:T(8,128)(2,1)S(1)} collective-permute-done((bf16[128,768]{1,0:T(8,128)(2,1)S(1)}, bf16[128,768]{1,0:T(8,128)(2,1)S(1)}, u32[]{:S(2)}, u32[]{:S(2)}) %collective-permute-start.16) | collective-permute-done | bytes 196640 | tf_op jit(solution)/shard_map/ppermute | solution.py:180
  70.8 1.6 %collective-permute-done.18.z3_ref = bf16[128,768]{1,0:T(8,128)(2,1)S(1)} collective-permute-done((bf16[128,768]{1,0:T(8,128)(2,1)S(1)}, bf16[128,768]{1,0:T(8,128)(2,1)S(1)}, u32[]{:S(2)}, u32[]{:S(2)}) %collective-permute-start.18) | collective-permute-done | bytes 196640 | tf_op jit(solution)/shard_map/ppermute | solution.py:180
  (42 shorter events, 9.8 us)
Async XLA Ops:
  0.0 26.7 %collective-permute-start = (bf16[2,2,128,2048]{3,2,1,0:T(8,128)(2,1)}, bf16[2,2,128,2048]{3,2,1,0:T(8,128)(2,1)S(1)}, u32[]{:S(2)}, u32[]{:S(2)}) collective-permute-start(bf16[2,2,128,2048]{3,2,1,0:T(8,128)(2,1)} %own_ref.1), channel_id=1, source_target_pairs={{0,1},{1,0},{2,3},{3,2},{4,5},{5,4},{6,7},{7,6},{8,9},{9,8},{10,11... | collective-permute-start | bytes 6291464 | tf_op jit(solution)/shard_map/ppermute | solution.py:180
  0.0 9.5 %collective-permute-start.6 = (bf16[2,2,128,256]{3,2,1,0:T(8,128)(2,1)}, bf16[2,2,128,256]{3,2,1,0:T(8,128)(2,1)S(1)}, u32[]{:S(2)}, u32[]{:S(2)}) collective-permute-start(bf16[2,2,128,256]{3,2,1,0:T(8,128)(2,1)} %a_ref.1), channel_id=1, source_target_pairs={{0,8},{8,0},{1,9},{9,1},{2,10},{10,2},{3,11},{11,3},{4,12},{12,4},... | collective-permute-start | bytes 786440 | tf_op jit(solution)/shard_map/ppermute | solution.py:180
  3.0 1.9 %collective-permute-start.1 = (bf16[2,128,256]{2,1,0:T(8,128)(2,1)S(1)}, bf16[2,128,256]{2,1,0:T(8,128)(2,1)S(1)}, u32[]{:S(2)}, u32[]{:S(2)}) collective-permute-start(bf16[2,128,256]{2,1,0:T(8,128)(2,1)S(1)} %get-tuple-element.28), channel_id=1, source_target_pairs={{0,1},{1,0},{2,3},{3,2},{4,5},{5,4},{6,7},{7,6},{8,9},{9,8},{10,11... | collective-permute-start | bytes 393224 | tf_op jit(solution)/shard_map/ppermute | solution.py:180
  3.3 8.9 %collective-permute-start.4 = (bf16[2,2,128,256]{3,2,1,0:T(8,128)(2,1)}, bf16[2,2,128,256]{3,2,1,0:T(8,128)(2,1)S(1)}, u32[]{:S(2)}, u32[]{:S(2)}) collective-permute-start(bf16[2,2,128,256]{3,2,1,0:T(8,128)(2,1)} %a_ref.1), channel_id=1, source_target_pairs={{0,2},{1,7},{2,0},{3,5},{4,6},{5,3},{6,4},{7,1},{8,10},{9,15},{10,... | collective-permute-start | bytes 786440 | tf_op jit(solution)/shard_map/ppermute | solution.py:185
  4.9 21.8 %copy-start = (bf16[2,2,128,2048]{3,2,1,0:T(8,128)(2,1)S(1)}, bf16[2,2,128,2048]{3,2,1,0:T(8,128)(2,1)}, u32[]{:S(2)}) copy-start(bf16[2,2,128,2048]{3,2,1,0:T(8,128)(2,1)} %own_ref.1) | copy-start | bytes 6291460
  5.0 9.0 %collective-permute-start.2 = (bf16[2,128,512]{2,1,0:T(8,128)(2,1)S(1)}, bf16[2,128,512]{2,1,0:T(8,128)(2,1)S(1)}, u32[]{:S(2)}, u32[]{:S(2)}) collective-permute-start(bf16[2,128,512]{2,1,0:T(8,128)(2,1)S(1)} %shard_map.48.a_ref), channel_id=1, source_target_pairs={{0,32},{1,97},{32,0},{33,65},{64,96},{65,33},{96,64},{97,1},{2,34}... | collective-permute-start | bytes 786440 | tf_op jit(solution)/shard_map/ppermute | solution.py:185
  5.9 12.1 %collective-permute-start.8 = (bf16[2,128,512]{2,1,0:T(8,128)(2,1)S(1)}, bf16[2,128,512]{2,1,0:T(8,128)(2,1)S(1)}, u32[]{:S(2)}, u32[]{:S(2)}) collective-permute-start(bf16[2,128,512]{2,1,0:T(8,128)(2,1)S(1)} %shard_map.48.a_ref), channel_id=1, source_target_pairs={{0,16},{16,0},{1,17},{17,1},{2,18},{18,2},{3,19},{19,3},{4,20},{20... | collective-permute-start | bytes 786440 | tf_op jit(solution)/shard_map/ppermute | solution.py:180
  9.5 8.6 %collective-permute-start.7 = (bf16[2,2,128,256]{3,2,1,0:T(8,128)(2,1)S(1)}, bf16[2,2,128,256]{3,2,1,0:T(8,128)(2,1)S(1)}, u32[]{:S(2)}, u32[]{:S(2)}) collective-permute-start(bf16[2,2,128,256]{3,2,1,0:T(8,128)(2,1)S(1)} %collective-permute-done.6.a_ref), channel_id=1, source_target_pairs={{0,6},{1,3},{2,4},{3,1},{4,2},{5,7},{6,0},{7,5},{8,14},{9,11},{10,... | collective-permute-start | bytes 786440 | tf_op jit(solution)/shard_map/ppermute | solution.py:185
  13.2 15.2 %collective-permute-start.5 = (bf16[2,2,2,128,256]{4,3,2,1,0:T(8,128)(2,1)S(1)}, bf16[2,2,2,128,256]{4,3,2,1,0:T(8,128)(2,1)S(1)}, u32[]{:S(2)}, u32[]{:S(2)}) collective-permute-start(bf16[2,2,2,128,256]{4,3,2,1,0:T(8,128)(2,1)S(1)} %shard_map.50.refs_0_), channel_id=1, source_target_pairs={{0,6},{1,3},{2,4},{3,1},{4,2},{5,7},{6,0},{7,5},{8,14},{9,11},{10,... | collective-permute-start | bytes 1572872 | tf_op jit(solution)/shard_map/ppermute | solution.py:185
  14.1 14.4 %collective-permute-start.3 = (bf16[2,2,128,512]{3,2,1,0:T(8,128)(2,1)S(1)}, bf16[2,2,128,512]{3,2,1,0:T(8,128)(2,1)S(1)}, u32[]{:S(2)}, u32[]{:S(2)}) collective-permute-start(bf16[2,2,128,512]{3,2,1,0:T(8,128)(2,1)S(1)} %shard_map.49.r0), channel_id=1, source_target_pairs={{0,96},{1,33},{32,64},{33,1},{64,32},{65,97},{96,0},{97,65},{2,98}... | collective-permute-start | bytes 1572872 | tf_op jit(solution)/shard_map/ppermute | solution.py:185
  18.1 10.3 %collective-permute-start.9 = (bf16[2,2,2,128,256]{4,3,2,1,0:T(8,128)(2,1)S(1)}, bf16[2,2,2,128,256]{4,3,2,1,0:T(8,128)(2,1)S(1)}, u32[]{:S(2)}, u32[]{:S(2)}) collective-permute-start(bf16[2,2,2,128,256]{4,3,2,1,0:T(8,128)(2,1)S(1)} %shard_map.51.refs_2_), channel_id=1, source_target_pairs={{0,2},{1,7},{2,0},{3,5},{4,6},{5,3},{6,4},{7,1},{8,10},{9,15},{10,... | collective-permute-start | bytes 1572872 | tf_op jit(solution)/shard_map/ppermute | solution.py:185
  19.8 6.4 %collective-permute-start.11 = (bf16[2,128,512]{2,1,0:T(8,128)(2,1)S(1)}, bf16[2,128,512]{2,1,0:T(8,128)(2,1)S(1)}, u32[]{:S(2)}, u32[]{:S(2)}) collective-permute-start(bf16[2,128,512]{2,1,0:T(8,128)(2,1)S(1)} %collective-permute-done.8.a_ref), channel_id=1, source_target_pairs={{0,32},{1,97},{32,0},{33,65},{64,96},{65,33},{96,64},{97,1},{2,34}... | collective-permute-start | bytes 786440 | tf_op jit(solution)/shard_map/ppermute | solution.py:185
  26.2 10.5 %collective-permute-start.12 = (bf16[2,2,128,512]{3,2,1,0:T(8,128)(2,1)S(1)}, bf16[2,2,128,512]{3,2,1,0:T(8,128)(2,1)S(1)}, u32[]{:S(2)}, u32[]{:S(2)}) collective-permute-start(bf16[2,2,128,512]{3,2,1,0:T(8,128)(2,1)S(1)} %shard_map.53.r2), channel_id=1, source_target_pairs={{0,96},{1,33},{32,64},{33,1},{64,32},{65,97},{96,0},{97,65},{2,98}... | collective-permute-start | bytes 1572872 | tf_op jit(solution)/shard_map/ppermute | solution.py:185
  31.4 5.2 %collective-permute-start.13 = (bf16[2,2,128,256]{3,2,1,0:T(8,128)(2,1)S(1)}, bf16[2,2,128,256]{3,2,1,0:T(8,128)(2,1)S(1)}, u32[]{:S(2)}, u32[]{:S(2)}) collective-permute-start(bf16[2,2,128,256]{3,2,1,0:T(8,128)(2,1)S(1)} %get-tuple-element.34.m0_ref), channel_id=1, source_target_pairs={{0,1},{1,0},{2,3},{3,2},{4,5},{5,4},{6,7},{7,6},{8,9},{9,8},{10,11... | collective-permute-start | bytes 786440 | tf_op jit(solution)/shard_map/ppermute | solution.py:180
  32.2 4.5 %collective-permute-start.14 = (bf16[2,2,128,256]{3,2,1,0:T(8,128)(2,1)S(1)}, bf16[2,2,128,256]{3,2,1,0:T(8,128)(2,1)S(1)}, u32[]{:S(2)}, u32[]{:S(2)}) collective-permute-start(bf16[2,2,128,256]{3,2,1,0:T(8,128)(2,1)S(1)} %get-tuple-element.35.m1_ref), channel_id=1, source_target_pairs={{0,1},{1,0},{2,3},{3,2},{4,5},{5,4},{6,7},{7,6},{8,9},{9,8},{10,11... | collective-permute-start | bytes 786440 | tf_op jit(solution)/shard_map/ppermute | solution.py:180
  32.3 5.7 %collective-permute-start.10 = (bf16[2,2,128,256]{3,2,1,0:T(8,128)(2,1)S(1)}, bf16[2,2,128,256]{3,2,1,0:T(8,128)(2,1)S(1)}, u32[]{:S(2)}, u32[]{:S(2)}) collective-permute-start(bf16[2,2,128,256]{3,2,1,0:T(8,128)(2,1)S(1)} %get-tuple-element.31.mine_ref), channel_id=1, source_target_pairs={{0,1},{1,0},{2,3},{3,2},{4,5},{5,4},{6,7},{7,6},{8,9},{9,8},{10,11... | collective-permute-start | bytes 786440 | tf_op jit(solution)/shard_map/ppermute | solution.py:180
  38.7 22.5 %collective-permute-start.15 = (bf16[4,128,768]{2,1,0:T(8,128)(2,1)S(1)}, bf16[4,128,768]{2,1,0:T(8,128)(2,1)S(1)}, u32[]{:S(2)}, u32[]{:S(2)}) collective-permute-start(bf16[4,128,768]{2,1,0:T(8,128)(2,1)S(1)} %get-tuple-element.38), channel_id=1, source_target_pairs={{0,8},{8,0},{1,9},{9,1},{2,10},{10,2},{3,11},{11,3},{4,12},{12,4},... | collective-permute-start | bytes 2359304 | tf_op jit(solution)/shard_map/ppermute | solution.py:180
  38.8 13.3 %collective-permute-start.19 = (bf16[2,128,768]{2,1,0:T(8,128)(2,1)S(1)}, bf16[2,128,768]{2,1,0:T(8,128)(2,1)S(1)}, u32[]{:S(2)}, u32[]{:S(2)}) collective-permute-start(bf16[2,128,768]{2,1,0:T(8,128)(2,1)S(1)} %get-tuple-element.44), channel_id=1, source_target_pairs={{0,2},{2,4},{4,6},{6,0},{1,3},{3,5},{5,7},{7,1},{8,10},{10,12},{12... | collective-permute-start | bytes 1179656 | tf_op jit(solution)/shard_map/ppermute | solution.py:180
  39.7 18.9 %collective-permute-start.20 = (bf16[2,128,768]{2,1,0:T(8,128)(2,1)S(1)}, bf16[2,128,768]{2,1,0:T(8,128)(2,1)S(1)}, u32[]{:S(2)}, u32[]{:S(2)}) collective-permute-start(bf16[2,128,768]{2,1,0:T(8,128)(2,1)S(1)} %get-tuple-element.45), channel_id=1, source_target_pairs={{0,6},{2,0},{4,2},{6,4},{1,7},{3,1},{5,3},{7,5},{8,14},{10,8},{12,... | collective-permute-start | bytes 1179656 | tf_op jit(solution)/shard_map/ppermute | solution.py:180
  42.1 17.4 %collective-permute-start.21 = (bf16[2,128,768]{2,1,0:T(8,128)(2,1)S(1)}, bf16[2,128,768]{2,1,0:T(8,128)(2,1)S(1)}, u32[]{:S(2)}, u32[]{:S(2)}) collective-permute-start(bf16[2,128,768]{2,1,0:T(8,128)(2,1)S(1)} %get-tuple-element.46), channel_id=1, source_target_pairs={{0,4},{2,6},{4,0},{6,2},{1,5},{3,7},{5,1},{7,3},{8,12},{10,14},{12... | collective-permute-start | bytes 1179656 | tf_op jit(solution)/shard_map/ppermute | solution.py:180
  59.7 5.8 %collective-permute-start.22 = (bf16[128,768]{1,0:T(8,128)(2,1)S(1)}, bf16[128,768]{1,0:T(8,128)(2,1)S(1)}, u32[]{:S(2)}, u32[]{:S(2)}) collective-permute-start(bf16[128,768]{1,0:T(8,128)(2,1)S(1)} %get-tuple-element.48), channel_id=1, source_target_pairs={{0,8},{8,0},{1,9},{9,1},{2,10},{10,2},{3,11},{11,3},{4,12},{12,4},... | collective-permute-start | bytes 589832 | tf_op jit(solution)/shard_map/ppermute | solution.py:180
  61.4 8.9 %collective-permute-start.16 = (bf16[128,768]{1,0:T(8,128)(2,1)S(1)}, bf16[128,768]{1,0:T(8,128)(2,1)S(1)}, u32[]{:S(2)}, u32[]{:S(2)}) collective-permute-start(bf16[128,768]{1,0:T(8,128)(2,1)S(1)} %get-tuple-element.40), channel_id=1, source_target_pairs={{0,2},{2,4},{4,6},{6,0},{1,3},{3,5},{5,7},{7,1},{8,10},{10,12},{12... | collective-permute-start | bytes 589832 | tf_op jit(solution)/shard_map/ppermute | solution.py:180
  62.6 8.2 %collective-permute-start.17 = (bf16[128,768]{1,0:T(8,128)(2,1)S(1)}, bf16[128,768]{1,0:T(8,128)(2,1)S(1)}, u32[]{:S(2)}, u32[]{:S(2)}) collective-permute-start(bf16[128,768]{1,0:T(8,128)(2,1)S(1)} %get-tuple-element.41), channel_id=1, source_target_pairs={{0,6},{2,0},{4,2},{6,4},{1,7},{3,1},{5,3},{7,5},{8,14},{10,8},{12,... | collective-permute-start | bytes 589832 | tf_op jit(solution)/shard_map/ppermute | solution.py:180
  64.7 7.7 %collective-permute-start.18 = (bf16[128,768]{1,0:T(8,128)(2,1)S(1)}, bf16[128,768]{1,0:T(8,128)(2,1)S(1)}, u32[]{:S(2)}, u32[]{:S(2)}) collective-permute-start(bf16[128,768]{1,0:T(8,128)(2,1)S(1)} %get-tuple-element.42), channel_id=1, source_target_pairs={{0,4},{2,6},{4,0},{6,2},{1,5},{3,7},{5,1},{7,3},{8,12},{10,14},{12... | collective-permute-start | bytes 589832 | tf_op jit(solution)/shard_map/ppermute | solution.py:180
  (2 other events, 43.6 us)

commit v4 on v3

--- a/solution.py
+++ b/solution.py
@@ -124,9 +124,10 @@
     x, zh, zl, y, c = (lax.axis_index(a) for a in ("x", "zh", "zl", "y", "c"))
     j = (zl ^ b) * 4 + lax.rem(y + s, 4)
     mask = (j // 2) ^ x
-    near = (mask == 0) | (mask == 1 + 2 * c)
-    unit = jnp.where((mask == 0) | (mask == 3 - 2 * c), 0, 1)
     same = lax.rem(j, 2) == zh
+    first = jnp.where(same, 1 + 2 * c, 3 - 2 * c)
+    near = (mask == 0) | (mask == first)
+    unit = jnp.where((mask == 0) | (mask == 4 - first), 0, 1)
     values = [ref[unit, k] for ref in pieces]
     own = jnp.where(near, values[0], values[1])
     far = jnp.where(near, values[2], values[3])
@@ -162,7 +163,7 @@
         ref[...] = (keep_ref[s].astype(F32) + got_ref[s].astype(F32)).astype(BF)
 
 
-def add_y(keep_ref, g1_ref, g2_ref, g3_ref, out_ref, send_ref):
+def add_y(keep_ref, g1_ref, g2_ref, g3_ref, after_ref, out_ref, send_ref):
     for b, ref in enumerate((out_ref, send_ref)):
         near = keep_ref[b].astype(F32) + g1_ref[b].astype(F32)
         ref[...] = (near + (g2_ref[b].astype(F32) + g3_ref[b].astype(F32))).astype(BF)
@@ -209,11 +210,11 @@
     rows_next = ring_swap(rows_near, "x", 1)
     m_far_got = ring_swap(m_far, "y", 1)
     m_far_got, rows_far = tie(m_far_got, rows_far)
-    rows_far_got = ring_swap(rows_far, "x", 0)
+    rows_far_got = ring_swap(rows_far, "x", 1)
     m_far_near = double(m_far, m_far_got)
     m_far_next = ring_swap(m_far_near, "y", 0)
     rows_far_near = double(rows_far, rows_far_got)
-    rows_far_next = ring_swap(rows_far_near, "x", 1)
+    rows_far_next = ring_swap(rows_far_near, "x", 0)
     (weights,) = call(
         weight_rows,
         [(2, 512, 2048)],
@@ -255,7 +256,7 @@
     z_got = shift(z_send, "zl", 2, 1)
     y_got = [shift(y1, "y", 4, 1), shift(y3, "y", 4, -1), shift(y2, "y", 4, 2)]
     z_sums = call(add_z, [(128, WIDE_Z)] * 4, [VMEM] * 2, z_keep, z_got)
-    y_keep, y_send = call(add_y, [(128, WIDE_Y)] * 2, [VMEM] * 4, y_keep, *y_got)
+    y_keep, y_send = call(add_y, [(128, WIDE_Y)] * 2, [VMEM] * 4 + [ANY], y_keep, *y_got, z_sums[0])
     z_last = [shift(z_sums[1], "y", 4, 1), shift(z_sums[3], "y", 4, -1), shift(z_sums[2], "y", 4, 2)]
     y_last = shift(y_send, "zl", 2, 1)
     (out,) = call(finish, [(3, 128, 512)], [SMEM] + [VMEM] * 6, pairs, z_sums[0], *z_last, y_keep, y_last)

time: 75.2 us -> 74.4 us (0.989)
  the two profiles are of different devices: /device:TPU:6 before, /device:TPU:68 now
where the time goes in v4:
time: 74.4 us; the launch traced here: 74.2 us
  waiting for transfers between devices  39.9 us (54%)
  starting transfers between devices  23.3 us (31%)
  Pallas kernels  10 us (13%)
  local copies, waits for them, and re-layouts  0.86 us (1%)
    ppermute x15, waiting for transfers between devices, shift(): return lax.ppermute(x, axis, [(i, (i + step) % size) for i in range(size)])  29.5 us
    ppermute x15, starting transfers between devices, shift(): return lax.ppermute(x, axis, [(i, (i + step) % size) for i in range(size)])  13 us
    ppermute x8, waiting for transfers between devices, ring_swap(): return lax.ppermute(x, (axis, 'c'), pairs)  10.4 us
    ppermute x8, starting transfers between devices, ring_swap(): return lax.ppermute(x, (axis, 'c'), pairs)  10.3 us
    pallas_call x13, Pallas kernels, call(): pl.pallas_call(body, out_shape=[jax.ShapeDtypeStruct(s, BF) for s in outs...  10 us
  transfers between devices with their start and end apart: 23, of which 12 were waited for; matrix products, arithmetic and copies ran while one was open for 0% of the time, Pallas kernels for 11%

profile of v4, /device:TPU:68, one launch (start us, length us, event | category | flops | bytes accessed | tf_op | source)
XLA Modules:
  0.0 74.2 jit_solution(16957729986021998557)
XLA Ops:
  0.0 1.6 %collective-permute-start.6 = (bf16[2,2,128,256]{3,2,1,0:T(8,128)(2,1)}, bf16[2,2,128,256]{3,2,1,0:T(8,128)(2,1)S(1)}, u32[]{:S(2)}, u32[]{:S(2)}) collective-permute-start(bf16[2,2,128,256]{3,2,1,0:T(8,128)(2,1)} %a_ref.1), channel_id=1, source_target_pairs={{0,8},{8,0},{1,9},{9,1},{2,10},{10,2},{3,11},{11,3},{4,12},{12,4},... | collective-permute-start | bytes 786440 | tf_op jit(solution)/shard_map/ppermute | solution.py:181
  1.6 1.1 %shard_map.47 = (bf16[2,128,256]{2,1,0:T(8,128)(2,1)S(1)}, bf16[2,128,256]{2,1,0:T(8,128)(2,1)S(1)}) custom-call(bf16[2,2,128,256]{3,2,1,0:T(8,128)(2,1)} %a_ref.1), custom_call_target="tpu_custom_call" | custom-call | tf_op jit(solution)/shard_map/pallas_call | solution.py:24
  3.0 1.6 %collective-permute-start.4 = (bf16[2,2,128,256]{3,2,1,0:T(8,128)(2,1)}, bf16[2,2,128,256]{3,2,1,0:T(8,128)(2,1)S(1)}, u32[]{:S(2)}, u32[]{:S(2)}) collective-permute-start(bf16[2,2,128,256]{3,2,1,0:T(8,128)(2,1)} %a_ref.1), channel_id=1, source_target_pairs={{0,2},{1,7},{2,0},{3,5},{4,6},{5,3},{6,4},{7,1},{8,10},{9,15},{10,... | collective-permute-start | bytes 786440 | tf_op jit(solution)/shard_map/ppermute | solution.py:186
  4.7 1.3 %collective-permute-start.2 = (bf16[2,128,512]{2,1,0:T(8,128)(2,1)S(1)}, bf16[2,128,512]{2,1,0:T(8,128)(2,1)S(1)}, u32[]{:S(2)}, u32[]{:S(2)}) collective-permute-start(bf16[2,128,512]{2,1,0:T(8,128)(2,1)S(1)} %shard_map.48.a_ref), channel_id=1, source_target_pairs={{0,32},{1,97},{32,0},{33,65},{64,96},{65,33},{96,64},{97,1},{2,34}... | collective-permute-start | bytes 786440 | tf_op jit(solution)/shard_map/ppermute | solution.py:186
  6.0 3.4 %collective-permute-done.6.a_ref = bf16[2,2,128,256]{3,2,1,0:T(8,128)(2,1)S(1)} collective-permute-done((bf16[2,2,128,256]{3,2,1,0:T(8,128)(2,1)}, bf16[2,2,128,256]{3,2,1,0:T(8,128)(2,1)S(1)}, u32[]{:S(2)}, u32[]{:S(2)}) %collective-permute-start.6) | collective-permute-done | bytes 262176 | tf_op jit(solution)/shard_map/ppermute | solution.py:181
  9.3 3.0 %collective-permute-start.7 = (bf16[2,2,128,256]{3,2,1,0:T(8,128)(2,1)S(1)}, bf16[2,2,128,256]{3,2,1,0:T(8,128)(2,1)S(1)}, u32[]{:S(2)}, u32[]{:S(2)}) collective-permute-start(bf16[2,2,128,256]{3,2,1,0:T(8,128)(2,1)S(1)} %collective-permute-done.6.a_ref), channel_id=1, source_target_pairs={{0,6},{1,3},{2,4},{3,1},{4,2},{5,7},{6,0},{7,5},{8,14},{9,11},{10,... | collective-permute-start | bytes 786440 | tf_op jit(solution)/shard_map/ppermute | solution.py:186
  14.4 1.8 %collective-permute-done.8.a_ref = bf16[2,128,512]{2,1,0:T(8,128)(2,1)S(1)} collective-permute-done((bf16[2,128,512]{2,1,0:T(8,128)(2,1)S(1)}, bf16[2,128,512]{2,1,0:T(8,128)(2,1)S(1)}, u32[]{:S(2)}, u32[]{:S(2)}) %collective-permute-start.8) | collective-permute-done | bytes 262176 | tf_op jit(solution)/shard_map/ppermute | solution.py:181
  18.0 7.9 %collective-permute-done.11.b_ref = bf16[2,128,512]{2,1,0:T(8,128)(2,1)S(1)} collective-permute-done((bf16[2,128,512]{2,1,0:T(8,128)(2,1)S(1)}, bf16[2,128,512]{2,1,0:T(8,128)(2,1)S(1)}, u32[]{:S(2)}, u32[]{:S(2)}) %collective-permute-start.11) | collective-permute-done | bytes 262176 | tf_op jit(solution)/shard_map/ppermute | solution.py:186
  25.9 2.5 %collective-permute-start.12 = (bf16[2,2,128,512]{3,2,1,0:T(8,128)(2,1)S(1)}, bf16[2,2,128,512]{3,2,1,0:T(8,128)(2,1)S(1)}, u32[]{:S(2)}, u32[]{:S(2)}) collective-permute-start(bf16[2,2,128,512]{3,2,1,0:T(8,128)(2,1)S(1)} %shard_map.53.r2), channel_id=1, source_target_pairs={{0,32},{1,97},{32,0},{33,65},{64,96},{65,33},{96,64},{97,1},{2,34}... | collective-permute-start | bytes 1572872 | tf_op jit(solution)/shard_map/ppermute | solution.py:186
  28.4 1.6 %shard_map.46.w_ref = bf16[2,512,2048]{2,1,0:T(8,128)(2,1)S(1)} custom-call(s32[2,3]{1,0:T(2,128)S(1)} %bitcast.1, s32[3]{0:T(128)S(1)} %copy-done.2, bf16[2,2,128,2048]{3,2,1,0:T(8,128)(2,1)S(1)} %copy-done, bf16[2,2,128,2048]{3,2,1,0:T(8,128)(2,1)S(1)} %collective-permute-done.mate_ref), custom_call_target="tpu_custom_call" | custom-call | tf_op jit(solution)/shard_map/pallas_call | solution.py:24
  30.1 3.0 %shard_map.52 = (bf16[2,2,128,256]{3,2,1,0:T(8,128)(2,1)S(1)}, bf16[2,2,128,256]{3,2,1,0:T(8,128)(2,1)S(1)}, bf16[2,2,128,256]{3,2,1,0:T(8,128)(2,1)S(1)}) custom-call(bf16[2,512,2048]{2,1,0:T(8,128)(2,1)S(1)} %shard_map.46.w_ref, bf16[2,2,2,128,256]{4,3,2,1,0:T(8,128)(2,1)S(1)} %shard_map.50.refs_0_, ...), custom_call_target="tpu_custom_call" | custom-call | tf_op jit(solution)/shard_map/pallas_call | solution.py:24
  33.8 1.8 %collective-permute-done.12.r3 = bf16[2,2,128,512]{3,2,1,0:T(8,128)(2,1)S(1)} collective-permute-done((bf16[2,2,128,512]{3,2,1,0:T(8,128)(2,1)S(1)}, bf16[2,2,128,512]{3,2,1,0:T(8,128)(2,1)S(1)}, u32[]{:S(2)}, u32[]{:S(2)}) %collective-permute-start.12) | collective-permute-done | bytes 524320 | tf_op jit(solution)/shard_map/ppermute | solution.py:186
  35.6 1.3 %shard_map.54 = (bf16[2,128,768]{2,1,0:T(8,128)(2,1)S(1)}, bf16[2,128,768]{2,1,0:T(8,128)(2,1)S(1)}, bf16[2,128,768]{2,1,0:T(8,128)(2,1)S(1)}, bf16[2,128,768]{2...) custom-call(bf16[2,2,128,256]{3,2,1,0:T(8,128)(2,1)S(1)} %get-tuple-element.34.m0_ref, ...), custom_call_target="tpu_custom_call" | custom-call | tf_op jit(solution)/shard_map/pallas_call | solution.py:24
  37.6 1.6 %collective-permute-start.15 = (bf16[4,128,768]{2,1,0:T(8,128)(2,1)S(1)}, bf16[4,128,768]{2,1,0:T(8,128)(2,1)S(1)}, u32[]{:S(2)}, u32[]{:S(2)}) collective-permute-start(bf16[4,128,768]{2,1,0:T(8,128)(2,1)S(1)} %get-tuple-element.38), channel_id=1, source_target_pairs={{0,8},{8,0},{1,9},{9,1},{2,10},{10,2},{3,11},{11,3},{4,12},{12,4},... | collective-permute-start | bytes 2359304 | tf_op jit(solution)/shard_map/ppermute | solution.py:181
  39.6 3.0 %collective-permute-start.20 = (bf16[2,128,768]{2,1,0:T(8,128)(2,1)S(1)}, bf16[2,128,768]{2,1,0:T(8,128)(2,1)S(1)}, u32[]{:S(2)}, u32[]{:S(2)}) collective-permute-start(bf16[2,128,768]{2,1,0:T(8,128)(2,1)S(1)} %get-tuple-element.45), channel_id=1, source_target_pairs={{0,6},{2,0},{4,2},{6,4},{1,7},{3,1},{5,3},{7,5},{8,14},{10,8},{12,... | collective-permute-start | bytes 1179656 | tf_op jit(solution)/shard_map/ppermute | solution.py:181
  42.6 1.5 %collective-permute-start.21 = (bf16[2,128,768]{2,1,0:T(8,128)(2,1)S(1)}, bf16[2,128,768]{2,1,0:T(8,128)(2,1)S(1)}, u32[]{:S(2)}, u32[]{:S(2)}) collective-permute-start(bf16[2,128,768]{2,1,0:T(8,128)(2,1)S(1)} %get-tuple-element.46), channel_id=1, source_target_pairs={{0,4},{2,6},{4,0},{6,2},{1,5},{3,7},{5,1},{7,3},{8,12},{10,14},{12... | collective-permute-start | bytes 1179656 | tf_op jit(solution)/shard_map/ppermute | solution.py:181
  44.0 12.8 %collective-permute-done.15.got_ref = bf16[4,128,768]{2,1,0:T(8,128)(2,1)S(1)} collective-permute-done((bf16[4,128,768]{2,1,0:T(8,128)(2,1)S(1)}, bf16[4,128,768]{2,1,0:T(8,128)(2,1)S(1)}, u32[]{:S(2)}, u32[]{:S(2)}) %collective-permute-start.15) | collective-permute-done | bytes 786464 | tf_op jit(solution)/shard_map/ppermute | solution.py:181
  57.0 1.8 %collective-permute-done.20.g2_ref = bf16[2,128,768]{2,1,0:T(8,128)(2,1)S(1)} collective-permute-done((bf16[2,128,768]{2,1,0:T(8,128)(2,1)S(1)}, bf16[2,128,768]{2,1,0:T(8,128)(2,1)S(1)}, u32[]{:S(2)}, u32[]{:S(2)}) %collective-permute-start.20) | collective-permute-done | bytes 393248 | tf_op jit(solution)/shard_map/ppermute | solution.py:181
  58.8 1.9 %collective-permute-done.21.g3_ref = bf16[2,128,768]{2,1,0:T(8,128)(2,1)S(1)} collective-permute-done((bf16[2,128,768]{2,1,0:T(8,128)(2,1)S(1)}, bf16[2,128,768]{2,1,0:T(8,128)(2,1)S(1)}, u32[]{:S(2)}, u32[]{:S(2)}) %collective-permute-start.21) | collective-permute-done | bytes 393248 | tf_op jit(solution)/shard_map/ppermute | solution.py:181
  61.6 1.1 %collective-permute-start.16 = (bf16[128,768]{1,0:T(8,128)(2,1)S(1)}, bf16[128,768]{1,0:T(8,128)(2,1)S(1)}, u32[]{:S(2)}, u32[]{:S(2)}) collective-permute-start(bf16[128,768]{1,0:T(8,128)(2,1)S(1)} %get-tuple-element.40), channel_id=1, source_target_pairs={{0,2},{2,4},{4,6},{6,0},{1,3},{3,5},{5,7},{7,1},{8,10},{10,12},{12... | collective-permute-start | bytes 589832 | tf_op jit(solution)/shard_map/ppermute | solution.py:181
  62.7 2.1 %collective-permute-start.17 = (bf16[128,768]{1,0:T(8,128)(2,1)S(1)}, bf16[128,768]{1,0:T(8,128)(2,1)S(1)}, u32[]{:S(2)}, u32[]{:S(2)}) collective-permute-start(bf16[128,768]{1,0:T(8,128)(2,1)S(1)} %get-tuple-element.41), channel_id=1, source_target_pairs={{0,6},{2,0},{4,2},{6,4},{1,7},{3,1},{5,3},{7,5},{8,14},{10,8},{12,... | collective-permute-start | bytes 589832 | tf_op jit(solution)/shard_map/ppermute | solution.py:181
  64.9 1.8 %collective-permute-done.22.y1_ref = bf16[128,768]{1,0:T(8,128)(2,1)S(1)} collective-permute-done((bf16[128,768]{1,0:T(8,128)(2,1)S(1)}, bf16[128,768]{1,0:T(8,128)(2,1)S(1)}, u32[]{:S(2)}, u32[]{:S(2)}) %collective-permute-start.22) | collective-permute-done | bytes 196640 | tf_op jit(solution)/shard_map/ppermute | solution.py:181
  66.7 3.8 %collective-permute-done.16.z1_ref = bf16[128,768]{1,0:T(8,128)(2,1)S(1)} collective-permute-done((bf16[128,768]{1,0:T(8,128)(2,1)S(1)}, bf16[128,768]{1,0:T(8,128)(2,1)S(1)}, u32[]{:S(2)}, u32[]{:S(2)}) %collective-permute-start.16) | collective-permute-done | bytes 196640 | tf_op jit(solution)/shard_map/ppermute | solution.py:181
  71.2 1.5 %collective-permute-done.18.z3_ref = bf16[128,768]{1,0:T(8,128)(2,1)S(1)} collective-permute-done((bf16[128,768]{1,0:T(8,128)(2,1)S(1)}, bf16[128,768]{1,0:T(8,128)(2,1)S(1)}, u32[]{:S(2)}, u32[]{:S(2)}) %collective-permute-start.18) | collective-permute-done | bytes 196640 | tf_op jit(solution)/shard_map/ppermute | solution.py:181
  (42 shorter events, 9.4 us)
Async XLA Ops:
  0.0 28.4 %collective-permute-start = (bf16[2,2,128,2048]{3,2,1,0:T(8,128)(2,1)}, bf16[2,2,128,2048]{3,2,1,0:T(8,128)(2,1)S(1)}, u32[]{:S(2)}, u32[]{:S(2)}) collective-permute-start(bf16[2,2,128,2048]{3,2,1,0:T(8,128)(2,1)} %own_ref.1), channel_id=1, source_target_pairs={{0,1},{1,0},{2,3},{3,2},{4,5},{5,4},{6,7},{7,6},{8,9},{9,8},{10,11... | collective-permute-start | bytes 6291464 | tf_op jit(solution)/shard_map/ppermute | solution.py:181
  0.0 9.3 %collective-permute-start.6 = (bf16[2,2,128,256]{3,2,1,0:T(8,128)(2,1)}, bf16[2,2,128,256]{3,2,1,0:T(8,128)(2,1)S(1)}, u32[]{:S(2)}, u32[]{:S(2)}) collective-permute-start(bf16[2,2,128,256]{3,2,1,0:T(8,128)(2,1)} %a_ref.1), channel_id=1, source_target_pairs={{0,8},{8,0},{1,9},{9,1},{2,10},{10,2},{3,11},{11,3},{4,12},{12,4},... | collective-permute-start | bytes 786440 | tf_op jit(solution)/shard_map/ppermute | solution.py:181
  2.7 1.9 %collective-permute-start.1 = (bf16[2,128,256]{2,1,0:T(8,128)(2,1)S(1)}, bf16[2,128,256]{2,1,0:T(8,128)(2,1)S(1)}, u32[]{:S(2)}, u32[]{:S(2)}) collective-permute-start(bf16[2,128,256]{2,1,0:T(8,128)(2,1)S(1)} %get-tuple-element.28), channel_id=1, source_target_pairs={{0,1},{1,0},{2,3},{3,2},{4,5},{5,4},{6,7},{7,6},{8,9},{9,8},{10,11... | collective-permute-start | bytes 393224 | tf_op jit(solution)/shard_map/ppermute | solution.py:181
  3.0 9.3 %collective-permute-start.4 = (bf16[2,2,128,256]{3,2,1,0:T(8,128)(2,1)}, bf16[2,2,128,256]{3,2,1,0:T(8,128)(2,1)S(1)}, u32[]{:S(2)}, u32[]{:S(2)}) collective-permute-start(bf16[2,2,128,256]{3,2,1,0:T(8,128)(2,1)} %a_ref.1), channel_id=1, source_target_pairs={{0,2},{1,7},{2,0},{3,5},{4,6},{5,3},{6,4},{7,1},{8,10},{9,15},{10,... | collective-permute-start | bytes 786440 | tf_op jit(solution)/shard_map/ppermute | solution.py:186
  4.6 23.8 %copy-start = (bf16[2,2,128,2048]{3,2,1,0:T(8,128)(2,1)S(1)}, bf16[2,2,128,2048]{3,2,1,0:T(8,128)(2,1)}, u32[]{:S(2)}) copy-start(bf16[2,2,128,2048]{3,2,1,0:T(8,128)(2,1)} %own_ref.1) | copy-start | bytes 6291460
  4.7 9.0 %collective-permute-start.2 = (bf16[2,128,512]{2,1,0:T(8,128)(2,1)S(1)}, bf16[2,128,512]{2,1,0:T(8,128)(2,1)S(1)}, u32[]{:S(2)}, u32[]{:S(2)}) collective-permute-start(bf16[2,128,512]{2,1,0:T(8,128)(2,1)S(1)} %shard_map.48.a_ref), channel_id=1, source_target_pairs={{0,32},{1,97},{32,0},{33,65},{64,96},{65,33},{96,64},{97,1},{2,34}... | collective-permute-start | bytes 786440 | tf_op jit(solution)/shard_map/ppermute | solution.py:186
  6.0 10.2 %collective-permute-start.8 = (bf16[2,128,512]{2,1,0:T(8,128)(2,1)S(1)}, bf16[2,128,512]{2,1,0:T(8,128)(2,1)S(1)}, u32[]{:S(2)}, u32[]{:S(2)}) collective-permute-start(bf16[2,128,512]{2,1,0:T(8,128)(2,1)S(1)} %shard_map.48.a_ref), channel_id=1, source_target_pairs={{0,16},{16,0},{1,17},{17,1},{2,18},{18,2},{3,19},{19,3},{4,20},{20... | collective-permute-start | bytes 786440 | tf_op jit(solution)/shard_map/ppermute | solution.py:181
  9.3 7.6 %collective-permute-start.7 = (bf16[2,2,128,256]{3,2,1,0:T(8,128)(2,1)S(1)}, bf16[2,2,128,256]{3,2,1,0:T(8,128)(2,1)S(1)}, u32[]{:S(2)}, u32[]{:S(2)}) collective-permute-start(bf16[2,2,128,256]{3,2,1,0:T(8,128)(2,1)S(1)} %collective-permute-done.6.a_ref), channel_id=1, source_target_pairs={{0,6},{1,3},{2,4},{3,1},{4,2},{5,7},{6,0},{7,5},{8,14},{9,11},{10,... | collective-permute-start | bytes 786440 | tf_op jit(solution)/shard_map/ppermute | solution.py:186
  13.3 16.8 %collective-permute-start.5 = (bf16[2,2,2,128,256]{4,3,2,1,0:T(8,128)(2,1)S(1)}, bf16[2,2,2,128,256]{4,3,2,1,0:T(8,128)(2,1)S(1)}, u32[]{:S(2)}, u32[]{:S(2)}) collective-permute-start(bf16[2,2,2,128,256]{4,3,2,1,0:T(8,128)(2,1)S(1)} %shard_map.50.refs_0_), channel_id=1, source_target_pairs={{0,6},{1,3},{2,4},{3,1},{4,2},{5,7},{6,0},{7,5},{8,14},{9,11},{10,... | collective-permute-start | bytes 1572872 | tf_op jit(solution)/shard_map/ppermute | solution.py:186
  13.8 16.3 %collective-permute-start.3 = (bf16[2,2,128,512]{3,2,1,0:T(8,128)(2,1)S(1)}, bf16[2,2,128,512]{3,2,1,0:T(8,128)(2,1)S(1)}, u32[]{:S(2)}, u32[]{:S(2)}) collective-permute-start(bf16[2,2,128,512]{3,2,1,0:T(8,128)(2,1)S(1)} %shard_map.49.r0), channel_id=1, source_target_pairs={{0,96},{1,33},{32,64},{33,1},{64,32},{65,97},{96,0},{97,65},{2,98}... | collective-permute-start | bytes 1572872 | tf_op jit(solution)/shard_map/ppermute | solution.py:186
  17.0 13.1 %collective-permute-start.9 = (bf16[2,2,2,128,256]{4,3,2,1,0:T(8,128)(2,1)S(1)}, bf16[2,2,2,128,256]{4,3,2,1,0:T(8,128)(2,1)S(1)}, u32[]{:S(2)}, u32[]{:S(2)}) collective-permute-start(bf16[2,2,2,128,256]{4,3,2,1,0:T(8,128)(2,1)S(1)} %shard_map.51.refs_2_), channel_id=1, source_target_pairs={{0,2},{1,7},{2,0},{3,5},{4,6},{5,3},{6,4},{7,1},{8,10},{9,15},{10,... | collective-permute-start | bytes 1572872 | tf_op jit(solution)/shard_map/ppermute | solution.py:186
  17.4 8.4 %collective-permute-start.11 = (bf16[2,128,512]{2,1,0:T(8,128)(2,1)S(1)}, bf16[2,128,512]{2,1,0:T(8,128)(2,1)S(1)}, u32[]{:S(2)}, u32[]{:S(2)}) collective-permute-start(bf16[2,128,512]{2,1,0:T(8,128)(2,1)S(1)} %collective-permute-done.8.a_ref), channel_id=1, source_target_pairs={{0,96},{1,33},{32,64},{33,1},{64,32},{65,97},{96,0},{97,65},{2,98}... | collective-permute-start | bytes 786440 | tf_op jit(solution)/shard_map/ppermute | solution.py:186
  25.9 9.6 %collective-permute-start.12 = (bf16[2,2,128,512]{3,2,1,0:T(8,128)(2,1)S(1)}, bf16[2,2,128,512]{3,2,1,0:T(8,128)(2,1)S(1)}, u32[]{:S(2)}, u32[]{:S(2)}) collective-permute-start(bf16[2,2,128,512]{3,2,1,0:T(8,128)(2,1)S(1)} %shard_map.53.r2), channel_id=1, source_target_pairs={{0,32},{1,97},{32,0},{33,65},{64,96},{65,33},{96,64},{97,1},{2,34}... | collective-permute-start | bytes 1572872 | tf_op jit(solution)/shard_map/ppermute | solution.py:186
  33.1 2.5 %collective-permute-start.13 = (bf16[2,2,128,256]{3,2,1,0:T(8,128)(2,1)S(1)}, bf16[2,2,128,256]{3,2,1,0:T(8,128)(2,1)S(1)}, u32[]{:S(2)}, u32[]{:S(2)}) collective-permute-start(bf16[2,2,128,256]{3,2,1,0:T(8,128)(2,1)S(1)} %get-tuple-element.34.m0_ref), channel_id=1, source_target_pairs={{0,1},{1,0},{2,3},{3,2},{4,5},{5,4},{6,7},{7,6},{8,9},{9,8},{10,11... | collective-permute-start | bytes 786440 | tf_op jit(solution)/shard_map/ppermute | solution.py:181
  33.2 2.4 %collective-permute-start.14 = (bf16[2,2,128,256]{3,2,1,0:T(8,128)(2,1)S(1)}, bf16[2,2,128,256]{3,2,1,0:T(8,128)(2,1)S(1)}, u32[]{:S(2)}, u32[]{:S(2)}) collective-permute-start(bf16[2,2,128,256]{3,2,1,0:T(8,128)(2,1)S(1)} %get-tuple-element.35.m1_ref), channel_id=1, source_target_pairs={{0,1},{1,0},{2,3},{3,2},{4,5},{5,4},{6,7},{7,6},{8,9},{9,8},{10,11... | collective-permute-start | bytes 786440 | tf_op jit(solution)/shard_map/ppermute | solution.py:181
  33.7 3.2 %collective-permute-start.10 = (bf16[2,2,128,256]{3,2,1,0:T(8,128)(2,1)S(1)}, bf16[2,2,128,256]{3,2,1,0:T(8,128)(2,1)S(1)}, u32[]{:S(2)}, u32[]{:S(2)}) collective-permute-start(bf16[2,2,128,256]{3,2,1,0:T(8,128)(2,1)S(1)} %get-tuple-element.31.mine_ref), channel_id=1, source_target_pairs={{0,1},{1,0},{2,3},{3,2},{4,5},{5,4},{6,7},{7,6},{8,9},{9,8},{10,11... | collective-permute-start | bytes 786440 | tf_op jit(solution)/shard_map/ppermute | solution.py:181
  37.6 19.2 %collective-permute-start.15 = (bf16[4,128,768]{2,1,0:T(8,128)(2,1)S(1)}, bf16[4,128,768]{2,1,0:T(8,128)(2,1)S(1)}, u32[]{:S(2)}, u32[]{:S(2)}) collective-permute-start(bf16[4,128,768]{2,1,0:T(8,128)(2,1)S(1)} %get-tuple-element.38), channel_id=1, source_target_pairs={{0,8},{8,0},{1,9},{9,1},{2,10},{10,2},{3,11},{11,3},{4,12},{12,4},... | collective-permute-start | bytes 2359304 | tf_op jit(solution)/shard_map/ppermute | solution.py:181
  39.3 17.7 %collective-permute-start.19 = (bf16[2,128,768]{2,1,0:T(8,128)(2,1)S(1)}, bf16[2,128,768]{2,1,0:T(8,128)(2,1)S(1)}, u32[]{:S(2)}, u32[]{:S(2)}) collective-permute-start(bf16[2,128,768]{2,1,0:T(8,128)(2,1)S(1)} %get-tuple-element.44), channel_id=1, source_target_pairs={{0,2},{2,4},{4,6},{6,0},{1,3},{3,5},{5,7},{7,1},{8,10},{10,12},{12... | collective-permute-start | bytes 1179656 | tf_op jit(solution)/shard_map/ppermute | solution.py:181
  39.6 19.2 %collective-permute-start.20 = (bf16[2,128,768]{2,1,0:T(8,128)(2,1)S(1)}, bf16[2,128,768]{2,1,0:T(8,128)(2,1)S(1)}, u32[]{:S(2)}, u32[]{:S(2)}) collective-permute-start(bf16[2,128,768]{2,1,0:T(8,128)(2,1)S(1)} %get-tuple-element.45), channel_id=1, source_target_pairs={{0,6},{2,0},{4,2},{6,4},{1,7},{3,1},{5,3},{7,5},{8,14},{10,8},{12,... | collective-permute-start | bytes 1179656 | tf_op jit(solution)/shard_map/ppermute | solution.py:181
  42.6 18.2 %collective-permute-start.21 = (bf16[2,128,768]{2,1,0:T(8,128)(2,1)S(1)}, bf16[2,128,768]{2,1,0:T(8,128)(2,1)S(1)}, u32[]{:S(2)}, u32[]{:S(2)}) collective-permute-start(bf16[2,128,768]{2,1,0:T(8,128)(2,1)S(1)} %get-tuple-element.46), channel_id=1, source_target_pairs={{0,4},{2,6},{4,0},{6,2},{1,5},{3,7},{5,1},{7,3},{8,12},{10,14},{12... | collective-permute-start | bytes 1179656 | tf_op jit(solution)/shard_map/ppermute | solution.py:181
  60.9 5.8 %collective-permute-start.22 = (bf16[128,768]{1,0:T(8,128)(2,1)S(1)}, bf16[128,768]{1,0:T(8,128)(2,1)S(1)}, u32[]{:S(2)}, u32[]{:S(2)}) collective-permute-start(bf16[128,768]{1,0:T(8,128)(2,1)S(1)} %get-tuple-element.48), channel_id=1, source_target_pairs={{0,8},{8,0},{1,9},{9,1},{2,10},{10,2},{3,11},{11,3},{4,12},{12,4},... | collective-permute-start | bytes 589832 | tf_op jit(solution)/shard_map/ppermute | solution.py:181
  61.6 8.9 %collective-permute-start.16 = (bf16[128,768]{1,0:T(8,128)(2,1)S(1)}, bf16[128,768]{1,0:T(8,128)(2,1)S(1)}, u32[]{:S(2)}, u32[]{:S(2)}) collective-permute-start(bf16[128,768]{1,0:T(8,128)(2,1)S(1)} %get-tuple-element.40), channel_id=1, source_target_pairs={{0,2},{2,4},{4,6},{6,0},{1,3},{3,5},{5,7},{7,1},{8,10},{10,12},{12... | collective-permute-start | bytes 589832 | tf_op jit(solution)/shard_map/ppermute | solution.py:181
  62.7 8.5 %collective-permute-start.17 = (bf16[128,768]{1,0:T(8,128)(2,1)S(1)}, bf16[128,768]{1,0:T(8,128)(2,1)S(1)}, u32[]{:S(2)}, u32[]{:S(2)}) collective-permute-start(bf16[128,768]{1,0:T(8,128)(2,1)S(1)} %get-tuple-element.41), channel_id=1, source_target_pairs={{0,6},{2,0},{4,2},{6,4},{1,7},{3,1},{5,3},{7,5},{8,14},{10,8},{12,... | collective-permute-start | bytes 589832 | tf_op jit(solution)/shard_map/ppermute | solution.py:181
  64.8 7.9 %collective-permute-start.18 = (bf16[128,768]{1,0:T(8,128)(2,1)S(1)}, bf16[128,768]{1,0:T(8,128)(2,1)S(1)}, u32[]{:S(2)}, u32[]{:S(2)}) collective-permute-start(bf16[128,768]{1,0:T(8,128)(2,1)S(1)} %get-tuple-element.42), channel_id=1, source_target_pairs={{0,4},{2,6},{4,0},{6,2},{1,5},{3,7},{5,1},{7,3},{8,12},{10,14},{12... | collective-permute-start | bytes 589832 | tf_op jit(solution)/shard_map/ppermute | solution.py:181
  (2 other events, 47.5 us)

commit v5 on v4

--- a/solution.py
+++ b/solution.py
@@ -257,7 +257,7 @@
     y_got = [shift(y1, "y", 4, 1), shift(y3, "y", 4, -1), shift(y2, "y", 4, 2)]
     z_sums = call(add_z, [(128, WIDE_Z)] * 4, [VMEM] * 2, z_keep, z_got)
     y_keep, y_send = call(add_y, [(128, WIDE_Y)] * 2, [VMEM] * 4 + [ANY], y_keep, *y_got, z_sums[0])
-    z_last = [shift(z_sums[1], "y", 4, 1), shift(z_sums[3], "y", 4, -1), shift(z_sums[2], "y", 4, 2)]
+    z_last = [shift(z_sums[2], "y", 4, 2), shift(z_sums[1], "y", 4, 1), shift(z_sums[3], "y", 4, -1)]
     y_last = shift(y_send, "zl", 2, 1)
     (out,) = call(finish, [(3, 128, 512)], [SMEM] + [VMEM] * 6, pairs, z_sums[0], *z_last, y_keep, y_last)
     return out.reshape(3, 128, 2, 256)

time: 74.4 us -> 73.9 us (level)
  the two profiles are of different devices: /device:TPU:68 before, /device:TPU:6 now
where the time goes in v5:
time: 73.9 us; the launch traced here: 73.6 us
  waiting for transfers between devices  34.1 us (46%)
  starting transfers between devices  28.4 us (38%)
  Pallas kernels  10 us (14%)
  local copies, waits for them, and re-layouts  0.86 us (1%)
    ppermute x15, waiting for transfers between devices, shift(): return lax.ppermute(x, axis, [(i, (i + step) % size) for i in range(size)])  23.3 us
    ppermute x15, starting transfers between devices, shift(): return lax.ppermute(x, axis, [(i, (i + step) % size) for i in range(size)])  19.1 us
    ppermute x8, waiting for transfers between devices, ring_swap(): return lax.ppermute(x, (axis, 'c'), pairs)  10.9 us
    pallas_call x13, Pallas kernels, call(): pl.pallas_call(body, out_shape=[jax.ShapeDtypeStruct(s, BF) for s in outs...  10 us
    ppermute x8, starting transfers between devices, ring_swap(): return lax.ppermute(x, (axis, 'c'), pairs)  9.24 us
  transfers between devices with their start and end apart: 23, of which 9 were waited for; matrix products, arithmetic and copies ran while one was open for 0% of the time, Pallas kernels for 11%

profile of v5, /device:TPU:6, one launch (start us, length us, event | category | flops | bytes accessed | tf_op | source)
XLA Modules:
  0.0 73.6 jit_solution(9618223949683868987)
XLA Ops:
  0.0 1.9 %collective-permute-start.6 = (bf16[2,2,128,256]{3,2,1,0:T(8,128)(2,1)}, bf16[2,2,128,256]{3,2,1,0:T(8,128)(2,1)S(1)}, u32[]{:S(2)}, u32[]{:S(2)}) collective-permute-start(bf16[2,2,128,256]{3,2,1,0:T(8,128)(2,1)} %a_ref.1), channel_id=1, source_target_pairs={{0,8},{8,0},{1,9},{9,1},{2,10},{10,2},{3,11},{11,3},{4,12},{12,4},... | collective-permute-start | bytes 786440 | tf_op jit(solution)/shard_map/ppermute | solution.py:181
  1.9 1.1 %shard_map.47 = (bf16[2,128,256]{2,1,0:T(8,128)(2,1)S(1)}, bf16[2,128,256]{2,1,0:T(8,128)(2,1)S(1)}) custom-call(bf16[2,2,128,256]{3,2,1,0:T(8,128)(2,1)} %a_ref.1), custom_call_target="tpu_custom_call" | custom-call | tf_op jit(solution)/shard_map/pallas_call | solution.py:24
  3.3 1.6 %collective-permute-start.4 = (bf16[2,2,128,256]{3,2,1,0:T(8,128)(2,1)}, bf16[2,2,128,256]{3,2,1,0:T(8,128)(2,1)S(1)}, u32[]{:S(2)}, u32[]{:S(2)}) collective-permute-start(bf16[2,2,128,256]{3,2,1,0:T(8,128)(2,1)} %a_ref.1), channel_id=1, source_target_pairs={{0,2},{1,7},{2,0},{3,5},{4,6},{5,3},{6,4},{7,1},{8,10},{9,15},{10,... | collective-permute-start | bytes 786440 | tf_op jit(solution)/shard_map/ppermute | solution.py:186
  5.9 3.6 %collective-permute-start.8 = (bf16[2,128,512]{2,1,0:T(8,128)(2,1)S(1)}, bf16[2,128,512]{2,1,0:T(8,128)(2,1)S(1)}, u32[]{:S(2)}, u32[]{:S(2)}) collective-permute-start(bf16[2,128,512]{2,1,0:T(8,128)(2,1)S(1)} %shard_map.48.a_ref), channel_id=1, source_target_pairs={{0,16},{16,0},{1,17},{17,1},{2,18},{18,2},{3,19},{19,3},{4,20},{20... | collective-permute-start | bytes 786440 | tf_op jit(solution)/shard_map/ppermute | solution.py:181
  9.5 2.7 %collective-permute-start.7 = (bf16[2,2,128,256]{3,2,1,0:T(8,128)(2,1)S(1)}, bf16[2,2,128,256]{3,2,1,0:T(8,128)(2,1)S(1)}, u32[]{:S(2)}, u32[]{:S(2)}) collective-permute-start(bf16[2,2,128,256]{3,2,1,0:T(8,128)(2,1)S(1)} %collective-permute-done.6.a_ref), channel_id=1, source_target_pairs={{0,6},{1,3},{2,4},{3,1},{4,2},{5,7},{6,0},{7,5},{8,14},{9,11},{10,... | collective-permute-start | bytes 786440 | tf_op jit(solution)/shard_map/ppermute | solution.py:186
  12.2 1.0 %shard_map.50.refs_0_ = bf16[2,2,2,128,256]{4,3,2,1,0:T(8,128)(2,1)S(1)} custom-call(bf16[2,2,128,256]{3,2,1,0:T(8,128)(2,1)} %a_ref.1, bf16[2,2,128,256]{3,2,1,0:T(8,128)(2,1)S(1)} %collective-permute-done.4.b_ref), custom_call_target="tpu_custom_call" | custom-call | tf_op jit(solution)/shard_map/pallas_call | solution.py:24
  14.1 1.0 %collective-permute-start.3 = (bf16[2,2,128,512]{3,2,1,0:T(8,128)(2,1)S(1)}, bf16[2,2,128,512]{3,2,1,0:T(8,128)(2,1)S(1)}, u32[]{:S(2)}, u32[]{:S(2)}) collective-permute-start(bf16[2,2,128,512]{3,2,1,0:T(8,128)(2,1)S(1)} %shard_map.49.r0), channel_id=1, source_target_pairs={{0,96},{1,33},{32,64},{33,1},{64,32},{65,97},{96,0},{97,65},{2,98}... | collective-permute-start | bytes 1572872 | tf_op jit(solution)/shard_map/ppermute | solution.py:186
  15.1 3.0 %collective-permute-done.8.a_ref = bf16[2,128,512]{2,1,0:T(8,128)(2,1)S(1)} collective-permute-done((bf16[2,128,512]{2,1,0:T(8,128)(2,1)S(1)}, bf16[2,128,512]{2,1,0:T(8,128)(2,1)S(1)}, u32[]{:S(2)}, u32[]{:S(2)}) %collective-permute-start.8) | collective-permute-done | bytes 262176 | tf_op jit(solution)/shard_map/ppermute | solution.py:181
  18.1 1.7 %collective-permute-start.9 = (bf16[2,2,2,128,256]{4,3,2,1,0:T(8,128)(2,1)S(1)}, bf16[2,2,2,128,256]{4,3,2,1,0:T(8,128)(2,1)S(1)}, u32[]{:S(2)}, u32[]{:S(2)}) collective-permute-start(bf16[2,2,2,128,256]{4,3,2,1,0:T(8,128)(2,1)S(1)} %shard_map.51.refs_2_), channel_id=1, source_target_pairs={{0,2},{1,7},{2,0},{3,5},{4,6},{5,3},{6,4},{7,1},{8,10},{9,15},{10,... | collective-permute-start | bytes 1572872 | tf_op jit(solution)/shard_map/ppermute | solution.py:186
  20.2 7.1 %collective-permute-done.11.b_ref = bf16[2,128,512]{2,1,0:T(8,128)(2,1)S(1)} collective-permute-done((bf16[2,128,512]{2,1,0:T(8,128)(2,1)S(1)}, bf16[2,128,512]{2,1,0:T(8,128)(2,1)S(1)}, u32[]{:S(2)}, u32[]{:S(2)}) %collective-permute-start.11) | collective-permute-done | bytes 262176 | tf_op jit(solution)/shard_map/ppermute | solution.py:186
  27.5 1.6 %shard_map.46.w_ref = bf16[2,512,2048]{2,1,0:T(8,128)(2,1)S(1)} custom-call(s32[2,3]{1,0:T(2,128)S(1)} %bitcast.1, s32[3]{0:T(128)S(1)} %copy-done.2, bf16[2,2,128,2048]{3,2,1,0:T(8,128)(2,1)S(1)} %copy-done, bf16[2,2,128,2048]{3,2,1,0:T(8,128)(2,1)S(1)} %collective-permute-done.mate_ref), custom_call_target="tpu_custom_call" | custom-call | tf_op jit(solution)/shard_map/pallas_call | solution.py:24
  29.2 3.0 %shard_map.52 = (bf16[2,2,128,256]{3,2,1,0:T(8,128)(2,1)S(1)}, bf16[2,2,128,256]{3,2,1,0:T(8,128)(2,1)S(1)}, bf16[2,2,128,256]{3,2,1,0:T(8,128)(2,1)S(1)}) custom-call(bf16[2,512,2048]{2,1,0:T(8,128)(2,1)S(1)} %shard_map.46.w_ref, bf16[2,2,2,128,256]{4,3,2,1,0:T(8,128)(2,1)S(1)} %shard_map.50.refs_0_, ...), custom_call_target="tpu_custom_call" | custom-call | tf_op jit(solution)/shard_map/pallas_call | solution.py:24
  32.9 3.8 %collective-permute-done.12.r3 = bf16[2,2,128,512]{3,2,1,0:T(8,128)(2,1)S(1)} collective-permute-done((bf16[2,2,128,512]{3,2,1,0:T(8,128)(2,1)S(1)}, bf16[2,2,128,512]{3,2,1,0:T(8,128)(2,1)S(1)}, u32[]{:S(2)}, u32[]{:S(2)}) %collective-permute-start.12) | collective-permute-done | bytes 524320 | tf_op jit(solution)/shard_map/ppermute | solution.py:186
  36.7 1.3 %shard_map.54 = (bf16[2,128,768]{2,1,0:T(8,128)(2,1)S(1)}, bf16[2,128,768]{2,1,0:T(8,128)(2,1)S(1)}, bf16[2,128,768]{2,1,0:T(8,128)(2,1)S(1)}, bf16[2,128,768]{2...) custom-call(bf16[2,2,128,256]{3,2,1,0:T(8,128)(2,1)S(1)} %get-tuple-element.34.m0_ref, ...), custom_call_target="tpu_custom_call" | custom-call | tf_op jit(solution)/shard_map/pallas_call | solution.py:24
  38.7 1.2 %collective-permute-start.15 = (bf16[4,128,768]{2,1,0:T(8,128)(2,1)S(1)}, bf16[4,128,768]{2,1,0:T(8,128)(2,1)S(1)}, u32[]{:S(2)}, u32[]{:S(2)}) collective-permute-start(bf16[4,128,768]{2,1,0:T(8,128)(2,1)S(1)} %get-tuple-element.38), channel_id=1, source_target_pairs={{0,8},{8,0},{1,9},{9,1},{2,10},{10,2},{3,11},{11,3},{4,12},{12,4},... | collective-permute-start | bytes 2359304 | tf_op jit(solution)/shard_map/ppermute | solution.py:181
  40.3 2.9 %collective-permute-start.20 = (bf16[2,128,768]{2,1,0:T(8,128)(2,1)S(1)}, bf16[2,128,768]{2,1,0:T(8,128)(2,1)S(1)}, u32[]{:S(2)}, u32[]{:S(2)}) collective-permute-start(bf16[2,128,768]{2,1,0:T(8,128)(2,1)S(1)} %get-tuple-element.45), channel_id=1, source_target_pairs={{0,6},{2,0},{4,2},{6,4},{1,7},{3,1},{5,3},{7,5},{8,14},{10,8},{12,... | collective-permute-start | bytes 1179656 | tf_op jit(solution)/shard_map/ppermute | solution.py:181
  43.2 1.3 %collective-permute-start.21 = (bf16[2,128,768]{2,1,0:T(8,128)(2,1)S(1)}, bf16[2,128,768]{2,1,0:T(8,128)(2,1)S(1)}, u32[]{:S(2)}, u32[]{:S(2)}) collective-permute-start(bf16[2,128,768]{2,1,0:T(8,128)(2,1)S(1)} %get-tuple-element.46), channel_id=1, source_target_pairs={{0,4},{2,6},{4,0},{6,2},{1,5},{3,7},{5,1},{7,3},{8,12},{10,14},{12... | collective-permute-start | bytes 1179656 | tf_op jit(solution)/shard_map/ppermute | solution.py:181
  44.5 12.6 %collective-permute-done.15.got_ref = bf16[4,128,768]{2,1,0:T(8,128)(2,1)S(1)} collective-permute-done((bf16[4,128,768]{2,1,0:T(8,128)(2,1)S(1)}, bf16[4,128,768]{2,1,0:T(8,128)(2,1)S(1)}, u32[]{:S(2)}, u32[]{:S(2)}) %collective-permute-start.15) | collective-permute-done | bytes 786464 | tf_op jit(solution)/shard_map/ppermute | solution.py:181
  57.7 1.5 %collective-permute-done.21.g3_ref = bf16[2,128,768]{2,1,0:T(8,128)(2,1)S(1)} collective-permute-done((bf16[2,128,768]{2,1,0:T(8,128)(2,1)S(1)}, bf16[2,128,768]{2,1,0:T(8,128)(2,1)S(1)}, u32[]{:S(2)}, u32[]{:S(2)}) %collective-permute-start.21) | collective-permute-done | bytes 393248 | tf_op jit(solution)/shard_map/ppermute | solution.py:181
  59.5 0.9 %collective-permute-start.22 = (bf16[128,768]{1,0:T(8,128)(2,1)S(1)}, bf16[128,768]{1,0:T(8,128)(2,1)S(1)}, u32[]{:S(2)}, u32[]{:S(2)}) collective-permute-start(bf16[128,768]{1,0:T(8,128)(2,1)S(1)} %get-tuple-element.48), channel_id=1, source_target_pairs={{0,8},{8,0},{1,9},{9,1},{2,10},{10,2},{3,11},{11,3},{4,12},{12,4},... | collective-permute-start | bytes 589832 | tf_op jit(solution)/shard_map/ppermute | solution.py:181
  61.0 5.3 %collective-permute-start.17 = (bf16[128,768]{1,0:T(8,128)(2,1)S(1)}, bf16[128,768]{1,0:T(8,128)(2,1)S(1)}, u32[]{:S(2)}, u32[]{:S(2)}) collective-permute-start(bf16[128,768]{1,0:T(8,128)(2,1)S(1)} %get-tuple-element.41), channel_id=1, source_target_pairs={{0,2},{2,4},{4,6},{6,0},{1,3},{3,5},{5,7},{7,1},{8,10},{10,12},{12... | collective-permute-start | bytes 589832 | tf_op jit(solution)/shard_map/ppermute | solution.py:181
  66.3 1.3 %collective-permute-done.16.z1_ref = bf16[128,768]{1,0:T(8,128)(2,1)S(1)} collective-permute-done((bf16[128,768]{1,0:T(8,128)(2,1)S(1)}, bf16[128,768]{1,0:T(8,128)(2,1)S(1)}, u32[]{:S(2)}, u32[]{:S(2)}) %collective-permute-start.16) | collective-permute-done | bytes 196640 | tf_op jit(solution)/shard_map/ppermute | solution.py:181
  67.6 2.0 %collective-permute-done.17.z2_ref = bf16[128,768]{1,0:T(8,128)(2,1)S(1)} collective-permute-done((bf16[128,768]{1,0:T(8,128)(2,1)S(1)}, bf16[128,768]{1,0:T(8,128)(2,1)S(1)}, u32[]{:S(2)}, u32[]{:S(2)}) %collective-permute-start.17) | collective-permute-done | bytes 196640 | tf_op jit(solution)/shard_map/ppermute | solution.py:181
  69.7 2.4 %collective-permute-done.18.z3_ref = bf16[128,768]{1,0:T(8,128)(2,1)S(1)} collective-permute-done((bf16[128,768]{1,0:T(8,128)(2,1)S(1)}, bf16[128,768]{1,0:T(8,128)(2,1)S(1)}, u32[]{:S(2)}, u32[]{:S(2)}) %collective-permute-start.18) | collective-permute-done | bytes 196640 | tf_op jit(solution)/shard_map/ppermute | solution.py:181
  (42 shorter events, 7.5 us)
Async XLA Ops:
  0.0 27.5 %collective-permute-start = (bf16[2,2,128,2048]{3,2,1,0:T(8,128)(2,1)}, bf16[2,2,128,2048]{3,2,1,0:T(8,128)(2,1)S(1)}, u32[]{:S(2)}, u32[]{:S(2)}) collective-permute-start(bf16[2,2,128,2048]{3,2,1,0:T(8,128)(2,1)} %own_ref.1), channel_id=1, source_target_pairs={{0,1},{1,0},{2,3},{3,2},{4,5},{5,4},{6,7},{7,6},{8,9},{9,8},{10,11... | collective-permute-start | bytes 6291464 | tf_op jit(solution)/shard_map/ppermute | solution.py:181
  0.0 9.5 %collective-permute-start.6 = (bf16[2,2,128,256]{3,2,1,0:T(8,128)(2,1)}, bf16[2,2,128,256]{3,2,1,0:T(8,128)(2,1)S(1)}, u32[]{:S(2)}, u32[]{:S(2)}) collective-permute-start(bf16[2,2,128,256]{3,2,1,0:T(8,128)(2,1)} %a_ref.1), channel_id=1, source_target_pairs={{0,8},{8,0},{1,9},{9,1},{2,10},{10,2},{3,11},{11,3},{4,12},{12,4},... | collective-permute-start | bytes 786440 | tf_op jit(solution)/shard_map/ppermute | solution.py:181
  3.0 1.9 %collective-permute-start.1 = (bf16[2,128,256]{2,1,0:T(8,128)(2,1)S(1)}, bf16[2,128,256]{2,1,0:T(8,128)(2,1)S(1)}, u32[]{:S(2)}, u32[]{:S(2)}) collective-permute-start(bf16[2,128,256]{2,1,0:T(8,128)(2,1)S(1)} %get-tuple-element.28), channel_id=1, source_target_pairs={{0,1},{1,0},{2,3},{3,2},{4,5},{5,4},{6,7},{7,6},{8,9},{9,8},{10,11... | collective-permute-start | bytes 393224 | tf_op jit(solution)/shard_map/ppermute | solution.py:181
  3.3 8.9 %collective-permute-start.4 = (bf16[2,2,128,256]{3,2,1,0:T(8,128)(2,1)}, bf16[2,2,128,256]{3,2,1,0:T(8,128)(2,1)S(1)}, u32[]{:S(2)}, u32[]{:S(2)}) collective-permute-start(bf16[2,2,128,256]{3,2,1,0:T(8,128)(2,1)} %a_ref.1), channel_id=1, source_target_pairs={{0,2},{1,7},{2,0},{3,5},{4,6},{5,3},{6,4},{7,1},{8,10},{9,15},{10,... | collective-permute-start | bytes 786440 | tf_op jit(solution)/shard_map/ppermute | solution.py:186
  4.9 22.6 %copy-start = (bf16[2,2,128,2048]{3,2,1,0:T(8,128)(2,1)S(1)}, bf16[2,2,128,2048]{3,2,1,0:T(8,128)(2,1)}, u32[]{:S(2)}) copy-start(bf16[2,2,128,2048]{3,2,1,0:T(8,128)(2,1)} %own_ref.1) | copy-start | bytes 6291460
  5.0 9.0 %collective-permute-start.2 = (bf16[2,128,512]{2,1,0:T(8,128)(2,1)S(1)}, bf16[2,128,512]{2,1,0:T(8,128)(2,1)S(1)}, u32[]{:S(2)}, u32[]{:S(2)}) collective-permute-start(bf16[2,128,512]{2,1,0:T(8,128)(2,1)S(1)} %shard_map.48.a_ref), channel_id=1, source_target_pairs={{0,32},{1,97},{32,0},{33,65},{64,96},{65,33},{96,64},{97,1},{2,34}... | collective-permute-start | bytes 786440 | tf_op jit(solution)/shard_map/ppermute | solution.py:186
  5.9 12.1 %collective-permute-start.8 = (bf16[2,128,512]{2,1,0:T(8,128)(2,1)S(1)}, bf16[2,128,512]{2,1,0:T(8,128)(2,1)S(1)}, u32[]{:S(2)}, u32[]{:S(2)}) collective-permute-start(bf16[2,128,512]{2,1,0:T(8,128)(2,1)S(1)} %shard_map.48.a_ref), channel_id=1, source_target_pairs={{0,16},{16,0},{1,17},{17,1},{2,18},{18,2},{3,19},{19,3},{4,20},{20... | collective-permute-start | bytes 786440 | tf_op jit(solution)/shard_map/ppermute | solution.py:181
  9.5 8.6 %collective-permute-start.7 = (bf16[2,2,128,256]{3,2,1,0:T(8,128)(2,1)S(1)}, bf16[2,2,128,256]{3,2,1,0:T(8,128)(2,1)S(1)}, u32[]{:S(2)}, u32[]{:S(2)}) collective-permute-start(bf16[2,2,128,256]{3,2,1,0:T(8,128)(2,1)S(1)} %collective-permute-done.6.a_ref), channel_id=1, source_target_pairs={{0,6},{1,3},{2,4},{3,1},{4,2},{5,7},{6,0},{7,5},{8,14},{9,11},{10,... | collective-permute-start | bytes 786440 | tf_op jit(solution)/shard_map/ppermute | solution.py:186
  13.2 16.0 %collective-permute-start.5 = (bf16[2,2,2,128,256]{4,3,2,1,0:T(8,128)(2,1)S(1)}, bf16[2,2,2,128,256]{4,3,2,1,0:T(8,128)(2,1)S(1)}, u32[]{:S(2)}, u32[]{:S(2)}) collective-permute-start(bf16[2,2,2,128,256]{4,3,2,1,0:T(8,128)(2,1)S(1)} %shard_map.50.refs_0_), channel_id=1, source_target_pairs={{0,6},{1,3},{2,4},{3,1},{4,2},{5,7},{6,0},{7,5},{8,14},{9,11},{10,... | collective-permute-start | bytes 1572872 | tf_op jit(solution)/shard_map/ppermute | solution.py:186
  14.1 15.1 %collective-permute-start.3 = (bf16[2,2,128,512]{3,2,1,0:T(8,128)(2,1)S(1)}, bf16[2,2,128,512]{3,2,1,0:T(8,128)(2,1)S(1)}, u32[]{:S(2)}, u32[]{:S(2)}) collective-permute-start(bf16[2,2,128,512]{3,2,1,0:T(8,128)(2,1)S(1)} %shard_map.49.r0), channel_id=1, source_target_pairs={{0,96},{1,33},{32,64},{33,1},{64,32},{65,97},{96,0},{97,65},{2,98}... | collective-permute-start | bytes 1572872 | tf_op jit(solution)/shard_map/ppermute | solution.py:186
  18.1 11.1 %collective-permute-start.9 = (bf16[2,2,2,128,256]{4,3,2,1,0:T(8,128)(2,1)S(1)}, bf16[2,2,2,128,256]{4,3,2,1,0:T(8,128)(2,1)S(1)}, u32[]{:S(2)}, u32[]{:S(2)}) collective-permute-start(bf16[2,2,2,128,256]{4,3,2,1,0:T(8,128)(2,1)S(1)} %shard_map.51.refs_2_), channel_id=1, source_target_pairs={{0,2},{1,7},{2,0},{3,5},{4,6},{5,3},{6,4},{7,1},{8,10},{9,15},{10,... | collective-permute-start | bytes 1572872 | tf_op jit(solution)/shard_map/ppermute | solution.py:186
  19.8 7.6 %collective-permute-start.11 = (bf16[2,128,512]{2,1,0:T(8,128)(2,1)S(1)}, bf16[2,128,512]{2,1,0:T(8,128)(2,1)S(1)}, u32[]{:S(2)}, u32[]{:S(2)}) collective-permute-start(bf16[2,128,512]{2,1,0:T(8,128)(2,1)S(1)} %collective-permute-done.8.a_ref), channel_id=1, source_target_pairs={{0,96},{1,33},{32,64},{33,1},{64,32},{65,97},{96,0},{97,65},{2,98}... | collective-permute-start | bytes 786440 | tf_op jit(solution)/shard_map/ppermute | solution.py:186
  27.4 9.3 %collective-permute-start.12 = (bf16[2,2,128,512]{3,2,1,0:T(8,128)(2,1)S(1)}, bf16[2,2,128,512]{3,2,1,0:T(8,128)(2,1)S(1)}, u32[]{:S(2)}, u32[]{:S(2)}) collective-permute-start(bf16[2,2,128,512]{3,2,1,0:T(8,128)(2,1)S(1)} %shard_map.53.r2), channel_id=1, source_target_pairs={{0,32},{1,97},{32,0},{33,65},{64,96},{65,33},{96,64},{97,1},{2,34}... | collective-permute-start | bytes 1572872 | tf_op jit(solution)/shard_map/ppermute | solution.py:186
  32.2 4.4 %collective-permute-start.13 = (bf16[2,2,128,256]{3,2,1,0:T(8,128)(2,1)S(1)}, bf16[2,2,128,256]{3,2,1,0:T(8,128)(2,1)S(1)}, u32[]{:S(2)}, u32[]{:S(2)}) collective-permute-start(bf16[2,2,128,256]{3,2,1,0:T(8,128)(2,1)S(1)} %get-tuple-element.34.m0_ref), channel_id=1, source_target_pairs={{0,1},{1,0},{2,3},{3,2},{4,5},{5,4},{6,7},{7,6},{8,9},{9,8},{10,11... | collective-permute-start | bytes 786440 | tf_op jit(solution)/shard_map/ppermute | solution.py:181
  32.3 4.4 %collective-permute-start.14 = (bf16[2,2,128,256]{3,2,1,0:T(8,128)(2,1)S(1)}, bf16[2,2,128,256]{3,2,1,0:T(8,128)(2,1)S(1)}, u32[]{:S(2)}, u32[]{:S(2)}) collective-permute-start(bf16[2,2,128,256]{3,2,1,0:T(8,128)(2,1)S(1)} %get-tuple-element.35.m1_ref), channel_id=1, source_target_pairs={{0,1},{1,0},{2,3},{3,2},{4,5},{5,4},{6,7},{7,6},{8,9},{9,8},{10,11... | collective-permute-start | bytes 786440 | tf_op jit(solution)/shard_map/ppermute | solution.py:181
  32.8 5.2 %collective-permute-start.10 = (bf16[2,2,128,256]{3,2,1,0:T(8,128)(2,1)S(1)}, bf16[2,2,128,256]{3,2,1,0:T(8,128)(2,1)S(1)}, u32[]{:S(2)}, u32[]{:S(2)}) collective-permute-start(bf16[2,2,128,256]{3,2,1,0:T(8,128)(2,1)S(1)} %get-tuple-element.31.mine_ref), channel_id=1, source_target_pairs={{0,1},{1,0},{2,3},{3,2},{4,5},{5,4},{6,7},{7,6},{8,9},{9,8},{10,11... | collective-permute-start | bytes 786440 | tf_op jit(solution)/shard_map/ppermute | solution.py:181
  38.7 18.4 %collective-permute-start.15 = (bf16[4,128,768]{2,1,0:T(8,128)(2,1)S(1)}, bf16[4,128,768]{2,1,0:T(8,128)(2,1)S(1)}, u32[]{:S(2)}, u32[]{:S(2)}) collective-permute-start(bf16[4,128,768]{2,1,0:T(8,128)(2,1)S(1)} %get-tuple-element.38), channel_id=1, source_target_pairs={{0,8},{8,0},{1,9},{9,1},{2,10},{10,2},{3,11},{11,3},{4,12},{12,4},... | collective-permute-start | bytes 2359304 | tf_op jit(solution)/shard_map/ppermute | solution.py:181
  40.0 17.4 %collective-permute-start.19 = (bf16[2,128,768]{2,1,0:T(8,128)(2,1)S(1)}, bf16[2,128,768]{2,1,0:T(8,128)(2,1)S(1)}, u32[]{:S(2)}, u32[]{:S(2)}) collective-permute-start(bf16[2,128,768]{2,1,0:T(8,128)(2,1)S(1)} %get-tuple-element.44), channel_id=1, source_target_pairs={{0,2},{2,4},{4,6},{6,0},{1,3},{3,5},{5,7},{7,1},{8,10},{10,12},{12... | collective-permute-start | bytes 1179656 | tf_op jit(solution)/shard_map/ppermute | solution.py:181
  40.3 17.4 %collective-permute-start.20 = (bf16[2,128,768]{2,1,0:T(8,128)(2,1)S(1)}, bf16[2,128,768]{2,1,0:T(8,128)(2,1)S(1)}, u32[]{:S(2)}, u32[]{:S(2)}) collective-permute-start(bf16[2,128,768]{2,1,0:T(8,128)(2,1)S(1)} %get-tuple-element.45), channel_id=1, source_target_pairs={{0,6},{2,0},{4,2},{6,4},{1,7},{3,1},{5,3},{7,5},{8,14},{10,8},{12,... | collective-permute-start | bytes 1179656 | tf_op jit(solution)/shard_map/ppermute | solution.py:181
  43.2 16.0 %collective-permute-start.21 = (bf16[2,128,768]{2,1,0:T(8,128)(2,1)S(1)}, bf16[2,128,768]{2,1,0:T(8,128)(2,1)S(1)}, u32[]{:S(2)}, u32[]{:S(2)}) collective-permute-start(bf16[2,128,768]{2,1,0:T(8,128)(2,1)S(1)} %get-tuple-element.46), channel_id=1, source_target_pairs={{0,4},{2,6},{4,0},{6,2},{1,5},{3,7},{5,1},{7,3},{8,12},{10,14},{12... | collective-permute-start | bytes 1179656 | tf_op jit(solution)/shard_map/ppermute | solution.py:181
  59.5 6.9 %collective-permute-start.22 = (bf16[128,768]{1,0:T(8,128)(2,1)S(1)}, bf16[128,768]{1,0:T(8,128)(2,1)S(1)}, u32[]{:S(2)}, u32[]{:S(2)}) collective-permute-start(bf16[128,768]{1,0:T(8,128)(2,1)S(1)} %get-tuple-element.48), channel_id=1, source_target_pairs={{0,8},{8,0},{1,9},{9,1},{2,10},{10,2},{3,11},{11,3},{4,12},{12,4},... | collective-permute-start | bytes 589832 | tf_op jit(solution)/shard_map/ppermute | solution.py:181
  60.4 7.2 %collective-permute-start.16 = (bf16[128,768]{1,0:T(8,128)(2,1)S(1)}, bf16[128,768]{1,0:T(8,128)(2,1)S(1)}, u32[]{:S(2)}, u32[]{:S(2)}) collective-permute-start(bf16[128,768]{1,0:T(8,128)(2,1)S(1)} %get-tuple-element.40), channel_id=1, source_target_pairs={{0,4},{2,6},{4,0},{6,2},{1,5},{3,7},{5,1},{7,3},{8,12},{10,14},{12... | collective-permute-start | bytes 589832 | tf_op jit(solution)/shard_map/ppermute | solution.py:181
  61.0 8.7 %collective-permute-start.17 = (bf16[128,768]{1,0:T(8,128)(2,1)S(1)}, bf16[128,768]{1,0:T(8,128)(2,1)S(1)}, u32[]{:S(2)}, u32[]{:S(2)}) collective-permute-start(bf16[128,768]{1,0:T(8,128)(2,1)S(1)} %get-tuple-element.41), channel_id=1, source_target_pairs={{0,2},{2,4},{4,6},{6,0},{1,3},{3,5},{5,7},{7,1},{8,10},{10,12},{12... | collective-permute-start | bytes 589832 | tf_op jit(solution)/shard_map/ppermute | solution.py:181
  66.3 5.8 %collective-permute-start.18 = (bf16[128,768]{1,0:T(8,128)(2,1)S(1)}, bf16[128,768]{1,0:T(8,128)(2,1)S(1)}, u32[]{:S(2)}, u32[]{:S(2)}) collective-permute-start(bf16[128,768]{1,0:T(8,128)(2,1)S(1)} %get-tuple-element.42), channel_id=1, source_target_pairs={{0,6},{2,0},{4,2},{6,4},{1,7},{3,1},{5,3},{7,5},{8,14},{10,8},{12,... | collective-permute-start | bytes 589832 | tf_op jit(solution)/shard_map/ppermute | solution.py:181
  (2 other events, 45.1 us)

commit v6 on v5

--- a/solution.py
+++ b/solution.py
@@ -96,12 +96,11 @@
 def screen(w_ref, *refs):
     pieces, outs, (acc, held, sems) = refs[:4], refs[4:7], refs[7:]
     copies = copy_all([(ref, held.at[i]) for i, ref in enumerate(pieces)], sems)
-    for i in range(8):
-        if i % 2 == 0:
-            copies[i // 2].wait()
-        cols = slice(i * 256, (i + 1) * 256)
+    for i in range(4):
+        copies[i].wait()
+        cols = slice(i * 512, (i + 1) * 512)
         for p, (k, kp) in enumerate(PAIRS):
-            rhs = held[i // 2, i % 2, kp].reshape(256, 256)
+            rhs = held[i, :, kp].reshape(512, 256)
             term = jnp.dot(w_ref[kp - k, :, cols], rhs, preferred_element_type=F32)
             if i == 0:
                 acc[p] = term

time: 73.9 us -> 73.9 us (level)
  no operation moved by 1% of the time
where the time goes in v6:
time: 73.9 us; the launch traced here: 73.6 us
  waiting for transfers between devices  34.1 us (46%)
  starting transfers between devices  28.4 us (38%)
  Pallas kernels  10 us (14%)
  local copies, waits for them, and re-layouts  0.86 us (1%)
    ppermute x15, waiting for transfers between devices, shift(): return lax.ppermute(x, axis, [(i, (i + step) % size) for i in range(size)])  23.3 us
    ppermute x15, starting transfers between devices, shift(): return lax.ppermute(x, axis, [(i, (i + step) % size) for i in range(size)])  19.1 us
    ppermute x8, waiting for transfers between devices, ring_swap(): return lax.ppermute(x, (axis, 'c'), pairs)  10.9 us
    pallas_call x13, Pallas kernels, call(): pl.pallas_call(body, out_shape=[jax.ShapeDtypeStruct(s, BF) for s in outs...  10 us
    ppermute x8, starting transfers between devices, ring_swap(): return lax.ppermute(x, (axis, 'c'), pairs)  9.24 us
  transfers between devices with their start and end apart: 23, of which 9 were waited for; matrix products, arithmetic and copies ran while one was open for 0% of the time, Pallas kernels for 11%

profile of v6, /device:TPU:6, one launch (start us, length us, event | category | flops | bytes accessed | tf_op | source)
XLA Modules:
  0.0 73.6 jit_solution(246526400645980983)
XLA Ops:
  0.0 1.9 %collective-permute-start.6 = (bf16[2,2,128,256]{3,2,1,0:T(8,128)(2,1)}, bf16[2,2,128,256]{3,2,1,0:T(8,128)(2,1)S(1)}, u32[]{:S(2)}, u32[]{:S(2)}) collective-permute-start(bf16[2,2,128,256]{3,2,1,0:T(8,128)(2,1)} %a_ref.1), channel_id=1, source_target_pairs={{0,8},{8,0},{1,9},{9,1},{2,10},{10,2},{3,11},{11,3},{4,12},{12,4},... | collective-permute-start | bytes 786440 | tf_op jit(solution)/shard_map/ppermute | solution.py:180
  1.9 1.1 %shard_map.47 = (bf16[2,128,256]{2,1,0:T(8,128)(2,1)S(1)}, bf16[2,128,256]{2,1,0:T(8,128)(2,1)S(1)}) custom-call(bf16[2,2,128,256]{3,2,1,0:T(8,128)(2,1)} %a_ref.1), custom_call_target="tpu_custom_call" | custom-call | tf_op jit(solution)/shard_map/pallas_call | solution.py:24
  3.3 1.6 %collective-permute-start.4 = (bf16[2,2,128,256]{3,2,1,0:T(8,128)(2,1)}, bf16[2,2,128,256]{3,2,1,0:T(8,128)(2,1)S(1)}, u32[]{:S(2)}, u32[]{:S(2)}) collective-permute-start(bf16[2,2,128,256]{3,2,1,0:T(8,128)(2,1)} %a_ref.1), channel_id=1, source_target_pairs={{0,2},{1,7},{2,0},{3,5},{4,6},{5,3},{6,4},{7,1},{8,10},{9,15},{10,... | collective-permute-start | bytes 786440 | tf_op jit(solution)/shard_map/ppermute | solution.py:185
  5.9 3.6 %collective-permute-start.8 = (bf16[2,128,512]{2,1,0:T(8,128)(2,1)S(1)}, bf16[2,128,512]{2,1,0:T(8,128)(2,1)S(1)}, u32[]{:S(2)}, u32[]{:S(2)}) collective-permute-start(bf16[2,128,512]{2,1,0:T(8,128)(2,1)S(1)} %shard_map.48.a_ref), channel_id=1, source_target_pairs={{0,16},{16,0},{1,17},{17,1},{2,18},{18,2},{3,19},{19,3},{4,20},{20... | collective-permute-start | bytes 786440 | tf_op jit(solution)/shard_map/ppermute | solution.py:180
  9.5 2.7 %collective-permute-start.7 = (bf16[2,2,128,256]{3,2,1,0:T(8,128)(2,1)S(1)}, bf16[2,2,128,256]{3,2,1,0:T(8,128)(2,1)S(1)}, u32[]{:S(2)}, u32[]{:S(2)}) collective-permute-start(bf16[2,2,128,256]{3,2,1,0:T(8,128)(2,1)S(1)} %collective-permute-done.6.a_ref), channel_id=1, source_target_pairs={{0,6},{1,3},{2,4},{3,1},{4,2},{5,7},{6,0},{7,5},{8,14},{9,11},{10,... | collective-permute-start | bytes 786440 | tf_op jit(solution)/shard_map/ppermute | solution.py:185
  12.2 1.0 %shard_map.50.refs_0_ = bf16[2,2,2,128,256]{4,3,2,1,0:T(8,128)(2,1)S(1)} custom-call(bf16[2,2,128,256]{3,2,1,0:T(8,128)(2,1)} %a_ref.1, bf16[2,2,128,256]{3,2,1,0:T(8,128)(2,1)S(1)} %collective-permute-done.4.b_ref), custom_call_target="tpu_custom_call" | custom-call | tf_op jit(solution)/shard_map/pallas_call | solution.py:24
  14.1 1.0 %collective-permute-start.3 = (bf16[2,2,128,512]{3,2,1,0:T(8,128)(2,1)S(1)}, bf16[2,2,128,512]{3,2,1,0:T(8,128)(2,1)S(1)}, u32[]{:S(2)}, u32[]{:S(2)}) collective-permute-start(bf16[2,2,128,512]{3,2,1,0:T(8,128)(2,1)S(1)} %shard_map.49.r0), channel_id=1, source_target_pairs={{0,96},{1,33},{32,64},{33,1},{64,32},{65,97},{96,0},{97,65},{2,98}... | collective-permute-start | bytes 1572872 | tf_op jit(solution)/shard_map/ppermute | solution.py:185
  15.1 3.0 %collective-permute-done.8.a_ref = bf16[2,128,512]{2,1,0:T(8,128)(2,1)S(1)} collective-permute-done((bf16[2,128,512]{2,1,0:T(8,128)(2,1)S(1)}, bf16[2,128,512]{2,1,0:T(8,128)(2,1)S(1)}, u32[]{:S(2)}, u32[]{:S(2)}) %collective-permute-start.8) | collective-permute-done | bytes 262176 | tf_op jit(solution)/shard_map/ppermute | solution.py:180
  18.1 1.7 %collective-permute-start.9 = (bf16[2,2,2,128,256]{4,3,2,1,0:T(8,128)(2,1)S(1)}, bf16[2,2,2,128,256]{4,3,2,1,0:T(8,128)(2,1)S(1)}, u32[]{:S(2)}, u32[]{:S(2)}) collective-permute-start(bf16[2,2,2,128,256]{4,3,2,1,0:T(8,128)(2,1)S(1)} %shard_map.51.refs_2_), channel_id=1, source_target_pairs={{0,2},{1,7},{2,0},{3,5},{4,6},{5,3},{6,4},{7,1},{8,10},{9,15},{10,... | collective-permute-start | bytes 1572872 | tf_op jit(solution)/shard_map/ppermute | solution.py:185
  20.2 7.1 %collective-permute-done.11.b_ref = bf16[2,128,512]{2,1,0:T(8,128)(2,1)S(1)} collective-permute-done((bf16[2,128,512]{2,1,0:T(8,128)(2,1)S(1)}, bf16[2,128,512]{2,1,0:T(8,128)(2,1)S(1)}, u32[]{:S(2)}, u32[]{:S(2)}) %collective-permute-start.11) | collective-permute-done | bytes 262176 | tf_op jit(solution)/shard_map/ppermute | solution.py:185
  27.5 1.6 %shard_map.46.w_ref = bf16[2,512,2048]{2,1,0:T(8,128)(2,1)S(1)} custom-call(s32[2,3]{1,0:T(2,128)S(1)} %bitcast.1, s32[3]{0:T(128)S(1)} %copy-done.2, bf16[2,2,128,2048]{3,2,1,0:T(8,128)(2,1)S(1)} %copy-done, bf16[2,2,128,2048]{3,2,1,0:T(8,128)(2,1)S(1)} %collective-permute-done.mate_ref), custom_call_target="tpu_custom_call" | custom-call | tf_op jit(solution)/shard_map/pallas_call | solution.py:24
  29.2 3.0 %shard_map.52 = (bf16[2,2,128,256]{3,2,1,0:T(8,128)(2,1)S(1)}, bf16[2,2,128,256]{3,2,1,0:T(8,128)(2,1)S(1)}, bf16[2,2,128,256]{3,2,1,0:T(8,128)(2,1)S(1)}) custom-call(bf16[2,512,2048]{2,1,0:T(8,128)(2,1)S(1)} %shard_map.46.w_ref, bf16[2,2,2,128,256]{4,3,2,1,0:T(8,128)(2,1)S(1)} %shard_map.50.refs_0_, ...), custom_call_target="tpu_custom_call" | custom-call | tf_op jit(solution)/shard_map/pallas_call | solution.py:24
  32.9 3.8 %collective-permute-done.12.r3 = bf16[2,2,128,512]{3,2,1,0:T(8,128)(2,1)S(1)} collective-permute-done((bf16[2,2,128,512]{3,2,1,0:T(8,128)(2,1)S(1)}, bf16[2,2,128,512]{3,2,1,0:T(8,128)(2,1)S(1)}, u32[]{:S(2)}, u32[]{:S(2)}) %collective-permute-start.12) | collective-permute-done | bytes 524320 | tf_op jit(solution)/shard_map/ppermute | solution.py:185
  36.7 1.3 %shard_map.54 = (bf16[2,128,768]{2,1,0:T(8,128)(2,1)S(1)}, bf16[2,128,768]{2,1,0:T(8,128)(2,1)S(1)}, bf16[2,128,768]{2,1,0:T(8,128)(2,1)S(1)}, bf16[2,128,768]{2...) custom-call(bf16[2,2,128,256]{3,2,1,0:T(8,128)(2,1)S(1)} %get-tuple-element.34.m0_ref, ...), custom_call_target="tpu_custom_call" | custom-call | tf_op jit(solution)/shard_map/pallas_call | solution.py:24
  38.7 1.2 %collective-permute-start.15 = (bf16[4,128,768]{2,1,0:T(8,128)(2,1)S(1)}, bf16[4,128,768]{2,1,0:T(8,128)(2,1)S(1)}, u32[]{:S(2)}, u32[]{:S(2)}) collective-permute-start(bf16[4,128,768]{2,1,0:T(8,128)(2,1)S(1)} %get-tuple-element.38), channel_id=1, source_target_pairs={{0,8},{8,0},{1,9},{9,1},{2,10},{10,2},{3,11},{11,3},{4,12},{12,4},... | collective-permute-start | bytes 2359304 | tf_op jit(solution)/shard_map/ppermute | solution.py:180
  40.3 2.9 %collective-permute-start.20 = (bf16[2,128,768]{2,1,0:T(8,128)(2,1)S(1)}, bf16[2,128,768]{2,1,0:T(8,128)(2,1)S(1)}, u32[]{:S(2)}, u32[]{:S(2)}) collective-permute-start(bf16[2,128,768]{2,1,0:T(8,128)(2,1)S(1)} %get-tuple-element.45), channel_id=1, source_target_pairs={{0,6},{2,0},{4,2},{6,4},{1,7},{3,1},{5,3},{7,5},{8,14},{10,8},{12,... | collective-permute-start | bytes 1179656 | tf_op jit(solution)/shard_map/ppermute | solution.py:180
  43.2 1.3 %collective-permute-start.21 = (bf16[2,128,768]{2,1,0:T(8,128)(2,1)S(1)}, bf16[2,128,768]{2,1,0:T(8,128)(2,1)S(1)}, u32[]{:S(2)}, u32[]{:S(2)}) collective-permute-start(bf16[2,128,768]{2,1,0:T(8,128)(2,1)S(1)} %get-tuple-element.46), channel_id=1, source_target_pairs={{0,4},{2,6},{4,0},{6,2},{1,5},{3,7},{5,1},{7,3},{8,12},{10,14},{12... | collective-permute-start | bytes 1179656 | tf_op jit(solution)/shard_map/ppermute | solution.py:180
  44.5 12.6 %collective-permute-done.15.got_ref = bf16[4,128,768]{2,1,0:T(8,128)(2,1)S(1)} collective-permute-done((bf16[4,128,768]{2,1,0:T(8,128)(2,1)S(1)}, bf16[4,128,768]{2,1,0:T(8,128)(2,1)S(1)}, u32[]{:S(2)}, u32[]{:S(2)}) %collective-permute-start.15) | collective-permute-done | bytes 786464 | tf_op jit(solution)/shard_map/ppermute | solution.py:180
  57.7 1.5 %collective-permute-done.21.g3_ref = bf16[2,128,768]{2,1,0:T(8,128)(2,1)S(1)} collective-permute-done((bf16[2,128,768]{2,1,0:T(8,128)(2,1)S(1)}, bf16[2,128,768]{2,1,0:T(8,128)(2,1)S(1)}, u32[]{:S(2)}, u32[]{:S(2)}) %collective-permute-start.21) | collective-permute-done | bytes 393248 | tf_op jit(solution)/shard_map/ppermute | solution.py:180
  59.5 0.9 %collective-permute-start.22 = (bf16[128,768]{1,0:T(8,128)(2,1)S(1)}, bf16[128,768]{1,0:T(8,128)(2,1)S(1)}, u32[]{:S(2)}, u32[]{:S(2)}) collective-permute-start(bf16[128,768]{1,0:T(8,128)(2,1)S(1)} %get-tuple-element.48), channel_id=1, source_target_pairs={{0,8},{8,0},{1,9},{9,1},{2,10},{10,2},{3,11},{11,3},{4,12},{12,4},... | collective-permute-start | bytes 589832 | tf_op jit(solution)/shard_map/ppermute | solution.py:180
  61.0 5.3 %collective-permute-start.17 = (bf16[128,768]{1,0:T(8,128)(2,1)S(1)}, bf16[128,768]{1,0:T(8,128)(2,1)S(1)}, u32[]{:S(2)}, u32[]{:S(2)}) collective-permute-start(bf16[128,768]{1,0:T(8,128)(2,1)S(1)} %get-tuple-element.41), channel_id=1, source_target_pairs={{0,2},{2,4},{4,6},{6,0},{1,3},{3,5},{5,7},{7,1},{8,10},{10,12},{12... | collective-permute-start | bytes 589832 | tf_op jit(solution)/shard_map/ppermute | solution.py:180
  66.3 1.3 %collective-permute-done.16.z1_ref = bf16[128,768]{1,0:T(8,128)(2,1)S(1)} collective-permute-done((bf16[128,768]{1,0:T(8,128)(2,1)S(1)}, bf16[128,768]{1,0:T(8,128)(2,1)S(1)}, u32[]{:S(2)}, u32[]{:S(2)}) %collective-permute-start.16) | collective-permute-done | bytes 196640 | tf_op jit(solution)/shard_map/ppermute | solution.py:180
  67.6 2.0 %collective-permute-done.17.z2_ref = bf16[128,768]{1,0:T(8,128)(2,1)S(1)} collective-permute-done((bf16[128,768]{1,0:T(8,128)(2,1)S(1)}, bf16[128,768]{1,0:T(8,128)(2,1)S(1)}, u32[]{:S(2)}, u32[]{:S(2)}) %collective-permute-start.17) | collective-permute-done | bytes 196640 | tf_op jit(solution)/shard_map/ppermute | solution.py:180
  69.7 2.4 %collective-permute-done.18.z3_ref = bf16[128,768]{1,0:T(8,128)(2,1)S(1)} collective-permute-done((bf16[128,768]{1,0:T(8,128)(2,1)S(1)}, bf16[128,768]{1,0:T(8,128)(2,1)S(1)}, u32[]{:S(2)}, u32[]{:S(2)}) %collective-permute-start.18) | collective-permute-done | bytes 196640 | tf_op jit(solution)/shard_map/ppermute | solution.py:180
  (42 shorter events, 7.5 us)
Async XLA Ops:
  0.0 27.5 %collective-permute-start = (bf16[2,2,128,2048]{3,2,1,0:T(8,128)(2,1)}, bf16[2,2,128,2048]{3,2,1,0:T(8,128)(2,1)S(1)}, u32[]{:S(2)}, u32[]{:S(2)}) collective-permute-start(bf16[2,2,128,2048]{3,2,1,0:T(8,128)(2,1)} %own_ref.1), channel_id=1, source_target_pairs={{0,1},{1,0},{2,3},{3,2},{4,5},{5,4},{6,7},{7,6},{8,9},{9,8},{10,11... | collective-permute-start | bytes 6291464 | tf_op jit(solution)/shard_map/ppermute | solution.py:180
  0.0 9.5 %collective-permute-start.6 = (bf16[2,2,128,256]{3,2,1,0:T(8,128)(2,1)}, bf16[2,2,128,256]{3,2,1,0:T(8,128)(2,1)S(1)}, u32[]{:S(2)}, u32[]{:S(2)}) collective-permute-start(bf16[2,2,128,256]{3,2,1,0:T(8,128)(2,1)} %a_ref.1), channel_id=1, source_target_pairs={{0,8},{8,0},{1,9},{9,1},{2,10},{10,2},{3,11},{11,3},{4,12},{12,4},... | collective-permute-start | bytes 786440 | tf_op jit(solution)/shard_map/ppermute | solution.py:180
  3.0 1.9 %collective-permute-start.1 = (bf16[2,128,256]{2,1,0:T(8,128)(2,1)S(1)}, bf16[2,128,256]{2,1,0:T(8,128)(2,1)S(1)}, u32[]{:S(2)}, u32[]{:S(2)}) collective-permute-start(bf16[2,128,256]{2,1,0:T(8,128)(2,1)S(1)} %get-tuple-element.28), channel_id=1, source_target_pairs={{0,1},{1,0},{2,3},{3,2},{4,5},{5,4},{6,7},{7,6},{8,9},{9,8},{10,11... | collective-permute-start | bytes 393224 | tf_op jit(solution)/shard_map/ppermute | solution.py:180
  3.3 8.9 %collective-permute-start.4 = (bf16[2,2,128,256]{3,2,1,0:T(8,128)(2,1)}, bf16[2,2,128,256]{3,2,1,0:T(8,128)(2,1)S(1)}, u32[]{:S(2)}, u32[]{:S(2)}) collective-permute-start(bf16[2,2,128,256]{3,2,1,0:T(8,128)(2,1)} %a_ref.1), channel_id=1, source_target_pairs={{0,2},{1,7},{2,0},{3,5},{4,6},{5,3},{6,4},{7,1},{8,10},{9,15},{10,... | collective-permute-start | bytes 786440 | tf_op jit(solution)/shard_map/ppermute | solution.py:185
  4.9 22.6 %copy-start = (bf16[2,2,128,2048]{3,2,1,0:T(8,128)(2,1)S(1)}, bf16[2,2,128,2048]{3,2,1,0:T(8,128)(2,1)}, u32[]{:S(2)}) copy-start(bf16[2,2,128,2048]{3,2,1,0:T(8,128)(2,1)} %own_ref.1) | copy-start | bytes 6291460
  5.0 9.0 %collective-permute-start.2 = (bf16[2,128,512]{2,1,0:T(8,128)(2,1)S(1)}, bf16[2,128,512]{2,1,0:T(8,128)(2,1)S(1)}, u32[]{:S(2)}, u32[]{:S(2)}) collective-permute-start(bf16[2,128,512]{2,1,0:T(8,128)(2,1)S(1)} %shard_map.48.a_ref), channel_id=1, source_target_pairs={{0,32},{1,97},{32,0},{33,65},{64,96},{65,33},{96,64},{97,1},{2,34}... | collective-permute-start | bytes 786440 | tf_op jit(solution)/shard_map/ppermute | solution.py:185
  5.9 12.1 %collective-permute-start.8 = (bf16[2,128,512]{2,1,0:T(8,128)(2,1)S(1)}, bf16[2,128,512]{2,1,0:T(8,128)(2,1)S(1)}, u32[]{:S(2)}, u32[]{:S(2)}) collective-permute-start(bf16[2,128,512]{2,1,0:T(8,128)(2,1)S(1)} %shard_map.48.a_ref), channel_id=1, source_target_pairs={{0,16},{16,0},{1,17},{17,1},{2,18},{18,2},{3,19},{19,3},{4,20},{20... | collective-permute-start | bytes 786440 | tf_op jit(solution)/shard_map/ppermute | solution.py:180
  9.5 8.6 %collective-permute-start.7 = (bf16[2,2,128,256]{3,2,1,0:T(8,128)(2,1)S(1)}, bf16[2,2,128,256]{3,2,1,0:T(8,128)(2,1)S(1)}, u32[]{:S(2)}, u32[]{:S(2)}) collective-permute-start(bf16[2,2,128,256]{3,2,1,0:T(8,128)(2,1)S(1)} %collective-permute-done.6.a_ref), channel_id=1, source_target_pairs={{0,6},{1,3},{2,4},{3,1},{4,2},{5,7},{6,0},{7,5},{8,14},{9,11},{10,... | collective-permute-start | bytes 786440 | tf_op jit(solution)/shard_map/ppermute | solution.py:185
  13.2 16.0 %collective-permute-start.5 = (bf16[2,2,2,128,256]{4,3,2,1,0:T(8,128)(2,1)S(1)}, bf16[2,2,2,128,256]{4,3,2,1,0:T(8,128)(2,1)S(1)}, u32[]{:S(2)}, u32[]{:S(2)}) collective-permute-start(bf16[2,2,2,128,256]{4,3,2,1,0:T(8,128)(2,1)S(1)} %shard_map.50.refs_0_), channel_id=1, source_target_pairs={{0,6},{1,3},{2,4},{3,1},{4,2},{5,7},{6,0},{7,5},{8,14},{9,11},{10,... | collective-permute-start | bytes 1572872 | tf_op jit(solution)/shard_map/ppermute | solution.py:185
  14.1 15.1 %collective-permute-start.3 = (bf16[2,2,128,512]{3,2,1,0:T(8,128)(2,1)S(1)}, bf16[2,2,128,512]{3,2,1,0:T(8,128)(2,1)S(1)}, u32[]{:S(2)}, u32[]{:S(2)}) collective-permute-start(bf16[2,2,128,512]{3,2,1,0:T(8,128)(2,1)S(1)} %shard_map.49.r0), channel_id=1, source_target_pairs={{0,96},{1,33},{32,64},{33,1},{64,32},{65,97},{96,0},{97,65},{2,98}... | collective-permute-start | bytes 1572872 | tf_op jit(solution)/shard_map/ppermute | solution.py:185
  18.1 11.1 %collective-permute-start.9 = (bf16[2,2,2,128,256]{4,3,2,1,0:T(8,128)(2,1)S(1)}, bf16[2,2,2,128,256]{4,3,2,1,0:T(8,128)(2,1)S(1)}, u32[]{:S(2)}, u32[]{:S(2)}) collective-permute-start(bf16[2,2,2,128,256]{4,3,2,1,0:T(8,128)(2,1)S(1)} %shard_map.51.refs_2_), channel_id=1, source_target_pairs={{0,2},{1,7},{2,0},{3,5},{4,6},{5,3},{6,4},{7,1},{8,10},{9,15},{10,... | collective-permute-start | bytes 1572872 | tf_op jit(solution)/shard_map/ppermute | solution.py:185
  19.8 7.6 %collective-permute-start.11 = (bf16[2,128,512]{2,1,0:T(8,128)(2,1)S(1)}, bf16[2,128,512]{2,1,0:T(8,128)(2,1)S(1)}, u32[]{:S(2)}, u32[]{:S(2)}) collective-permute-start(bf16[2,128,512]{2,1,0:T(8,128)(2,1)S(1)} %collective-permute-done.8.a_ref), channel_id=1, source_target_pairs={{0,96},{1,33},{32,64},{33,1},{64,32},{65,97},{96,0},{97,65},{2,98}... | collective-permute-start | bytes 786440 | tf_op jit(solution)/shard_map/ppermute | solution.py:185
  27.4 9.3 %collective-permute-start.12 = (bf16[2,2,128,512]{3,2,1,0:T(8,128)(2,1)S(1)}, bf16[2,2,128,512]{3,2,1,0:T(8,128)(2,1)S(1)}, u32[]{:S(2)}, u32[]{:S(2)}) collective-permute-start(bf16[2,2,128,512]{3,2,1,0:T(8,128)(2,1)S(1)} %shard_map.53.r2), channel_id=1, source_target_pairs={{0,32},{1,97},{32,0},{33,65},{64,96},{65,33},{96,64},{97,1},{2,34}... | collective-permute-start | bytes 1572872 | tf_op jit(solution)/shard_map/ppermute | solution.py:185
  32.2 4.5 %collective-permute-start.13 = (bf16[2,2,128,256]{3,2,1,0:T(8,128)(2,1)S(1)}, bf16[2,2,128,256]{3,2,1,0:T(8,128)(2,1)S(1)}, u32[]{:S(2)}, u32[]{:S(2)}) collective-permute-start(bf16[2,2,128,256]{3,2,1,0:T(8,128)(2,1)S(1)} %get-tuple-element.34.m0_ref), channel_id=1, source_target_pairs={{0,1},{1,0},{2,3},{3,2},{4,5},{5,4},{6,7},{7,6},{8,9},{9,8},{10,11... | collective-permute-start | bytes 786440 | tf_op jit(solution)/shard_map/ppermute | solution.py:180
  32.3 4.4 %collective-permute-start.14 = (bf16[2,2,128,256]{3,2,1,0:T(8,128)(2,1)S(1)}, bf16[2,2,128,256]{3,2,1,0:T(8,128)(2,1)S(1)}, u32[]{:S(2)}, u32[]{:S(2)}) collective-permute-start(bf16[2,2,128,256]{3,2,1,0:T(8,128)(2,1)S(1)} %get-tuple-element.35.m1_ref), channel_id=1, source_target_pairs={{0,1},{1,0},{2,3},{3,2},{4,5},{5,4},{6,7},{7,6},{8,9},{9,8},{10,11... | collective-permute-start | bytes 786440 | tf_op jit(solution)/shard_map/ppermute | solution.py:180
  32.8 5.2 %collective-permute-start.10 = (bf16[2,2,128,256]{3,2,1,0:T(8,128)(2,1)S(1)}, bf16[2,2,128,256]{3,2,1,0:T(8,128)(2,1)S(1)}, u32[]{:S(2)}, u32[]{:S(2)}) collective-permute-start(bf16[2,2,128,256]{3,2,1,0:T(8,128)(2,1)S(1)} %get-tuple-element.31.mine_ref), channel_id=1, source_target_pairs={{0,1},{1,0},{2,3},{3,2},{4,5},{5,4},{6,7},{7,6},{8,9},{9,8},{10,11... | collective-permute-start | bytes 786440 | tf_op jit(solution)/shard_map/ppermute | solution.py:180
  38.7 18.4 %collective-permute-start.15 = (bf16[4,128,768]{2,1,0:T(8,128)(2,1)S(1)}, bf16[4,128,768]{2,1,0:T(8,128)(2,1)S(1)}, u32[]{:S(2)}, u32[]{:S(2)}) collective-permute-start(bf16[4,128,768]{2,1,0:T(8,128)(2,1)S(1)} %get-tuple-element.38), channel_id=1, source_target_pairs={{0,8},{8,0},{1,9},{9,1},{2,10},{10,2},{3,11},{11,3},{4,12},{12,4},... | collective-permute-start | bytes 2359304 | tf_op jit(solution)/shard_map/ppermute | solution.py:180
  40.0 17.4 %collective-permute-start.19 = (bf16[2,128,768]{2,1,0:T(8,128)(2,1)S(1)}, bf16[2,128,768]{2,1,0:T(8,128)(2,1)S(1)}, u32[]{:S(2)}, u32[]{:S(2)}) collective-permute-start(bf16[2,128,768]{2,1,0:T(8,128)(2,1)S(1)} %get-tuple-element.44), channel_id=1, source_target_pairs={{0,2},{2,4},{4,6},{6,0},{1,3},{3,5},{5,7},{7,1},{8,10},{10,12},{12... | collective-permute-start | bytes 1179656 | tf_op jit(solution)/shard_map/ppermute | solution.py:180
  40.3 17.4 %collective-permute-start.20 = (bf16[2,128,768]{2,1,0:T(8,128)(2,1)S(1)}, bf16[2,128,768]{2,1,0:T(8,128)(2,1)S(1)}, u32[]{:S(2)}, u32[]{:S(2)}) collective-permute-start(bf16[2,128,768]{2,1,0:T(8,128)(2,1)S(1)} %get-tuple-element.45), channel_id=1, source_target_pairs={{0,6},{2,0},{4,2},{6,4},{1,7},{3,1},{5,3},{7,5},{8,14},{10,8},{12,... | collective-permute-start | bytes 1179656 | tf_op jit(solution)/shard_map/ppermute | solution.py:180
  43.2 16.0 %collective-permute-start.21 = (bf16[2,128,768]{2,1,0:T(8,128)(2,1)S(1)}, bf16[2,128,768]{2,1,0:T(8,128)(2,1)S(1)}, u32[]{:S(2)}, u32[]{:S(2)}) collective-permute-start(bf16[2,128,768]{2,1,0:T(8,128)(2,1)S(1)} %get-tuple-element.46), channel_id=1, source_target_pairs={{0,4},{2,6},{4,0},{6,2},{1,5},{3,7},{5,1},{7,3},{8,12},{10,14},{12... | collective-permute-start | bytes 1179656 | tf_op jit(solution)/shard_map/ppermute | solution.py:180
  59.5 6.9 %collective-permute-start.22 = (bf16[128,768]{1,0:T(8,128)(2,1)S(1)}, bf16[128,768]{1,0:T(8,128)(2,1)S(1)}, u32[]{:S(2)}, u32[]{:S(2)}) collective-permute-start(bf16[128,768]{1,0:T(8,128)(2,1)S(1)} %get-tuple-element.48), channel_id=1, source_target_pairs={{0,8},{8,0},{1,9},{9,1},{2,10},{10,2},{3,11},{11,3},{4,12},{12,4},... | collective-permute-start | bytes 589832 | tf_op jit(solution)/shard_map/ppermute | solution.py:180
  60.4 7.2 %collective-permute-start.16 = (bf16[128,768]{1,0:T(8,128)(2,1)S(1)}, bf16[128,768]{1,0:T(8,128)(2,1)S(1)}, u32[]{:S(2)}, u32[]{:S(2)}) collective-permute-start(bf16[128,768]{1,0:T(8,128)(2,1)S(1)} %get-tuple-element.40), channel_id=1, source_target_pairs={{0,4},{2,6},{4,0},{6,2},{1,5},{3,7},{5,1},{7,3},{8,12},{10,14},{12... | collective-permute-start | bytes 589832 | tf_op jit(solution)/shard_map/ppermute | solution.py:180
  61.0 8.7 %collective-permute-start.17 = (bf16[128,768]{1,0:T(8,128)(2,1)S(1)}, bf16[128,768]{1,0:T(8,128)(2,1)S(1)}, u32[]{:S(2)}, u32[]{:S(2)}) collective-permute-start(bf16[128,768]{1,0:T(8,128)(2,1)S(1)} %get-tuple-element.41), channel_id=1, source_target_pairs={{0,2},{2,4},{4,6},{6,0},{1,3},{3,5},{5,7},{7,1},{8,10},{10,12},{12... | collective-permute-start | bytes 589832 | tf_op jit(solution)/shard_map/ppermute | solution.py:180
  66.3 5.8 %collective-permute-start.18 = (bf16[128,768]{1,0:T(8,128)(2,1)S(1)}, bf16[128,768]{1,0:T(8,128)(2,1)S(1)}, u32[]{:S(2)}, u32[]{:S(2)}) collective-permute-start(bf16[128,768]{1,0:T(8,128)(2,1)S(1)} %get-tuple-element.42), channel_id=1, source_target_pairs={{0,6},{2,0},{4,2},{6,4},{1,7},{3,1},{5,3},{7,5},{8,14},{10,8},{12,... | collective-permute-start | bytes 589832 | tf_op jit(solution)/shard_map/ppermute | solution.py:180
  (2 other events, 45.1 us)

commit v7 on v6

--- a/solution.py
+++ b/solution.py
@@ -96,11 +96,12 @@
 def screen(w_ref, *refs):
     pieces, outs, (acc, held, sems) = refs[:4], refs[4:7], refs[7:]
     copies = copy_all([(ref, held.at[i]) for i, ref in enumerate(pieces)], sems)
-    for i in range(4):
-        copies[i].wait()
-        cols = slice(i * 512, (i + 1) * 512)
+    for i in range(2):
+        copies[2 * i].wait()
+        copies[2 * i + 1].wait()
+        cols = slice(i * 1024, (i + 1) * 1024)
         for p, (k, kp) in enumerate(PAIRS):
-            rhs = held[i, :, kp].reshape(512, 256)
+            rhs = held[2 * i : 2 * i + 2, :, kp].reshape(1024, 256)
             term = jnp.dot(w_ref[kp - k, :, cols], rhs, preferred_element_type=F32)
             if i == 0:
                 acc[p] = term

time: 73.9 us -> 73.8 us (level)
  no operation moved by 1% of the time
where the time goes in v7:
time: 73.8 us; the launch traced here: 73.6 us
  waiting for transfers between devices  34.1 us (46%)
  starting transfers between devices  28.8 us (39%)
  Pallas kernels  9.55 us (13%)
  local copies, waits for them, and re-layouts  0.86 us (1%)
    ppermute x15, waiting for transfers between devices, shift(): return lax.ppermute(x, axis, [(i, (i + step) % size) for i in range(size)])  22.8 us
    ppermute x15, starting transfers between devices, shift(): return lax.ppermute(x, axis, [(i, (i + step) % size) for i in range(size)])  19.6 us
    ppermute x8, waiting for transfers between devices, ring_swap(): return lax.ppermute(x, (axis, 'c'), pairs)  11.3 us
    pallas_call x13, Pallas kernels, call(): pl.pallas_call(body, out_shape=[jax.ShapeDtypeStruct(s, BF) for s in outs...  9.55 us
    ppermute x8, starting transfers between devices, ring_swap(): return lax.ppermute(x, (axis, 'c'), pairs)  9.24 us
  transfers between devices with their start and end apart: 23, of which 9 were waited for; matrix products, arithmetic and copies ran while one was open for 0% of the time, Pallas kernels for 11%

profile of v7, /device:TPU:6, one launch (start us, length us, event | category | flops | bytes accessed | tf_op | source)
XLA Modules:
  0.0 73.6 jit_solution(8537904993193229071)
XLA Ops:
  0.0 1.9 %collective-permute-start.6 = (bf16[2,2,128,256]{3,2,1,0:T(8,128)(2,1)}, bf16[2,2,128,256]{3,2,1,0:T(8,128)(2,1)S(1)}, u32[]{:S(2)}, u32[]{:S(2)}) collective-permute-start(bf16[2,2,128,256]{3,2,1,0:T(8,128)(2,1)} %a_ref.1), channel_id=1, source_target_pairs={{0,8},{8,0},{1,9},{9,1},{2,10},{10,2},{3,11},{11,3},{4,12},{12,4},... | collective-permute-start | bytes 786440 | tf_op jit(solution)/shard_map/ppermute | solution.py:181
  1.9 1.1 %shard_map.47 = (bf16[2,128,256]{2,1,0:T(8,128)(2,1)S(1)}, bf16[2,128,256]{2,1,0:T(8,128)(2,1)S(1)}) custom-call(bf16[2,2,128,256]{3,2,1,0:T(8,128)(2,1)} %a_ref.1), custom_call_target="tpu_custom_call" | custom-call | tf_op jit(solution)/shard_map/pallas_call | solution.py:24
  3.3 1.6 %collective-permute-start.4 = (bf16[2,2,128,256]{3,2,1,0:T(8,128)(2,1)}, bf16[2,2,128,256]{3,2,1,0:T(8,128)(2,1)S(1)}, u32[]{:S(2)}, u32[]{:S(2)}) collective-permute-start(bf16[2,2,128,256]{3,2,1,0:T(8,128)(2,1)} %a_ref.1), channel_id=1, source_target_pairs={{0,2},{1,7},{2,0},{3,5},{4,6},{5,3},{6,4},{7,1},{8,10},{9,15},{10,... | collective-permute-start | bytes 786440 | tf_op jit(solution)/shard_map/ppermute | solution.py:186
  5.9 3.6 %collective-permute-start.8 = (bf16[2,128,512]{2,1,0:T(8,128)(2,1)S(1)}, bf16[2,128,512]{2,1,0:T(8,128)(2,1)S(1)}, u32[]{:S(2)}, u32[]{:S(2)}) collective-permute-start(bf16[2,128,512]{2,1,0:T(8,128)(2,1)S(1)} %shard_map.48.a_ref), channel_id=1, source_target_pairs={{0,16},{16,0},{1,17},{17,1},{2,18},{18,2},{3,19},{19,3},{4,20},{20... | collective-permute-start | bytes 786440 | tf_op jit(solution)/shard_map/ppermute | solution.py:181
  9.5 2.7 %collective-permute-start.7 = (bf16[2,2,128,256]{3,2,1,0:T(8,128)(2,1)S(1)}, bf16[2,2,128,256]{3,2,1,0:T(8,128)(2,1)S(1)}, u32[]{:S(2)}, u32[]{:S(2)}) collective-permute-start(bf16[2,2,128,256]{3,2,1,0:T(8,128)(2,1)S(1)} %collective-permute-done.6.a_ref), channel_id=1, source_target_pairs={{0,6},{1,3},{2,4},{3,1},{4,2},{5,7},{6,0},{7,5},{8,14},{9,11},{10,... | collective-permute-start | bytes 786440 | tf_op jit(solution)/shard_map/ppermute | solution.py:186
  12.2 1.0 %shard_map.50.refs_0_ = bf16[2,2,2,128,256]{4,3,2,1,0:T(8,128)(2,1)S(1)} custom-call(bf16[2,2,128,256]{3,2,1,0:T(8,128)(2,1)} %a_ref.1, bf16[2,2,128,256]{3,2,1,0:T(8,128)(2,1)S(1)} %collective-permute-done.4.b_ref), custom_call_target="tpu_custom_call" | custom-call | tf_op jit(solution)/shard_map/pallas_call | solution.py:24
  14.1 1.0 %collective-permute-start.3 = (bf16[2,2,128,512]{3,2,1,0:T(8,128)(2,1)S(1)}, bf16[2,2,128,512]{3,2,1,0:T(8,128)(2,1)S(1)}, u32[]{:S(2)}, u32[]{:S(2)}) collective-permute-start(bf16[2,2,128,512]{3,2,1,0:T(8,128)(2,1)S(1)} %shard_map.49.r0), channel_id=1, source_target_pairs={{0,96},{1,33},{32,64},{33,1},{64,32},{65,97},{96,0},{97,65},{2,98}... | collective-permute-start | bytes 1572872 | tf_op jit(solution)/shard_map/ppermute | solution.py:186
  15.1 3.0 %collective-permute-done.8.a_ref = bf16[2,128,512]{2,1,0:T(8,128)(2,1)S(1)} collective-permute-done((bf16[2,128,512]{2,1,0:T(8,128)(2,1)S(1)}, bf16[2,128,512]{2,1,0:T(8,128)(2,1)S(1)}, u32[]{:S(2)}, u32[]{:S(2)}) %collective-permute-start.8) | collective-permute-done | bytes 262176 | tf_op jit(solution)/shard_map/ppermute | solution.py:181
  18.1 1.7 %collective-permute-start.9 = (bf16[2,2,2,128,256]{4,3,2,1,0:T(8,128)(2,1)S(1)}, bf16[2,2,2,128,256]{4,3,2,1,0:T(8,128)(2,1)S(1)}, u32[]{:S(2)}, u32[]{:S(2)}) collective-permute-start(bf16[2,2,2,128,256]{4,3,2,1,0:T(8,128)(2,1)S(1)} %shard_map.51.refs_2_), channel_id=1, source_target_pairs={{0,2},{1,7},{2,0},{3,5},{4,6},{5,3},{6,4},{7,1},{8,10},{9,15},{10,... | collective-permute-start | bytes 1572872 | tf_op jit(solution)/shard_map/ppermute | solution.py:186
  20.2 7.1 %collective-permute-done.11.b_ref = bf16[2,128,512]{2,1,0:T(8,128)(2,1)S(1)} collective-permute-done((bf16[2,128,512]{2,1,0:T(8,128)(2,1)S(1)}, bf16[2,128,512]{2,1,0:T(8,128)(2,1)S(1)}, u32[]{:S(2)}, u32[]{:S(2)}) %collective-permute-start.11) | collective-permute-done | bytes 262176 | tf_op jit(solution)/shard_map/ppermute | solution.py:186
  27.5 1.6 %shard_map.46.w_ref = bf16[2,512,2048]{2,1,0:T(8,128)(2,1)S(1)} custom-call(s32[2,3]{1,0:T(2,128)S(1)} %bitcast.1, s32[3]{0:T(128)S(1)} %copy-done.2, bf16[2,2,128,2048]{3,2,1,0:T(8,128)(2,1)S(1)} %copy-done, bf16[2,2,128,2048]{3,2,1,0:T(8,128)(2,1)S(1)} %collective-permute-done.mate_ref), custom_call_target="tpu_custom_call" | custom-call | tf_op jit(solution)/shard_map/pallas_call | solution.py:24
  29.2 2.5 %shard_map.52 = (bf16[2,2,128,256]{3,2,1,0:T(8,128)(2,1)S(1)}, bf16[2,2,128,256]{3,2,1,0:T(8,128)(2,1)S(1)}, bf16[2,2,128,256]{3,2,1,0:T(8,128)(2,1)S(1)}) custom-call(bf16[2,512,2048]{2,1,0:T(8,128)(2,1)S(1)} %shard_map.46.w_ref, bf16[2,2,2,128,256]{4,3,2,1,0:T(8,128)(2,1)S(1)} %shard_map.50.refs_0_, ...), custom_call_target="tpu_custom_call" | custom-call | tf_op jit(solution)/shard_map/pallas_call | solution.py:24
  32.4 4.2 %collective-permute-done.12.r3 = bf16[2,2,128,512]{3,2,1,0:T(8,128)(2,1)S(1)} collective-permute-done((bf16[2,2,128,512]{3,2,1,0:T(8,128)(2,1)S(1)}, bf16[2,2,128,512]{3,2,1,0:T(8,128)(2,1)S(1)}, u32[]{:S(2)}, u32[]{:S(2)}) %collective-permute-start.12) | collective-permute-done | bytes 524320 | tf_op jit(solution)/shard_map/ppermute | solution.py:186
  36.7 1.3 %shard_map.54 = (bf16[2,128,768]{2,1,0:T(8,128)(2,1)S(1)}, bf16[2,128,768]{2,1,0:T(8,128)(2,1)S(1)}, bf16[2,128,768]{2,1,0:T(8,128)(2,1)S(1)}, bf16[2,128,768]{2...) custom-call(bf16[2,2,128,256]{3,2,1,0:T(8,128)(2,1)S(1)} %get-tuple-element.34.m0_ref, ...), custom_call_target="tpu_custom_call" | custom-call | tf_op jit(solution)/shard_map/pallas_call | solution.py:24
  38.7 1.2 %collective-permute-start.15 = (bf16[4,128,768]{2,1,0:T(8,128)(2,1)S(1)}, bf16[4,128,768]{2,1,0:T(8,128)(2,1)S(1)}, u32[]{:S(2)}, u32[]{:S(2)}) collective-permute-start(bf16[4,128,768]{2,1,0:T(8,128)(2,1)S(1)} %get-tuple-element.38), channel_id=1, source_target_pairs={{0,8},{8,0},{1,9},{9,1},{2,10},{10,2},{3,11},{11,3},{4,12},{12,4},... | collective-permute-start | bytes 2359304 | tf_op jit(solution)/shard_map/ppermute | solution.py:181
  40.3 2.9 %collective-permute-start.20 = (bf16[2,128,768]{2,1,0:T(8,128)(2,1)S(1)}, bf16[2,128,768]{2,1,0:T(8,128)(2,1)S(1)}, u32[]{:S(2)}, u32[]{:S(2)}) collective-permute-start(bf16[2,128,768]{2,1,0:T(8,128)(2,1)S(1)} %get-tuple-element.45), channel_id=1, source_target_pairs={{0,6},{2,0},{4,2},{6,4},{1,7},{3,1},{5,3},{7,5},{8,14},{10,8},{12,... | collective-permute-start | bytes 1179656 | tf_op jit(solution)/shard_map/ppermute | solution.py:181
  43.2 1.3 %collective-permute-start.21 = (bf16[2,128,768]{2,1,0:T(8,128)(2,1)S(1)}, bf16[2,128,768]{2,1,0:T(8,128)(2,1)S(1)}, u32[]{:S(2)}, u32[]{:S(2)}) collective-permute-start(bf16[2,128,768]{2,1,0:T(8,128)(2,1)S(1)} %get-tuple-element.46), channel_id=1, source_target_pairs={{0,4},{2,6},{4,0},{6,2},{1,5},{3,7},{5,1},{7,3},{8,12},{10,14},{12... | collective-permute-start | bytes 1179656 | tf_op jit(solution)/shard_map/ppermute | solution.py:181
  44.5 12.6 %collective-permute-done.15.got_ref = bf16[4,128,768]{2,1,0:T(8,128)(2,1)S(1)} collective-permute-done((bf16[4,128,768]{2,1,0:T(8,128)(2,1)S(1)}, bf16[4,128,768]{2,1,0:T(8,128)(2,1)S(1)}, u32[]{:S(2)}, u32[]{:S(2)}) %collective-permute-start.15) | collective-permute-done | bytes 786464 | tf_op jit(solution)/shard_map/ppermute | solution.py:181
  57.7 1.1 %collective-permute-done.21.g3_ref = bf16[2,128,768]{2,1,0:T(8,128)(2,1)S(1)} collective-permute-done((bf16[2,128,768]{2,1,0:T(8,128)(2,1)S(1)}, bf16[2,128,768]{2,1,0:T(8,128)(2,1)S(1)}, u32[]{:S(2)}, u32[]{:S(2)}) %collective-permute-start.21) | collective-permute-done | bytes 393248 | tf_op jit(solution)/shard_map/ppermute | solution.py:181
  59.0 1.4 %collective-permute-start.22 = (bf16[128,768]{1,0:T(8,128)(2,1)S(1)}, bf16[128,768]{1,0:T(8,128)(2,1)S(1)}, u32[]{:S(2)}, u32[]{:S(2)}) collective-permute-start(bf16[128,768]{1,0:T(8,128)(2,1)S(1)} %get-tuple-element.48), channel_id=1, source_target_pairs={{0,8},{8,0},{1,9},{9,1},{2,10},{10,2},{3,11},{11,3},{4,12},{12,4},... | collective-permute-start | bytes 589832 | tf_op jit(solution)/shard_map/ppermute | solution.py:181
  61.0 5.3 %collective-permute-start.17 = (bf16[128,768]{1,0:T(8,128)(2,1)S(1)}, bf16[128,768]{1,0:T(8,128)(2,1)S(1)}, u32[]{:S(2)}, u32[]{:S(2)}) collective-permute-start(bf16[128,768]{1,0:T(8,128)(2,1)S(1)} %get-tuple-element.41), channel_id=1, source_target_pairs={{0,2},{2,4},{4,6},{6,0},{1,3},{3,5},{5,7},{7,1},{8,10},{10,12},{12... | collective-permute-start | bytes 589832 | tf_op jit(solution)/shard_map/ppermute | solution.py:181
  66.3 1.3 %collective-permute-done.16.z1_ref = bf16[128,768]{1,0:T(8,128)(2,1)S(1)} collective-permute-done((bf16[128,768]{1,0:T(8,128)(2,1)S(1)}, bf16[128,768]{1,0:T(8,128)(2,1)S(1)}, u32[]{:S(2)}, u32[]{:S(2)}) %collective-permute-start.16) | collective-permute-done | bytes 196640 | tf_op jit(solution)/shard_map/ppermute | solution.py:181
  67.6 2.0 %collective-permute-done.17.z2_ref = bf16[128,768]{1,0:T(8,128)(2,1)S(1)} collective-permute-done((bf16[128,768]{1,0:T(8,128)(2,1)S(1)}, bf16[128,768]{1,0:T(8,128)(2,1)S(1)}, u32[]{:S(2)}, u32[]{:S(2)}) %collective-permute-start.17) | collective-permute-done | bytes 196640 | tf_op jit(solution)/shard_map/ppermute | solution.py:181
  69.7 2.4 %collective-permute-done.18.z3_ref = bf16[128,768]{1,0:T(8,128)(2,1)S(1)} collective-permute-done((bf16[128,768]{1,0:T(8,128)(2,1)S(1)}, bf16[128,768]{1,0:T(8,128)(2,1)S(1)}, u32[]{:S(2)}, u32[]{:S(2)}) %collective-permute-start.18) | collective-permute-done | bytes 196640 | tf_op jit(solution)/shard_map/ppermute | solution.py:181
  (42 shorter events, 7.5 us)
Async XLA Ops:
  0.0 27.5 %collective-permute-start = (bf16[2,2,128,2048]{3,2,1,0:T(8,128)(2,1)}, bf16[2,2,128,2048]{3,2,1,0:T(8,128)(2,1)S(1)}, u32[]{:S(2)}, u32[]{:S(2)}) collective-permute-start(bf16[2,2,128,2048]{3,2,1,0:T(8,128)(2,1)} %own_ref.1), channel_id=1, source_target_pairs={{0,1},{1,0},{2,3},{3,2},{4,5},{5,4},{6,7},{7,6},{8,9},{9,8},{10,11... | collective-permute-start | bytes 6291464 | tf_op jit(solution)/shard_map/ppermute | solution.py:181
  0.0 9.5 %collective-permute-start.6 = (bf16[2,2,128,256]{3,2,1,0:T(8,128)(2,1)}, bf16[2,2,128,256]{3,2,1,0:T(8,128)(2,1)S(1)}, u32[]{:S(2)}, u32[]{:S(2)}) collective-permute-start(bf16[2,2,128,256]{3,2,1,0:T(8,128)(2,1)} %a_ref.1), channel_id=1, source_target_pairs={{0,8},{8,0},{1,9},{9,1},{2,10},{10,2},{3,11},{11,3},{4,12},{12,4},... | collective-permute-start | bytes 786440 | tf_op jit(solution)/shard_map/ppermute | solution.py:181
  3.0 1.9 %collective-permute-start.1 = (bf16[2,128,256]{2,1,0:T(8,128)(2,1)S(1)}, bf16[2,128,256]{2,1,0:T(8,128)(2,1)S(1)}, u32[]{:S(2)}, u32[]{:S(2)}) collective-permute-start(bf16[2,128,256]{2,1,0:T(8,128)(2,1)S(1)} %get-tuple-element.28), channel_id=1, source_target_pairs={{0,1},{1,0},{2,3},{3,2},{4,5},{5,4},{6,7},{7,6},{8,9},{9,8},{10,11... | collective-permute-start | bytes 393224 | tf_op jit(solution)/shard_map/ppermute | solution.py:181
  3.3 8.9 %collective-permute-start.4 = (bf16[2,2,128,256]{3,2,1,0:T(8,128)(2,1)}, bf16[2,2,128,256]{3,2,1,0:T(8,128)(2,1)S(1)}, u32[]{:S(2)}, u32[]{:S(2)}) collective-permute-start(bf16[2,2,128,256]{3,2,1,0:T(8,128)(2,1)} %a_ref.1), channel_id=1, source_target_pairs={{0,2},{1,7},{2,0},{3,5},{4,6},{5,3},{6,4},{7,1},{8,10},{9,15},{10,... | collective-permute-start | bytes 786440 | tf_op jit(solution)/shard_map/ppermute | solution.py:186
  4.9 22.6 %copy-start = (bf16[2,2,128,2048]{3,2,1,0:T(8,128)(2,1)S(1)}, bf16[2,2,128,2048]{3,2,1,0:T(8,128)(2,1)}, u32[]{:S(2)}) copy-start(bf16[2,2,128,2048]{3,2,1,0:T(8,128)(2,1)} %own_ref.1) | copy-start | bytes 6291460
  5.0 9.0 %collective-permute-start.2 = (bf16[2,128,512]{2,1,0:T(8,128)(2,1)S(1)}, bf16[2,128,512]{2,1,0:T(8,128)(2,1)S(1)}, u32[]{:S(2)}, u32[]{:S(2)}) collective-permute-start(bf16[2,128,512]{2,1,0:T(8,128)(2,1)S(1)} %shard_map.48.a_ref), channel_id=1, source_target_pairs={{0,32},{1,97},{32,0},{33,65},{64,96},{65,33},{96,64},{97,1},{2,34}... | collective-permute-start | bytes 786440 | tf_op jit(solution)/shard_map/ppermute | solution.py:186
  5.9 12.1 %collective-permute-start.8 = (bf16[2,128,512]{2,1,0:T(8,128)(2,1)S(1)}, bf16[2,128,512]{2,1,0:T(8,128)(2,1)S(1)}, u32[]{:S(2)}, u32[]{:S(2)}) collective-permute-start(bf16[2,128,512]{2,1,0:T(8,128)(2,1)S(1)} %shard_map.48.a_ref), channel_id=1, source_target_pairs={{0,16},{16,0},{1,17},{17,1},{2,18},{18,2},{3,19},{19,3},{4,20},{20... | collective-permute-start | bytes 786440 | tf_op jit(solution)/shard_map/ppermute | solution.py:181
  9.5 8.6 %collective-permute-start.7 = (bf16[2,2,128,256]{3,2,1,0:T(8,128)(2,1)S(1)}, bf16[2,2,128,256]{3,2,1,0:T(8,128)(2,1)S(1)}, u32[]{:S(2)}, u32[]{:S(2)}) collective-permute-start(bf16[2,2,128,256]{3,2,1,0:T(8,128)(2,1)S(1)} %collective-permute-done.6.a_ref), channel_id=1, source_target_pairs={{0,6},{1,3},{2,4},{3,1},{4,2},{5,7},{6,0},{7,5},{8,14},{9,11},{10,... | collective-permute-start | bytes 786440 | tf_op jit(solution)/shard_map/ppermute | solution.py:186
  13.2 16.0 %collective-permute-start.5 = (bf16[2,2,2,128,256]{4,3,2,1,0:T(8,128)(2,1)S(1)}, bf16[2,2,2,128,256]{4,3,2,1,0:T(8,128)(2,1)S(1)}, u32[]{:S(2)}, u32[]{:S(2)}) collective-permute-start(bf16[2,2,2,128,256]{4,3,2,1,0:T(8,128)(2,1)S(1)} %shard_map.50.refs_0_), channel_id=1, source_target_pairs={{0,6},{1,3},{2,4},{3,1},{4,2},{5,7},{6,0},{7,5},{8,14},{9,11},{10,... | collective-permute-start | bytes 1572872 | tf_op jit(solution)/shard_map/ppermute | solution.py:186
  14.1 15.1 %collective-permute-start.3 = (bf16[2,2,128,512]{3,2,1,0:T(8,128)(2,1)S(1)}, bf16[2,2,128,512]{3,2,1,0:T(8,128)(2,1)S(1)}, u32[]{:S(2)}, u32[]{:S(2)}) collective-permute-start(bf16[2,2,128,512]{3,2,1,0:T(8,128)(2,1)S(1)} %shard_map.49.r0), channel_id=1, source_target_pairs={{0,96},{1,33},{32,64},{33,1},{64,32},{65,97},{96,0},{97,65},{2,98}... | collective-permute-start | bytes 1572872 | tf_op jit(solution)/shard_map/ppermute | solution.py:186
  18.1 11.1 %collective-permute-start.9 = (bf16[2,2,2,128,256]{4,3,2,1,0:T(8,128)(2,1)S(1)}, bf16[2,2,2,128,256]{4,3,2,1,0:T(8,128)(2,1)S(1)}, u32[]{:S(2)}, u32[]{:S(2)}) collective-permute-start(bf16[2,2,2,128,256]{4,3,2,1,0:T(8,128)(2,1)S(1)} %shard_map.51.refs_2_), channel_id=1, source_target_pairs={{0,2},{1,7},{2,0},{3,5},{4,6},{5,3},{6,4},{7,1},{8,10},{9,15},{10,... | collective-permute-start | bytes 1572872 | tf_op jit(solution)/shard_map/ppermute | solution.py:186
  19.8 7.6 %collective-permute-start.11 = (bf16[2,128,512]{2,1,0:T(8,128)(2,1)S(1)}, bf16[2,128,512]{2,1,0:T(8,128)(2,1)S(1)}, u32[]{:S(2)}, u32[]{:S(2)}) collective-permute-start(bf16[2,128,512]{2,1,0:T(8,128)(2,1)S(1)} %collective-permute-done.8.a_ref), channel_id=1, source_target_pairs={{0,96},{1,33},{32,64},{33,1},{64,32},{65,97},{96,0},{97,65},{2,98}... | collective-permute-start | bytes 786440 | tf_op jit(solution)/shard_map/ppermute | solution.py:186
  27.4 9.3 %collective-permute-start.12 = (bf16[2,2,128,512]{3,2,1,0:T(8,128)(2,1)S(1)}, bf16[2,2,128,512]{3,2,1,0:T(8,128)(2,1)S(1)}, u32[]{:S(2)}, u32[]{:S(2)}) collective-permute-start(bf16[2,2,128,512]{3,2,1,0:T(8,128)(2,1)S(1)} %shard_map.53.r2), channel_id=1, source_target_pairs={{0,32},{1,97},{32,0},{33,65},{64,96},{65,33},{96,64},{97,1},{2,34}... | collective-permute-start | bytes 1572872 | tf_op jit(solution)/shard_map/ppermute | solution.py:186
  31.8 4.9 %collective-permute-start.13 = (bf16[2,2,128,256]{3,2,1,0:T(8,128)(2,1)S(1)}, bf16[2,2,128,256]{3,2,1,0:T(8,128)(2,1)S(1)}, u32[]{:S(2)}, u32[]{:S(2)}) collective-permute-start(bf16[2,2,128,256]{3,2,1,0:T(8,128)(2,1)S(1)} %get-tuple-element.34.m0_ref), channel_id=1, source_target_pairs={{0,1},{1,0},{2,3},{3,2},{4,5},{5,4},{6,7},{7,6},{8,9},{9,8},{10,11... | collective-permute-start | bytes 786440 | tf_op jit(solution)/shard_map/ppermute | solution.py:181
  31.9 4.8 %collective-permute-start.14 = (bf16[2,2,128,256]{3,2,1,0:T(8,128)(2,1)S(1)}, bf16[2,2,128,256]{3,2,1,0:T(8,128)(2,1)S(1)}, u32[]{:S(2)}, u32[]{:S(2)}) collective-permute-start(bf16[2,2,128,256]{3,2,1,0:T(8,128)(2,1)S(1)} %get-tuple-element.35.m1_ref), channel_id=1, source_target_pairs={{0,1},{1,0},{2,3},{3,2},{4,5},{5,4},{6,7},{7,6},{8,9},{9,8},{10,11... | collective-permute-start | bytes 786440 | tf_op jit(solution)/shard_map/ppermute | solution.py:181
  32.4 5.6 %collective-permute-start.10 = (bf16[2,2,128,256]{3,2,1,0:T(8,128)(2,1)S(1)}, bf16[2,2,128,256]{3,2,1,0:T(8,128)(2,1)S(1)}, u32[]{:S(2)}, u32[]{:S(2)}) collective-permute-start(bf16[2,2,128,256]{3,2,1,0:T(8,128)(2,1)S(1)} %get-tuple-element.31.mine_ref), channel_id=1, source_target_pairs={{0,1},{1,0},{2,3},{3,2},{4,5},{5,4},{6,7},{7,6},{8,9},{9,8},{10,11... | collective-permute-start | bytes 786440 | tf_op jit(solution)/shard_map/ppermute | solution.py:181
  38.7 18.4 %collective-permute-start.15 = (bf16[4,128,768]{2,1,0:T(8,128)(2,1)S(1)}, bf16[4,128,768]{2,1,0:T(8,128)(2,1)S(1)}, u32[]{:S(2)}, u32[]{:S(2)}) collective-permute-start(bf16[4,128,768]{2,1,0:T(8,128)(2,1)S(1)} %get-tuple-element.38), channel_id=1, source_target_pairs={{0,8},{8,0},{1,9},{9,1},{2,10},{10,2},{3,11},{11,3},{4,12},{12,4},... | collective-permute-start | bytes 2359304 | tf_op jit(solution)/shard_map/ppermute | solution.py:181
  40.0 17.4 %collective-permute-start.19 = (bf16[2,128,768]{2,1,0:T(8,128)(2,1)S(1)}, bf16[2,128,768]{2,1,0:T(8,128)(2,1)S(1)}, u32[]{:S(2)}, u32[]{:S(2)}) collective-permute-start(bf16[2,128,768]{2,1,0:T(8,128)(2,1)S(1)} %get-tuple-element.44), channel_id=1, source_target_pairs={{0,2},{2,4},{4,6},{6,0},{1,3},{3,5},{5,7},{7,1},{8,10},{10,12},{12... | collective-permute-start | bytes 1179656 | tf_op jit(solution)/shard_map/ppermute | solution.py:181
  40.3 17.4 %collective-permute-start.20 = (bf16[2,128,768]{2,1,0:T(8,128)(2,1)S(1)}, bf16[2,128,768]{2,1,0:T(8,128)(2,1)S(1)}, u32[]{:S(2)}, u32[]{:S(2)}) collective-permute-start(bf16[2,128,768]{2,1,0:T(8,128)(2,1)S(1)} %get-tuple-element.45), channel_id=1, source_target_pairs={{0,6},{2,0},{4,2},{6,4},{1,7},{3,1},{5,3},{7,5},{8,14},{10,8},{12,... | collective-permute-start | bytes 1179656 | tf_op jit(solution)/shard_map/ppermute | solution.py:181
  43.2 15.6 %collective-permute-start.21 = (bf16[2,128,768]{2,1,0:T(8,128)(2,1)S(1)}, bf16[2,128,768]{2,1,0:T(8,128)(2,1)S(1)}, u32[]{:S(2)}, u32[]{:S(2)}) collective-permute-start(bf16[2,128,768]{2,1,0:T(8,128)(2,1)S(1)} %get-tuple-element.46), channel_id=1, source_target_pairs={{0,4},{2,6},{4,0},{6,2},{1,5},{3,7},{5,1},{7,3},{8,12},{10,14},{12... | collective-permute-start | bytes 1179656 | tf_op jit(solution)/shard_map/ppermute | solution.py:181
  59.0 7.3 %collective-permute-start.22 = (bf16[128,768]{1,0:T(8,128)(2,1)S(1)}, bf16[128,768]{1,0:T(8,128)(2,1)S(1)}, u32[]{:S(2)}, u32[]{:S(2)}) collective-permute-start(bf16[128,768]{1,0:T(8,128)(2,1)S(1)} %get-tuple-element.48), channel_id=1, source_target_pairs={{0,8},{8,0},{1,9},{9,1},{2,10},{10,2},{3,11},{11,3},{4,12},{12,4},... | collective-permute-start | bytes 589832 | tf_op jit(solution)/shard_map/ppermute | solution.py:181
  60.4 7.2 %collective-permute-start.16 = (bf16[128,768]{1,0:T(8,128)(2,1)S(1)}, bf16[128,768]{1,0:T(8,128)(2,1)S(1)}, u32[]{:S(2)}, u32[]{:S(2)}) collective-permute-start(bf16[128,768]{1,0:T(8,128)(2,1)S(1)} %get-tuple-element.40), channel_id=1, source_target_pairs={{0,4},{2,6},{4,0},{6,2},{1,5},{3,7},{5,1},{7,3},{8,12},{10,14},{12... | collective-permute-start | bytes 589832 | tf_op jit(solution)/shard_map/ppermute | solution.py:181
  61.0 8.7 %collective-permute-start.17 = (bf16[128,768]{1,0:T(8,128)(2,1)S(1)}, bf16[128,768]{1,0:T(8,128)(2,1)S(1)}, u32[]{:S(2)}, u32[]{:S(2)}) collective-permute-start(bf16[128,768]{1,0:T(8,128)(2,1)S(1)} %get-tuple-element.41), channel_id=1, source_target_pairs={{0,2},{2,4},{4,6},{6,0},{1,3},{3,5},{5,7},{7,1},{8,10},{10,12},{12... | collective-permute-start | bytes 589832 | tf_op jit(solution)/shard_map/ppermute | solution.py:181
  66.3 5.8 %collective-permute-start.18 = (bf16[128,768]{1,0:T(8,128)(2,1)S(1)}, bf16[128,768]{1,0:T(8,128)(2,1)S(1)}, u32[]{:S(2)}, u32[]{:S(2)}) collective-permute-start(bf16[128,768]{1,0:T(8,128)(2,1)S(1)} %get-tuple-element.42), channel_id=1, source_target_pairs={{0,6},{2,0},{4,2},{6,4},{1,7},{3,1},{5,3},{7,5},{8,14},{10,8},{12,... | collective-permute-start | bytes 589832 | tf_op jit(solution)/shard_map/ppermute | solution.py:181
  (2 other events, 45.1 us)
